TPU v7x, 32 devices: a whole 2x2x4 slice. The times are simulated.
32 devices in a mesh: sec: 4 (over y, core), tile: 8 (over z, x).
Axes of the slice: x: 2, y: 2, z: 4, core: 2. Of those that a mesh axis runs over, the one named last changes fastest.
Arguments:
- parent_old: float32 [128, 24, 4096], P('tile', None, 'sec'), may hold values from -6 to 6
- nest_state: float32 [4, 128, 24, 512], P('sec', 'tile'), may hold values from -6 to 6
- diffusion: float32 [24], replicated, may hold values from 0.04 to 0.1
- wind_speed: float32 [2, 24], replicated, may hold values from 0.05 to 0.25
- conversion: float32 [2, 8], replicated, may hold values from 0.05 to 0.4
- vert_mix: float32 [3], replicated, may hold values from 0.5 to 4
- nest_box: int32 [4, 4], replicated, may hold values from 0 to 3968, as said below
Outputs:
- parent_new: float32 [128, 24, 4096], P('tile', None, 'sec')
- nest_new: float32 [4, 128, 24, 512], P('sec', 'tile')
Inputs may be any that keep to these rules, and one draw needn't show every extreme that they name: `nest_box`: row n belongs to nest n, which lives on section n. Anchors are parent cells and keep the footprint of 32 by 128 parent cells inside the parent grid; live rows lie between 64 and 128, live columns between 256 and 512; some nest is live everywhere.
All inputs are finite; a program needn't handle non-finite values.
Results may differ from a plain program's by a relative error of at most 0.00002.
Values sent between devices are 32-bit elements; how exact they have to be, the bound alone decides.
No kernel may reach another device: no remote copies, remote signals or barrier semaphores. Data moves between devices by JAX's collectives and lax.ppermute only.
A program may use at most 64 MiB of HBM per device.

v0:
```python
import jax
import jax.numpy as jnp
from jax import lax
from jax.sharding import PartitionSpec as P

NSTEP = 4


def extended_2(block, sides, width):
    for axis, dim in sides:
        count = lax.axis_size(axis)
        forward = [(i, i + 1) for i in range(count - 1)]
        backward = [(target, source) for source, target in forward]
        low = lax.ppermute(
            lax.slice_in_dim(block, block.shape[dim] - width, None, axis=dim), axis, forward
        )
        high = lax.ppermute(lax.slice_in_dim(block, 0, width, axis=dim), axis, backward)
        block = jnp.concatenate([low, block, high], axis=dim)
    return block


def shifted(block, axis, distance):
    devices = range(lax.axis_size(axis))
    route = [(i - distance, i) for i in devices if i - distance in devices]
    return lax.ppermute(block, axis, route)


def horizontal(padded, diffusion, wind_speed):
    center = padded[1:-1, :, 1:-1]
    above_row = padded[:-2, :, 1:-1]
    below_row = padded[2:, :, 1:-1]
    left_col = padded[1:-1, :, :-2]
    right_col = padded[1:-1, :, 2:]
    spread = diffusion[:, None]
    drift_x = wind_speed[0][:, None]
    drift_y = wind_speed[1][:, None]
    return (
        center
        + spread * (above_row + below_row + left_col + right_col - 4.0 * center)
        - drift_x * (center - above_row)
        - drift_y * (center - left_col)
    )


def vertical(column_data, mixing):
    levels = column_data.shape[1]
    off_diag = -mixing
    ratios = []
    partials = []
    for level_idx in range(levels):
        neighbours = 1.0 if level_idx in (0, levels - 1) else 2.0
        pivot_val = 1.0 + neighbours * mixing
        rhs_now = column_data[:, level_idx]
        if level_idx > 0:
            pivot_val = pivot_val - off_diag * ratios[-1]
            rhs_now = rhs_now - off_diag * partials[-1]
        ratios.append(off_diag / pivot_val)
        partials.append(rhs_now / pivot_val)
    solved = [partials[-1]]
    for level_idx in range(levels - 2, -1, -1):
        solved.insert(0, partials[level_idx] - ratios[level_idx] * solved[0])
    return jnp.stack(solved, axis=1)


def physics(fields, conversion, vert_mix):
    row_count, chan_count, col_count = fields.shape
    levels = conversion.shape[1]
    grouped = fields.reshape(row_count, 3, levels, col_count)
    vapour = grouped[:, 0]
    cloud = grouped[:, 1]
    rain_water = grouped[:, 2]
    condense = conversion[0][:, None] * vapour
    vapour = vapour - condense
    cloud = cloud + condense
    fallout = conversion[1][:, None] * cloud
    cloud = cloud - fallout
    rain_water = rain_water + fallout
    solved = [
        vertical(vapour, vert_mix[0]),
        vertical(cloud, vert_mix[1]),
        vertical(rain_water, vert_mix[2]),
    ]
    return jnp.stack(solved, axis=1).reshape(row_count, chan_count, col_count)


def upsample(coarse, base, targets, foot_rows, foot_cols, nest_cols):
    low_row = jnp.floor_divide(targets, 4)
    weight_row = ((targets - 4 * low_row).astype(jnp.float32) / 4.0)[:, None, None]
    first_row = jnp.clip(low_row, 0, foot_rows - 1)
    second_row = jnp.clip(low_row + 1, 0, foot_rows - 1)
    lower_vals = jnp.take(coarse, first_row - base, axis=0)
    upper_vals = jnp.take(coarse, second_row - base, axis=0)
    row_mix = lower_vals + weight_row * (upper_vals - lower_vals)
    col_ids = jnp.arange(nest_cols, dtype=jnp.int32)
    first_col = jnp.floor_divide(col_ids, 4)
    second_col = jnp.minimum(first_col + 1, foot_cols - 1)
    weight_col = (col_ids - 4 * first_col).astype(jnp.float32) / 4.0
    left_vals = jnp.take(row_mix, first_col, axis=2)
    right_vals = jnp.take(row_mix, second_col, axis=2)
    return left_vals + weight_col * (right_vals - left_vals)


def nest_fields(targets, nest_cols, extent_x, extent_y):
    row_ids = targets[:, None]
    col_ids = jnp.arange(nest_cols, dtype=jnp.int32)[None, :]
    live_mask = ((row_ids >= 0) & (row_ids < extent_x) & (col_ids < extent_y)).astype(jnp.float32)
    distance = jnp.minimum(
        jnp.minimum(row_ids, col_ids), jnp.minimum(extent_x - 1 - row_ids, extent_y - 1 - col_ids)
    )
    distance = jnp.maximum(distance, 0).astype(jnp.float32)
    nudging = 0.1 + 0.4 * jnp.exp(-distance / 3.0)
    return (live_mask[:, None, :], nudging[:, None, :])


def nest_step(
    rows_padded, live_mask, nudging, forcing_now, diffusion, wind_speed, conversion, vert_mix
):
    padded = jnp.pad(rows_padded, ((0, 0), (0, 0), (1, 1)))
    moved = physics(horizontal(padded, diffusion, wind_speed), conversion, vert_mix)
    moved = moved + nudging * (forcing_now - moved)
    return moved * live_mask


def body(parent_old, nest_state, diffusion, wind_speed, conversion, vert_mix, nest_box):
    sec_pos = lax.axis_index("sec")
    tile_pos = lax.axis_index("tile")
    tile_count = lax.axis_size("tile")
    rows_tile, chan_count, cols_sec = parent_old.shape
    nest_rows = nest_state.shape[1]
    nest_cols = nest_state.shape[3]
    nest_count = nest_box.shape[0]
    own_rows = nest_rows // 4
    foot_rows = own_rows * tile_count
    foot_cols = nest_cols // 4
    my_box = nest_box[sec_pos]
    anchor_x = my_box[0]
    extent_x = my_box[2]
    extent_y = my_box[3]
    padded = extended_2(parent_old, (("sec", 2), ("tile", 0)), 1)
    parent_new = physics(horizontal(padded, diffusion, wind_speed), conversion, vert_mix)
    both_times = jnp.concatenate([parent_old, parent_new], axis=1)
    margin = 0
    send_chan = both_times.shape[1]
    strip_width = foot_cols + 2 * margin
    col_ids = (
        nest_box[:, 1][:, None]
        - margin
        + jnp.arange(strip_width, dtype=jnp.int32)[None, :]
        - sec_pos * cols_sec
    )
    col_valid = ((col_ids >= 0) & (col_ids < cols_sec)).astype(jnp.float32)
    picked = jnp.take(both_times, jnp.clip(col_ids, 0, cols_sec - 1).reshape(-1), axis=2)
    picked = picked.reshape(rows_tile, send_chan, nest_count, strip_width) * col_valid[None, None]
    routed = lax.psum_scatter(picked, "sec", scatter_dimension=2, tiled=True)
    col_strip = routed.reshape(rows_tile, send_chan, strip_width)
    row_ids = (
        anchor_x
        + jnp.arange(lax.axis_size("tile") * own_rows, dtype=jnp.int32)
        - tile_pos * rows_tile
    )
    row_valid = ((row_ids >= 0) & (row_ids < rows_tile)).astype(jnp.float32)
    taken = jnp.take(col_strip, jnp.clip(row_ids, 0, rows_tile - 1), axis=0)
    routed_rows = lax.psum_scatter(
        taken * row_valid[:, None, None], "tile", scatter_dimension=0, tiled=True
    )
    next_row = shifted(routed_rows[:1], "tile", -1)
    extended = jnp.concatenate([routed_rows, next_row], axis=0)
    targets = tile_pos * nest_rows + jnp.arange(nest_rows, dtype=jnp.int32)
    forcing = upsample(extended, tile_pos * own_rows, targets, foot_rows, foot_cols, nest_cols)
    live_mask, nudging = nest_fields(targets, nest_cols, extent_x, extent_y)
    forcing_old = forcing[:, :chan_count]
    forcing_new = forcing[:, chan_count:]
    nest_now = nest_state[0] * live_mask
    for step_num in range(NSTEP):
        weight_now = (step_num + 1) / NSTEP
        forcing_now = forcing_old + weight_now * (forcing_new - forcing_old)
        rows_padded = extended_2(nest_now, (("tile", 0),), 1)
        nest_now = nest_step(
            rows_padded,
            live_mask,
            nudging,
            forcing_now,
            diffusion,
            wind_speed,
            conversion,
            vert_mix,
        )
    return (parent_new, nest_now[None])


def solution(mesh):
    placed = (P("tile", None, "sec"), P("sec", "tile", None, None), P(), P(), P(), P(), P())
    return jax.shard_map(
        body,
        mesh=mesh,
        in_specs=placed,
        out_specs=(P("tile", None, "sec"), P("sec", "tile", None, None)),
        check_vma=False,
    )
```

profile of v0, /device:TPU:0, one launch (start us, length us, event | category | flops | bytes accessed | tf_op | source)
XLA Modules:
  0.0 248.0 jit_solution(92701052762024968)
XLA Ops:
  8.5 2.4 collective-permute-start
  17.7 4.2 %collective-permute-start.4 = (f32[1,24,512]{2,1,0:T(8,128)}, f32[1,24,512]{2,1,0:T(8,128)S(1)}, u32[]{:S(2)}, u32[]{:S(2)}) collective-permute-start(f32[1,24,512]{2,1,0:T(8,128)} %get-tuple-element.152), channel_id=1, source_target_pairs={{0,1},{1,2},{2,3},{3,4},{4,5},{5,6},{6,7},{8,9},{9,10},{10,11},{11... | collective-permute-start | bytes 147464 | tf_op jit(solution)/shard_map/ppermute | solution.py:14
  39.8 1.9 concatenate.58
  41.8 4.7 %collective-permute-start.2 = (f32[1,24,1026]{2,1,0:T(8,128)S(1)}, f32[1,24,1026]{2,1,0:T(8,128)S(1)}, u32[]{:S(2)}, u32[]{:S(2)}) collective-permute-start(f32[1,24,1026]{2,1,0:T(8,128)S(1)} %get-tuple-element.125), channel_id=1, source_target_pairs={{0,1},{1,2},{2,3},{3,4},{4,5},{5,6},{6,7},{8,9},{9,10},{10,11},{11... | collective-permute-start | bytes 295496 | tf_op jit(solution)/shard_map/ppermute | solution.py:14
  50.7 3.2 %collective-permute-done.3 = f32[1,24,1026]{2,1,0:T(8,128)S(1)} collective-permute-done((f32[1,24,1026]{2,1,0:T(8,128)S(1)}, f32[1,24,1026]{2,1,0:T(8,128)S(1)}, u32[]{:S(2)}, u32[]{:S(2)}) %collective-permute-start.3) | collective-permute-done | bytes 98528 | tf_op jit(solution)/shard_map/ppermute | solution.py:17
  53.9 2.7 %fusion.6 = f32[16,3,8,1024]{3,2,1,0:T(8,128)S(1)} fusion(f32[16,24,1024]{2,1,0:T(8,128)S(1)} %copy-done, f32[16,24,1]{2,1,0:T(8,128)} %collective-permute-done.1, f32[16,24,1]{2,1,0:T(8,128)S(1)} %copy-done.6, f32[1,24,1026]{2,1,0:T(8,128)S(1)} %collective-permute-done.3, f32[16,24,1026]{2,1,0:T(8,128)S(1)} %concatenate.58, ...), kind=kLoop, calls=%fused_computation.16 | loop fusion | flops 6684672 | bytes 4922016 | tf_op jit(solution)/shard_map/reshape | solution.py:68
  59.5 2.0 pad_maximum_fusion
  61.6 7.9 %copy.246 = f32[16,48,1024]{1,0,2:T(8,128)} copy(f32[16,48,1024]{2,1,0:T(8,128)} %pad_maximum_fusion) | data formatting | bytes 6291456 | tf_op jit(solution)/shard_map/concatenate | solution.py:141
  69.5 6.5 %gather_fusion = f32[512,16,48]{2,1,0:T(8,128)} fusion(f32[16,48,1024]{1,0,2:T(8,128)} %copy.246, s32[1024]{0:T(1024)S(1)} %pad_clamp_fusion.5), kind=kCustom, calls=%fused_computation.4 | custom fusion | bytes 3147776 | tf_op jit(solution)/shard_map/jit(_take)/gather | solution.py:152
  76.0 3.1 %copy.247 = f32[16,48,4,128]{3,1,0,2:T(8,128)S(1)} copy(f32[16,48,4,128]{1,0,3,2:T(8,128)} %bitcast.216) | data formatting | bytes 3145728 | tf_op jit(solution)/shard_map/jit(_take)/gather | solution.py:152
  82.5 30.2 %reduce-scatter.3.cloned.1.call-done = f32[16,48,1,128]{3,1,0,2:T(8,128)} async-done(((f32[16,48,4,128]{3,1,0,2:T(8,128)}), f32[16,48,1,128]{3,1,0,2:T(8,128)}) %reduce-scatter.3.cloned.1.call-update) | async-done | bytes 393232 | tf_op jit(solution)/shard_map/reduce_scatter | solution.py:154
  112.6 1.7 gather_fusion.1
  115.7 63.7 %reduce-scatter.5.cloned.1.call-done = f32[4,48,128]{2,1,0:T(8,128)} async-done(((f32[32,48,128]{2,1,0:T(8,128)}), f32[4,48,128]{2,1,0:T(8,128)}) %reduce-scatter.5.cloned.1.call-update) | async-done | bytes 98320 | tf_op jit(solution)/shard_map/reduce_scatter | solution.py:163
  182.5 3.3 %collective-permute-done.6 = f32[1,48,128]{2,1,0:T(8,128)S(1)} collective-permute-done((f32[1,48,128]{2,1,0:T(8,128)S(1)}, f32[1,48,128]{2,1,0:T(8,128)S(1)}, u32[]{:S(2)}, u32[]{:S(2)}) %collective-permute-start.6) | collective-permute-done | bytes 24608 | tf_op jit(solution)/shard_map/ppermute | solution.py:25
  187.9 3.1 %gather_fusion.4 = f32[512,16,48]{2,1,0:T(8,128)} fusion(f32[16,48,128]{1,0,2:T(8,128)S(1)} %copy.248, s32[1024]{0:T(1024)S(1)} %get-tuple-element.190), kind=kCustom, calls=%fused_computation.1.clone | custom fusion | bytes 3147776 | tf_op jit(solution)/shard_map/jit(_take)/gather | solution.py:98
  191.0 2.8 %copy.249 = f32[512,16,48]{0,2,1:T(8,128)S(1)} copy(f32[512,16,48]{2,1,0:T(8,128)} %gather_fusion.4) | data formatting | bytes 3145728 | tf_op jit(solution)/shard_map/jit(_take)/gather | solution.py:98
  193.9 3.1 %gather_fusion.5 = f32[512,16,48]{2,1,0:T(8,128)} fusion(f32[16,48,128]{1,0,2:T(8,128)S(1)} %copy.248, s32[1024]{0:T(1024)S(1)} %get-tuple-element.189), kind=kCustom, calls=%fused_computation.3.clone | custom fusion | bytes 3147776 | tf_op jit(solution)/shard_map/jit(_take)/gather | solution.py:99
  197.0 3.7 %copy.251 = f32[512,16,48]{0,2,1:T(8,128)} copy(f32[512,16,48]{2,1,0:T(8,128)} %gather_fusion.5) | data formatting | bytes 3145728 | tf_op jit(solution)/shard_map/jit(_take)/gather | solution.py:99
  200.7 1.8 fusion.14
  203.2 4.0 %collective-permute-start.7 = (f32[1,24,512]{2,1,0:T(8,128)S(1)}, f32[1,24,512]{2,1,0:T(8,128)S(1)}, u32[]{:S(2)}, u32[]{:S(2)}) collective-permute-start(f32[1,24,512]{2,1,0:T(8,128)S(1)} %get-tuple-element.147), channel_id=1, source_target_pairs={{0,1},{1,2},{2,3},{3,4},{4,5},{5,6},{6,7},{8,9},{9,10},{10,11},{11... | collective-permute-start | bytes 147464 | tf_op jit(solution)/shard_map/ppermute | solution.py:14
  209.0 4.3 %collective-permute-done.8 = f32[1,24,512]{2,1,0:T(8,128)S(1)} collective-permute-done((f32[1,24,512]{2,1,0:T(8,128)S(1)}, f32[1,24,512]{2,1,0:T(8,128)S(1)}, u32[]{:S(2)}, u32[]{:S(2)}) %collective-permute-start.8) | collective-permute-done | bytes 49184 | tf_op jit(solution)/shard_map/ppermute | solution.py:17
  217.2 4.5 %collective-permute-start.9 = (f32[1,24,512]{2,1,0:T(8,128)S(1)}, f32[1,24,512]{2,1,0:T(8,128)S(1)}, u32[]{:S(2)}, u32[]{:S(2)}) collective-permute-start(f32[1,24,512]{2,1,0:T(8,128)S(1)} %get-tuple-element.142), channel_id=1, source_target_pairs={{0,1},{1,2},{2,3},{3,4},{4,5},{5,6},{6,7},{8,9},{9,10},{10,11},{11... | collective-permute-start | bytes 147464 | tf_op jit(solution)/shard_map/ppermute | solution.py:14
  226.2 4.3 %collective-permute-start.11 = (f32[1,24,512]{2,1,0:T(8,128)S(1)}, f32[1,24,512]{2,1,0:T(8,128)S(1)}, u32[]{:S(2)}, u32[]{:S(2)}) collective-permute-start(f32[1,24,512]{2,1,0:T(8,128)S(1)} %get-tuple-element.137), channel_id=1, source_target_pairs={{0,1},{1,2},{2,3},{3,4},{4,5},{5,6},{6,7},{8,9},{9,10},{10,11},{11... | collective-permute-start | bytes 147464 | tf_op jit(solution)/shard_map/ppermute | solution.py:14
  232.2 5.5 %collective-permute-done.12 = f32[1,24,512]{2,1,0:T(8,128)S(1)} collective-permute-done((f32[1,24,512]{2,1,0:T(8,128)S(1)}, f32[1,24,512]{2,1,0:T(8,128)S(1)}, u32[]{:S(2)}, u32[]{:S(2)}) %collective-permute-start.12) | collective-permute-done | bytes 49184 | tf_op jit(solution)/shard_map/ppermute | solution.py:17
  (254 shorter events, 49.6 us)
Async XLA Ops:
  7.2 32.6 %copy-start = (f32[16,24,1024]{2,1,0:T(8,128)S(1)}, f32[16,24,1024]{2,1,0:T(8,128)}, u32[]{:S(2)}) copy-start(f32[16,24,1024]{2,1,0:T(8,128)} %param.11) | copy-start | bytes 4718596
  7.2 22.6 %copy-start.16 = (s32[4,4]{1,0:T(4,128)S(1)}, s32[4,4]{1,0:T(4,128)}, u32[]{:S(2)}) copy-start(s32[4,4]{1,0:T(4,128)} %param.17) | copy-start | bytes 196
  7.2 28.7 %copy-start.17 = (f32[2,24]{1,0:T(2,128)S(1)}, f32[2,24]{1,0:T(2,128)}, u32[]{:S(2)}) copy-start(f32[2,24]{1,0:T(2,128)} %param.14) | copy-start | bytes 580
  7.2 28.7 %copy-start.18 = (f32[2,8]{1,0:T(2,128)S(1)}, f32[2,8]{1,0:T(2,128)}, u32[]{:S(2)}) copy-start(f32[2,8]{1,0:T(2,128)} %param.15) | copy-start | bytes 196
  7.2 105.4 %reduce-scatter.3.cloned.1.call-start = ((), (), s32[]{:S(2)}) async-start(), calls=%async_computation.2 | async-start | bytes 1966080 | tf_op jit(solution)/shard_map/reduce_scatter | solution.py:154
  8.5 30.6 %collective-permute-start = (f32[16,24,1]{2,1,0:T(8,128)S(1)}, f32[16,24,1]{2,1,0:T(8,128)S(1)}, u32[]{:S(2)}, u32[]{:S(2)}) collective-permute-start(f32[16,24,1]{2,1,0:T(8,128)S(1)} %get-tuple-element.130), channel_id=1, source_target_pairs={{0,8},{8,16},{16,24},{1,9},{9,17},{17,25},{2,10},{10,18},{18,26},{... | collective-permute-start | bytes 4616 | tf_op jit(solution)/shard_map/ppermute | solution.py:14
  10.9 28.9 %collective-permute-start.1 = (f32[16,24,1]{2,1,0:T(8,128)S(1)}, f32[16,24,1]{2,1,0:T(8,128)}, u32[]{:S(2)}, u32[]{:S(2)}) collective-permute-start(f32[16,24,1]{2,1,0:T(8,128)S(1)} %get-tuple-element.131), channel_id=1, source_target_pairs={{8,0},{16,8},{24,16},{9,1},{17,9},{25,17},{10,2},{18,10},{26,18},{... | collective-permute-start | bytes 4616 | tf_op jit(solution)/shard_map/ppermute | solution.py:17
  17.7 30.1 %collective-permute-start.4 = (f32[1,24,512]{2,1,0:T(8,128)}, f32[1,24,512]{2,1,0:T(8,128)S(1)}, u32[]{:S(2)}, u32[]{:S(2)}) collective-permute-start(f32[1,24,512]{2,1,0:T(8,128)} %get-tuple-element.152), channel_id=1, source_target_pairs={{0,1},{1,2},{2,3},{3,4},{4,5},{5,6},{6,7},{8,9},{9,10},{10,11},{11... | collective-permute-start | bytes 147464 | tf_op jit(solution)/shard_map/ppermute | solution.py:14
  21.9 25.9 %collective-permute-start.5 = (f32[1,24,512]{2,1,0:T(8,128)}, f32[1,24,512]{2,1,0:T(8,128)S(1)}, u32[]{:S(2)}, u32[]{:S(2)}) collective-permute-start(f32[1,24,512]{2,1,0:T(8,128)} %get-tuple-element.153), channel_id=1, source_target_pairs={{1,0},{2,1},{3,2},{4,3},{5,4},{6,5},{7,6},{9,8},{10,9},{11,10},{12... | collective-permute-start | bytes 147464 | tf_op jit(solution)/shard_map/ppermute | solution.py:17
  41.8 8.9 %collective-permute-start.2 = (f32[1,24,1026]{2,1,0:T(8,128)S(1)}, f32[1,24,1026]{2,1,0:T(8,128)S(1)}, u32[]{:S(2)}, u32[]{:S(2)}) collective-permute-start(f32[1,24,1026]{2,1,0:T(8,128)S(1)} %get-tuple-element.125), channel_id=1, source_target_pairs={{0,1},{1,2},{2,3},{3,4},{4,5},{5,6},{6,7},{8,9},{9,10},{10,11},{11... | collective-permute-start | bytes 295496 | tf_op jit(solution)/shard_map/ppermute | solution.py:14
  46.5 7.4 %collective-permute-start.3 = (f32[1,24,1026]{2,1,0:T(8,128)S(1)}, f32[1,24,1026]{2,1,0:T(8,128)S(1)}, u32[]{:S(2)}, u32[]{:S(2)}) collective-permute-start(f32[1,24,1026]{2,1,0:T(8,128)S(1)} %get-tuple-element.126), channel_id=1, source_target_pairs={{1,0},{2,1},{3,2},{4,3},{5,4},{6,5},{7,6},{9,8},{10,9},{11,10},{12... | collective-permute-start | bytes 295496 | tf_op jit(solution)/shard_map/ppermute | solution.py:17
  80.4 98.9 %reduce-scatter.5.cloned.1.call-start = ((), (), s32[]{:S(2)}) async-start(), calls=%async_computation.3 | async-start | bytes 884736 | tf_op jit(solution)/shard_map/reduce_scatter | solution.py:163
  82.2 32.2 %copy-start.14 = (f32[32]{0:T(128)S(1)}, f32[32]{0:T(128)}, u32[]{:S(2)}) copy-start(f32[32]{0:T(128)} %get-tuple-element.183) | copy-start | bytes 388
  82.2 32.2 %copy-start.15 = (pred[32]{0:T(512)(128)(4,1)S(1)}, pred[32]{0:T(512)(128)(4,1)}, u32[]{:S(2)}) copy-start(pred[32]{0:T(512)(128)(4,1)} %get-tuple-element.184) | copy-start | bytes 100
  115.6 71.6 %copy-start.11 = (pred[16]{0:T(512)(128)(4,1)S(1)}, pred[16]{0:T(512)(128)(4,1)}, u32[]{:S(2)}) copy-start(pred[16]{0:T(512)(128)(4,1)} %get-tuple-element.81) | copy-start | bytes 52
  115.6 71.6 %copy-start.12 = (pred[16]{0:T(512)(128)(4,1)S(1)}, pred[16]{0:T(512)(128)(4,1)}, u32[]{:S(2)}) copy-start(pred[16]{0:T(512)(128)(4,1)} %get-tuple-element.181) | copy-start | bytes 52
  115.6 71.6 %copy-start.19 = (f32[16]{0:T(128)S(1)}, f32[16]{0:T(128)}, u32[]{:S(2)}) copy-start(f32[16]{0:T(128)} %convert_multiply_fusion) | copy-start | bytes 196
  180.1 5.7 %collective-permute-start.6 = (f32[1,48,128]{2,1,0:T(8,128)S(1)}, f32[1,48,128]{2,1,0:T(8,128)S(1)}, u32[]{:S(2)}, u32[]{:S(2)}) collective-permute-start(f32[1,48,128]{2,1,0:T(8,128)S(1)} %slice.855), channel_id=1, source_target_pairs={{1,0},{2,1},{3,2},{4,3},{5,4},{6,5},{7,6},{9,8},{10,9},{11,10},{12... | collective-permute-start | bytes 73736 | tf_op jit(solution)/shard_map/ppermute | solution.py:25
  203.2 5.8 %collective-permute-start.7 = (f32[1,24,512]{2,1,0:T(8,128)S(1)}, f32[1,24,512]{2,1,0:T(8,128)S(1)}, u32[]{:S(2)}, u32[]{:S(2)}) collective-permute-start(f32[1,24,512]{2,1,0:T(8,128)S(1)} %get-tuple-element.147), channel_id=1, source_target_pairs={{0,1},{1,2},{2,3},{3,4},{4,5},{5,6},{6,7},{8,9},{9,10},{10,11},{11... | collective-permute-start | bytes 147464 | tf_op jit(solution)/shard_map/ppermute | solution.py:14
  207.3 6.0 %collective-permute-start.8 = (f32[1,24,512]{2,1,0:T(8,128)S(1)}, f32[1,24,512]{2,1,0:T(8,128)S(1)}, u32[]{:S(2)}, u32[]{:S(2)}) collective-permute-start(f32[1,24,512]{2,1,0:T(8,128)S(1)} %get-tuple-element.148), channel_id=1, source_target_pairs={{1,0},{2,1},{3,2},{4,3},{5,4},{6,5},{7,6},{9,8},{10,9},{11,10},{12... | collective-permute-start | bytes 147464 | tf_op jit(solution)/shard_map/ppermute | solution.py:17
  215.9 6.0 %collective-permute-start.10 = (f32[1,24,512]{2,1,0:T(8,128)S(1)}, f32[1,24,512]{2,1,0:T(8,128)S(1)}, u32[]{:S(2)}, u32[]{:S(2)}) collective-permute-start(f32[1,24,512]{2,1,0:T(8,128)S(1)} %get-tuple-element.143), channel_id=1, source_target_pairs={{1,0},{2,1},{3,2},{4,3},{5,4},{6,5},{7,6},{9,8},{10,9},{11,10},{12... | collective-permute-start | bytes 147464 | tf_op jit(solution)/shard_map/ppermute | solution.py:17
  217.2 6.3 %collective-permute-start.9 = (f32[1,24,512]{2,1,0:T(8,128)S(1)}, f32[1,24,512]{2,1,0:T(8,128)S(1)}, u32[]{:S(2)}, u32[]{:S(2)}) collective-permute-start(f32[1,24,512]{2,1,0:T(8,128)S(1)} %get-tuple-element.142), channel_id=1, source_target_pairs={{0,1},{1,2},{2,3},{3,4},{4,5},{5,6},{6,7},{8,9},{9,10},{10,11},{11... | collective-permute-start | bytes 147464 | tf_op jit(solution)/shard_map/ppermute | solution.py:14
  226.2 6.0 %collective-permute-start.11 = (f32[1,24,512]{2,1,0:T(8,128)S(1)}, f32[1,24,512]{2,1,0:T(8,128)S(1)}, u32[]{:S(2)}, u32[]{:S(2)}) collective-permute-start(f32[1,24,512]{2,1,0:T(8,128)S(1)} %get-tuple-element.137), channel_id=1, source_target_pairs={{0,1},{1,2},{2,3},{3,4},{4,5},{5,6},{6,7},{8,9},{9,10},{10,11},{11... | collective-permute-start | bytes 147464 | tf_op jit(solution)/shard_map/ppermute | solution.py:14
  230.5 7.2 %collective-permute-start.12 = (f32[1,24,512]{2,1,0:T(8,128)S(1)}, f32[1,24,512]{2,1,0:T(8,128)S(1)}, u32[]{:S(2)}, u32[]{:S(2)}) collective-permute-start(f32[1,24,512]{2,1,0:T(8,128)S(1)} %get-tuple-element.138), channel_id=1, source_target_pairs={{1,0},{2,1},{3,2},{4,3},{5,4},{6,5},{7,6},{9,8},{10,9},{11,10},{12... | collective-permute-start | bytes 147464 | tf_op jit(solution)/shard_map/ppermute | solution.py:17
  (13 other events, 57.9 us)
Sparse Core Ops, SparseCore 0:
  80.6 32.0 reduce-scatter.2
  116.9 62.4 reduce-scatter.4
where the time goes:
time: 249 us; the launch traced here: 248 us
  waiting for transfers between devices  113 us (45%)
  local copies, waits for them, and re-layouts  45.9 us (18%)
  starting transfers between devices  33.7 us (14%)
  other arithmetic  32.2 us (13%)
  between operations  23.8 us (10%)
    reduce_scatter x1, waiting for transfers between devices, body(): lax.psum_scatter(taken * row_valid[:, None, None], 'tile', scatter_dimens...  63.7 us
    reduce_scatter x1, waiting for transfers between devices, body(): routed = lax.psum_scatter(picked, 'sec', scatter_dimension=2, tiled=True)  30.2 us
    ppermute x6, starting transfers between devices, extended_2(): lax.ppermute(lax.slice_in_dim(block, block.shape[dim] - width, None, axis...  24.1 us
    ppermute x6, waiting for transfers between devices, extended_2(): lax.ppermute(lax.slice_in_dim(block, 0, width, axis=dim), axis, backward)  13.1 us
    gather x2, local copies, waits for them, and re-layouts, body(): jnp.take(both_times, jnp.clip(col_ids, 0, cols_sec - 1).reshape(-1), axis=2)  9.51 us
    ppermute x6, starting transfers between devices, extended_2(): lax.ppermute(lax.slice_in_dim(block, 0, width, axis=dim), axis, backward)  7.97 us
    concatenate x1, local copies, waits for them, and re-layouts, body(): both_times = jnp.concatenate([parent_old, parent_new], axis=1)  7.91 us
    gather x2, local copies, waits for them, and re-layouts, upsample(): right_vals = jnp.take(row_mix, second_col, axis=2)  6.82 us
  transfers between devices with their start and end apart: 15, of which 10 were waited for; matrix products, arithmetic and copies ran while one was open for 8% of the time, Pallas kernels for 0%

commit v1 on v0

v1 whole, which is shorter than its diff:
```python
import jax
import jax.numpy as jnp
from jax import lax
from jax.experimental import pallas as pl
from jax.experimental.pallas import tpu as pltpu
from jax.sharding import PartitionSpec as P

NSTEP = 4
RATIO = 4
LANES = 128
F32 = jnp.float32
VMEM = pl.BlockSpec(memory_space=pltpu.VMEM)
SMEM = pl.BlockSpec(memory_space=pltpu.SMEM)


def call(kernel, outs, args, specs, scratch=(), limit=16, flops=0):
    single = not isinstance(outs, (list, tuple))
    shapes = [outs] if single else list(outs)
    moved = sum(4 * a.size for a in args) + sum(4 * s.size for s in shapes)
    out = pl.pallas_call(
        kernel,
        out_shape=shapes,
        in_specs=list(specs),
        out_specs=[VMEM] * len(shapes),
        scratch_shapes=list(scratch),
        compiler_params=pltpu.CompilerParams(vmem_limit_bytes=limit << 20),
        cost_estimate=pl.CostEstimate(flops=flops, bytes_accessed=moved, transcendentals=0),
    )(*args)
    return out[0] if single else out


def shape(*dims):
    return jax.ShapeDtypeStruct(dims, F32)


def lane_ids():
    return lax.broadcasted_iota(jnp.int32, (8, LANES), 1)


def sublane_ids():
    return lax.broadcasted_iota(jnp.int32, (8, LANES), 0)


def exchange(block, axis, bit):
    return lax.ppermute(block, axis, [(i, i ^ bit) for i in range(lax.axis_size(axis))])


def extract(rows, chan, box, parent, keep, send):
    cols = parent.shape[1]
    blocks = cols // LANES
    sec = lax.axis_index("sec")
    half = lax.rem(sec, 2)
    lane = lane_ids()
    groups = chan // 8
    for which, dest in ((1 - half, send), (half, keep)):
        for i in range(dest.shape[0]):
            nest = 2 * i + which
            offset = box[nest, 1] - sec * cols
            first = lax.shift_right_arithmetic(offset, 7)
            shift = lax.bitwise_and(offset, LANES - 1)
            back = lax.bitwise_and(LANES - shift, LANES - 1)

            def place(k):
                start = pl.multiple_of(jnp.clip(k, 0, blocks - 1) * LANES, LANES)
                return start, jnp.where((k >= 0) & (k < blocks), 1.0, 0.0).astype(F32)

            start_a, on_a = place(first)
            start_b, on_b = place(first + 1)
            start_c, on_c = place(first - 1)
            is_low = jnp.where(nest == sec + 1, 1.0, 0.0).astype(F32)
            is_high = jnp.where(nest == sec - 1, 1.0, 0.0).astype(F32)
            extra = [jnp.zeros((8, LANES), F32) for _ in range(groups)]
            for row in range(rows):
                for g in range(groups):
                    at = pl.ds(row * chan + 8 * g, 8)
                    a = pltpu.roll(parent[at, pl.ds(start_a, LANES)] * on_a, back, axis=1)
                    b = pltpu.roll(parent[at, pl.ds(start_b, LANES)] * on_b, back, axis=1)
                    c = parent[at, pl.ds(start_c, LANES)] * on_c
                    dest[i, at, :] = jnp.where(lane < LANES - shift, a, b)
                    west = jnp.where(shift == 0, c, a)
                    last = parent[at, pl.ds(cols - LANES, LANES)] * is_low
                    head = parent[at, pl.ds(0, LANES)] * is_high
                    e = extra[g]
                    e = jnp.where(lane == row, pltpu.roll(west, row + 1, axis=1), e)
                    e = jnp.where(lane == rows + row, pltpu.roll(b, rows + row, axis=1), e)
                    e = jnp.where(lane == 2 * rows + row, pltpu.roll(last, 2 * rows + row + 1, axis=1), e)
                    e = jnp.where(lane == 3 * rows + row, pltpu.roll(head, 3 * rows + row, axis=1), e)
                    extra[g] = e
            for g in range(groups):
                dest[i, pl.ds(rows * chan + 8 * g, 8), :] = extra[g]


def combine(bit, own, got, keep, send):
    mine = lax.rem(lax.axis_index("sec") // bit, 2)
    for i in range(keep.shape[0]):
        send[i] = own[2 * i + 1 - mine] + got[2 * i + 1 - mine]
        keep[i] = own[2 * i + mine] + got[2 * i + mine]


def total(own, got, out):
    out[...] = own[0] + got[0]


def held_block(anchor, rows, own_rows, group):
    tile = lax.axis_index("tile")
    first = lax.div(tile, group) * group
    low = jnp.maximum(anchor + own_rows * first - 2, 0)
    base = lax.div(low, rows)
    return base + lax.bitwise_and(tile - base, group - 1)


def choose(rows, own_rows, group, count, box, own, got, out):
    anchor = box[lax.axis_index("sec"), 0]
    before = held_block(anchor, rows, own_rows, 2 * group)
    if 2 * group == count:
        before = lax.axis_index("tile")
    after = held_block(anchor, rows, own_rows, group)

    @pl.when(before == after)
    def _():
        out[...] = own[...]

    @pl.when(before != after)
    def _():
        out[...] = got[...]


def window(rows, chan, own_rows, box, block, out):
    tile = lax.bitwise_xor(lax.axis_index("tile"), 1)
    start = box[lax.axis_index("sec"), 0] + own_rows * tile - 2
    span = out.shape[0] // chan - 1
    for m in range(span):
        at = pl.multiple_of(lax.bitwise_and(start + m, rows - 1) * chan, 8)
        out[pl.ds(m * chan, chan), :] = block[pl.ds(at, chan), :]
    out[pl.ds(span * chan, chan), :] = block[pl.ds(rows * chan, chan), :]


def coefficients(levels, mix, coef):
    for f in range(3):
        m = jnp.full((8, LANES), mix[f], F32)
        ratio = None
        for l in range(levels):
            pivot = 1.0 + (1.0 if l in (0, levels - 1) else 2.0) * m
            if l:
                pivot = pivot - m * ratio
            inverse = 1.0 / pivot
            ratio = m * inverse
            coef[f, 0, l] = inverse
            coef[f, 1, l] = ratio


def step_block(levels, diff, wind, conv, mix, coef, loads, store):
    passed = None
    for f in range(3):
        m = mix[f]
        ys, carry = [], []
        for l in range(levels):
            c = f * levels + l
            v, n, s, w, e = loads(c)
            d, wx, wy = diff[c], wind[0, c], wind[1, c]
            h = (1.0 - 4.0 * d - wx - wy) * v + (d + wx) * n + (d + wy) * w + d * (s + e)
            if passed is not None:
                h = h + passed[l]
            if f < 2:
                out = conv[f, l] * h
                carry.append(out)
                h = h - out
            if l:
                h = h + coef[f, 1, l - 1] * ys[-1]
            ys.append(h)
        passed = carry
        x = None
        for l in range(levels - 1, -1, -1):
            x = coef[f, 0, l] * (ys[l] if x is None else ys[l] + m * x)
            store(f * levels + l, x)


def parent_step(rows, chan, diff, wind, conv, mix, parent, low, high, strip, out, ext, done, coef, sems):
    levels = conv.shape[1]
    blocks = parent.shape[1] // LANES
    coefficients(levels, mix, coef)
    lane = lane_ids()

    def columns(j):
        return pl.ds(pl.multiple_of(j * LANES, LANES), LANES)

    for row in range(rows):
        for g in range(chan // 8):
            packed = strip[pl.ds(rows * chan + 8 * g, 8), :]
            at = pl.ds((row + 1) * chan + 8 * g, 8)
            ext[0, at, :] = pltpu.roll(packed, LANES - 1 - (2 * rows + row), axis=1)
            ext[blocks + 1, at, :] = pltpu.roll(packed, LANES - (3 * rows + row), axis=1)

    @pl.loop(0, blocks)
    def _(j):
        ext[j + 1, pl.ds(0, chan), :] = low[:, columns(j)]
        ext[j + 1, pl.ds(chan, rows * chan), :] = parent[:, columns(j)]
        ext[j + 1, pl.ds((rows + 1) * chan, chan), :] = high[:, columns(j)]

    @pl.loop(0, blocks)
    def _(j):
        for first in range(0, rows, 8):
            def loads(c):
                def at(r):
                    return pl.ds((first + r) * chan + c, 8, stride=chan)

                v = ext[j + 1, at(1), :]
                w = pltpu.roll(jnp.where(lane == LANES - 1, ext[j, at(1), :], v), 1, axis=1)
                e = pltpu.roll(jnp.where(lane == 0, ext[j + 2, at(1), :], v), LANES - 1, axis=1)
                return v, ext[j + 1, at(0), :], ext[j + 1, at(2), :], w, e

            def store(c, x):
                done[j, pl.ds(first * chan + c, 8, stride=chan), :] = x

            step_block(levels, diff, wind, conv, mix, coef, loads, store)
        pltpu.make_async_copy(done.at[j], out.at[:, columns(j)], sems.at[j]).start()

    @pl.loop(0, blocks)
    def _(j):
        pltpu.make_async_copy(done.at[j], out.at[:, columns(j)], sems.at[j]).wait()


def nest_step(
    rows, chan, own_rows, tiles, parent_rows,
    box, diff, wind, conv, mix, block, got, nest, low, high, out,
    natural, foot, up, state, force, nudge, done, coef, sems,
):
    levels = conv.shape[1]
    nest_rows = nest.shape[0] // chan
    col_blocks = nest.shape[1] // LANES
    deep = low.shape[0] // chan
    ext_rows = nest_rows + 2 * deep
    sec, tile = lax.axis_index("sec"), lax.axis_index("tile")
    anchor, extent_x, extent_y = box[sec, 0], box[sec, 2], box[sec, 3]
    lane, sub = lane_ids(), sublane_ids()
    first_row = nest_rows * tile - deep
    zero = jnp.zeros((8, LANES), F32)

    def columns(j):
        return pl.ds(j * LANES, LANES)

    coefficients(levels, mix, coef)

    for j in range(col_blocks):
        natural[j, pl.ds(0, deep * chan), :] = low[:, columns(j)]
        natural[j, pl.ds(deep * chan, nest_rows * chan), :] = nest[:, columns(j)]
        natural[j, pl.ds((deep + nest_rows) * chan, deep * chan), :] = high[:, columns(j)]

    for j in range(col_blocks):
        for rb in range(0, ext_rows, 8):
            i = first_row + rb + sub
            col = j * LANES + lane
            live = jnp.where((i >= 0) & (i < extent_x) & (col < extent_y), 1.0, 0.0).astype(F32)
            dist = jnp.minimum(jnp.minimum(i, col), jnp.minimum(extent_x - 1 - i, extent_y - 1 - col))
            dist = jnp.maximum(dist, 0).astype(F32)
            rate = 0.1 + 0.4 * jnp.exp(-dist / 3.0)
            nudge[0, j, pl.ds(rb, 8), :] = live * (1.0 - rate)
            nudge[1, j, pl.ds(rb, 8), :] = live * rate
            nudge[2, j, pl.ds(rb, 8), :] = live

    @pl.loop(0, chan)
    def _(c):
        for k in range(2):
            for r in range(0, ext_rows + 16, 8):
                state[k, 0, c, pl.ds(r, 8), :] = zero
                state[k, col_blocks + 1, c, pl.ds(r, 8), :] = zero
            for j in range(col_blocks):
                state[k, j + 1, c, pl.ds(0, 8), :] = zero
                state[k, j + 1, c, pl.ds(ext_rows + 8, 8), :] = zero
        for j in range(col_blocks):
            for rb in range(0, ext_rows, 8):
                v = natural[j, pl.ds(rb * chan + c, 8, stride=chan), :]
                state[0, j + 1, c, pl.ds(8 + rb, 8), :] = v * nudge[2, j, pl.ds(rb, 8), :]

    span = got.shape[0] // chan - 1
    start = anchor + own_rows * tile - 2
    side = lax.rem(tile, 2)
    for m in range(span):
        row = start + m
        local = lax.bitwise_and(row, rows - 1)
        inside = jnp.where((row >= 0) & (row < parent_rows), 1.0, 0.0).astype(F32)
        ours = lax.rem(lax.div(jnp.maximum(row, 0), rows), 2) == side
        west_by = lax.bitwise_and(LANES - 1 - local, LANES - 1)
        east_by = lax.bitwise_and(LANES - rows - local, LANES - 1)
        for g in range(chan // 8):
            mine = block[pl.ds(pl.multiple_of(local * chan + 8 * g, 8), 8), :]
            theirs = got[pl.ds(m * chan + 8 * g, 8), :]
            edge_mine = block[pl.ds(rows * chan + 8 * g, 8), :]
            edge_theirs = got[pl.ds(span * chan + 8 * g, 8), :]
            edge = jnp.where(ours, edge_mine, edge_theirs) * inside
            at = pl.ds(m * chan + 8 * g, 8)
            foot[0, at, :] = pltpu.roll(edge, west_by, axis=1)
            foot[1, at, :] = jnp.where(ours, mine, theirs) * inside
            foot[2, at, :] = pltpu.roll(edge, east_by, axis=1)
    foot[:, pl.ds(span * chan, chan), :] = jnp.zeros((3, chan, LANES), F32)

    def foot_loads(c):
        def at(r):
            return pl.ds(r * chan + c, 8, stride=chan)

        v = foot[1, at(1), :]
        w = pltpu.roll(jnp.where(lane == LANES - 1, foot[0, at(1), :], v), 1, axis=1)
        e = pltpu.roll(jnp.where(lane == 0, foot[2, at(1), :], v), LANES - 1, axis=1)
        return v, foot[1, at(0), :], foot[1, at(2), :], w, e

    def foot_store(c, x):
        old = foot[1, pl.ds(chan + c, 8, stride=chan), :]
        per = LANES // RATIO
        q = lax.rem(lane, RATIO).astype(F32) / RATIO
        for j in range(col_blocks):
            left = j * per + lax.div(lane, RATIO)
            right = jnp.minimum(left + 1, LANES - 1)
            for k, value in enumerate((old, x - old)):
                a = jnp.take_along_axis(value, left, axis=1)
                b = jnp.take_along_axis(value, right, axis=1)
                up[k, j, c] = a + q * (b - a)

    step_block(levels, diff, wind, conv, mix, coef, foot_loads, foot_store)

    @pl.loop(0, chan)
    def _(c):
        for rb in range(0, ext_rows, 8):
            u = rb // RATIO
            i = first_row + rb + sub
            p = lax.rem(sub, RATIO).astype(F32) / RATIO
            p = jnp.where(i >= RATIO * (own_rows * tiles - 1), 0.0, p)
            for j in range(col_blocks):
                b = nudge[1, j, pl.ds(rb, 8), :]
                for k in range(2):
                    r0 = jnp.broadcast_to(up[k, j, c, pl.ds(u, 1), :], (8, LANES))
                    r1 = jnp.broadcast_to(up[k, j, c, pl.ds(u + 1, 1), :], (8, LANES))
                    r2 = jnp.broadcast_to(up[k, j, c, pl.ds(u + 2, 1), :], (8, LANES))
                    a0 = jnp.where(sub < RATIO, r0, r1)
                    a1 = jnp.where(sub < RATIO, r1, r2)
                    force[k, j, c, pl.ds(rb, 8), :] = b * (a0 + p * (a1 - a0))

    for step in range(NSTEP):
        weight = (step + 1) / NSTEP
        last = step == NSTEP - 1
        src, dst = step % 2, (step + 1) % 2

        @pl.loop(0, col_blocks)
        def _(j):
            for rb in range(deep, deep + nest_rows, 8) if last else range(0, ext_rows, 8):
                def loads(c):
                    v = state[src, j + 1, c, pl.ds(8 + rb, 8), :]
                    west = state[src, j, c, pl.ds(8 + rb, 8), :]
                    east = state[src, j + 2, c, pl.ds(8 + rb, 8), :]
                    w = pltpu.roll(jnp.where(lane == LANES - 1, west, v), 1, axis=1)
                    e = pltpu.roll(jnp.where(lane == 0, east, v), LANES - 1, axis=1)
                    n = state[src, j + 1, c, pl.ds(7 + rb, 8), :]
                    return v, n, state[src, j + 1, c, pl.ds(9 + rb, 8), :], w, e

                def store(c, x):
                    at = pl.ds(rb, 8)
                    g = force[0, j, c, at, :] + weight * force[1, j, c, at, :]
                    x = nudge[0, j, at, :] * x + g
                    if last:
                        done[j, pl.ds((rb - deep) * chan + c, 8, stride=chan), :] = x
                    else:
                        state[dst, j + 1, c, pl.ds(8 + rb, 8), :] = x

                step_block(levels, diff, wind, conv, mix, coef, loads, store)
            if last:
                at = pl.ds(pl.multiple_of(j * LANES, LANES), LANES)
                pltpu.make_async_copy(done.at[j], out.at[:, at], sems.at[j]).start()

    for j in range(col_blocks):
        pltpu.make_async_copy(done.at[j], out.at[:, columns(j)], sems.at[j]).wait()


def bound(kernel, *static):
    def run(*refs):
        return kernel(*static, *refs)

    return run


def body(parent_old, nest_state, diffusion, wind_speed, conversion, vert_mix, nest_box):
    rows, chan, cols = parent_old.shape
    nest_rows, nest_cols = nest_state.shape[1], nest_state.shape[3]
    secs, tiles = lax.axis_size("sec"), lax.axis_size("tile")
    own_rows = nest_rows // RATIO
    levels = conversion.shape[1]
    deep = NSTEP
    ext_rows = nest_rows + 2 * deep
    col_blocks = nest_cols // LANES
    blocks = cols // LANES
    span = (ext_rows // RATIO + 1) + 2
    strip_rows = (rows + 1) * chan
    parent = parent_old.reshape(rows * chan, cols)
    nest = nest_state.reshape(nest_rows * chan, nest_cols)
    params = (diffusion, wind_speed, conversion, vert_mix)

    def neighbours(block, axis, low, high):
        forward = [(i, i + 1) for i in range(lax.axis_size(axis) - 1)]
        backward = [(j, i) for i, j in forward]
        return lax.ppermute(high, axis, forward), lax.ppermute(low, axis, backward)

    half = shape(secs // 2, strip_rows, LANES)
    keep, send = call(
        bound(extract, rows, chan), [half, half], (nest_box, parent), (SMEM, VMEM)
    )
    got = exchange(send, "sec", 1)
    bit = 2
    while bit < secs:
        half = shape(secs // (2 * bit), strip_rows, LANES)
        keep, send = call(
            bound(combine, bit), [half, half], (keep, got), (VMEM, VMEM)
        )
        got = exchange(send, "sec", bit)
        bit *= 2
    strip = call(total, shape(strip_rows, LANES), (keep, got), (VMEM, VMEM))

    nest_low, nest_high = neighbours(nest, "tile", nest[: deep * chan], nest[-deep * chan :])
    parent_low, parent_high = neighbours(parent, "tile", parent[:chan], parent[-chan:])

    block = strip
    group = tiles // 2
    while group > 1:
        got = exchange(block, "tile", group)
        block = call(
            bound(choose, rows, own_rows, group, tiles), shape(strip_rows, LANES),
            (nest_box, block, got), (SMEM, VMEM, VMEM),
        )
        group //= 2
    message = call(
        bound(window, rows, chan, own_rows), shape((span + 1) * chan, LANES),
        (nest_box, block), (SMEM, VMEM),
    )
    got = exchange(message, "tile", 1)

    parent_new = pl.pallas_call(
        bound(parent_step, rows, chan),
        out_shape=shape(rows * chan, cols),
        in_specs=[SMEM] * 4 + [VMEM] * 4,
        out_specs=pl.BlockSpec(memory_space=pl.ANY),
        scratch_shapes=[
            pltpu.VMEM((blocks + 2, (rows + 2) * chan, LANES), F32),
            pltpu.VMEM((blocks, rows * chan, LANES), F32),
            pltpu.VMEM((3, 2, levels, 8, LANES), F32),
            pltpu.SemaphoreType.DMA((blocks,)),
        ],
        compiler_params=pltpu.CompilerParams(vmem_limit_bytes=16 << 20),
        cost_estimate=pl.CostEstimate(flops=30 * parent.size, bytes_accessed=8 * parent.size, transcendentals=0),
    )(*params, parent, parent_low, parent_high, strip)

    nest_new = pl.pallas_call(
        bound(nest_step, rows, chan, own_rows, tiles, rows * tiles),
        out_shape=shape(nest_rows * chan, nest_cols),
        in_specs=[SMEM] * 5 + [VMEM] * 5,
        out_specs=pl.BlockSpec(memory_space=pl.ANY),
        scratch_shapes=[
            pltpu.VMEM((col_blocks, ext_rows * chan, LANES), F32),
            pltpu.VMEM((3, (span + 1) * chan, LANES), F32),
            pltpu.VMEM((2, col_blocks, chan, 8, LANES), F32),
            pltpu.VMEM((2, col_blocks + 2, chan, ext_rows + 16, LANES), F32),
            pltpu.VMEM((2, col_blocks, chan, ext_rows, LANES), F32),
            pltpu.VMEM((3, col_blocks, ext_rows, LANES), F32),
            pltpu.VMEM((col_blocks, nest_rows * chan, LANES), F32),
            pltpu.VMEM((3, 2, levels, 8, LANES), F32),
            pltpu.SemaphoreType.DMA((col_blocks,)),
        ],
        compiler_params=pltpu.CompilerParams(vmem_limit_bytes=32 << 20),
        cost_estimate=pl.CostEstimate(flops=120 * nest.size, bytes_accessed=16 * nest.size, transcendentals=0),
    )(nest_box, *params, block, got, nest, nest_low, nest_high)

    return (
        parent_new.reshape(parent_old.shape),
        nest_new.reshape(nest_state.shape),
    )


def solution(mesh):
    placed = (P("tile", None, "sec"), P("sec", "tile", None, None), P(), P(), P(), P(), P())
    return jax.shard_map(
        body,
        mesh=mesh,
        in_specs=placed,
        out_specs=(P("tile", None, "sec"), P("sec", "tile", None, None)),
        check_vma=False,
    )
```

time: 249 us -> 73.1 us (0.29)
  the two profiles are of different devices: /device:TPU:0 before, /device:TPU:9 now
where the time goes in v1:
time: 73.1 us; the launch traced here: 72.8 us
  Pallas kernels  27.6 us (38%)
  waiting for transfers between devices  24 us (33%)
  starting transfers between devices  18.2 us (25%)
  local copies, waits for them, and re-layouts  2.15 us (3%)
  between operations  0.8 us (1%)
    ppermute x5, waiting for transfers between devices, exchange(): lax.ppermute(block, axis, [(i, i ^ bit) for i in range(lax.axis_size(axis...  15.8 us
    pallas_call x6, Pallas kernels, call(): pl.pallas_call(kernel, out_shape=shapes, in_specs=list(specs), out_specs=...  14.7 us
    pallas_call x1, Pallas kernels, body(): pl.pallas_call(bound(nest_step, rows, chan, own_rows, tiles, rows * tiles...  9.44 us
    ppermute x2, waiting for transfers between devices, neighbours(): lax.ppermute(low, axis, backward)  8.24 us
    ppermute x5, starting transfers between devices, exchange(): lax.ppermute(block, axis, [(i, i ^ bit) for i in range(lax.axis_size(axis...  6.76 us
    ppermute x2, starting transfers between devices, neighbours(): lax.ppermute(high, axis, forward)  6.29 us
    ppermute x2, starting transfers between devices, neighbours(): lax.ppermute(low, axis, backward)  5.17 us
    pallas_call x1, Pallas kernels, body(): pl.pallas_call(bound(parent_step, rows, chan), out_shape=shape(rows * cha...  3.5 us
  transfers between devices with their start and end apart: 9, of which 4 were waited for; matrix products, arithmetic and copies ran while one was open for 0% of the time, Pallas kernels for 6%

profile of v1, /device:TPU:9, one launch (start us, length us, event | category | flops | bytes accessed | tf_op | source)
XLA Modules:
  0.0 72.8 jit_solution(13707103488937422413)
XLA Ops:
  0.6 0.0 copy-start
  0.6 1.4 %copy-done = f32[16,24,1024]{2,1,0:T(8,128)S(1)} copy-done((f32[16,24,1024]{2,1,0:T(8,128)S(1)}, f32[16,24,1024]{2,1,0:T(8,128)}, u32[]{:S(2)}) %copy-start) | copy-done | bytes 1572888
  2.0 0.7 copy-done.3
  2.7 12.8 %shard_map.86 = (f32[2,408,128]{2,1,0:T(8,128)S(1)}, f32[2,408,128]{2,1,0:T(8,128)S(1)}) custom-call(s32[4,4]{1,0:T(4,128)S(1)} %copy-done.3, f32[384,1024]{1,0:T(8,128)S(1)} %bitcast.10), custom_call_target="tpu_custom_call" | custom-call | bytes 2408512 | tf_op jit(solution)/shard_map/pallas_call | solution.py:20
  15.5 0.7 %collective-permute-start.2 = (f32[2,408,128]{2,1,0:T(8,128)S(1)}, f32[2,408,128]{2,1,0:T(8,128)S(1)}, u32[]{:S(2)}, u32[]{:S(2)}) collective-permute-start(f32[2,408,128]{2,1,0:T(8,128)S(1)} %get-tuple-element.7), channel_id=1, source_target_pairs={{0,8},{8,0},{16,24},{24,16},{1,9},{9,1},{17,25},{25,17},{2,10},{10... | collective-permute-start | bytes 1253384 | tf_op jit(solution)/shard_map/ppermute | solution.py:45
  16.3 1.4 %collective-permute-done.2.refs_1_ = f32[2,408,128]{2,1,0:T(8,128)S(1)} collective-permute-done((f32[2,408,128]{2,1,0:T(8,128)S(1)}, f32[2,408,128]{2,1,0:T(8,128)S(1)}, u32[]{:S(2)}, u32[]{:S(2)}) %collective-permute-start.2) | collective-permute-done | bytes 417824 | tf_op jit(solution)/shard_map/ppermute | solution.py:45
  17.7 0.0 copy-start.1
  17.7 1.3 %collective-permute-start.3 = (f32[1,408,128]{2,1,0:T(8,128)S(1)}, f32[1,408,128]{2,1,0:T(8,128)S(1)}, u32[]{:S(2)}, u32[]{:S(2)}) collective-permute-start(f32[1,408,128]{2,1,0:T(8,128)S(1)} %get-tuple-element.9), channel_id=1, source_target_pairs={{0,16},{8,24},{16,0},{24,8},{1,17},{9,25},{17,1},{25,9},{2,18},{10... | collective-permute-start | bytes 626696 | tf_op jit(solution)/shard_map/ppermute | solution.py:45
  19.0 5.1 %collective-permute-done.3.got = f32[1,408,128]{2,1,0:T(8,128)S(1)} collective-permute-done((f32[1,408,128]{2,1,0:T(8,128)S(1)}, f32[1,408,128]{2,1,0:T(8,128)S(1)}, u32[]{:S(2)}, u32[]{:S(2)}) %collective-permute-start.3) | collective-permute-done | bytes 208928 | tf_op jit(solution)/shard_map/ppermute | solution.py:45
  24.2 2.4 %collective-permute-start.4 = (f32[408,128]{1,0:T(8,128)S(1)}, f32[408,128]{1,0:T(8,128)S(1)}, u32[]{:S(2)}, u32[]{:S(2)}) collective-permute-start(f32[408,128]{1,0:T(8,128)S(1)} %shard_map.88.refs_7_.refs_1_), channel_id=1, source_target_pairs={{0,4},{1,5},{2,6},{3,7},{4,0},{5,1},{6,2},{7,3},{8,12},{9,13},{10,... | collective-permute-start | bytes 626696 | tf_op jit(solution)/shard_map/ppermute | solution.py:45
  26.6 9.2 %collective-permute-done.4.refs_2_ = f32[408,128]{1,0:T(8,128)S(1)} collective-permute-done((f32[408,128]{1,0:T(8,128)S(1)}, f32[408,128]{1,0:T(8,128)S(1)}, u32[]{:S(2)}, u32[]{:S(2)}) %collective-permute-start.4) | collective-permute-done | bytes 208928 | tf_op jit(solution)/shard_map/ppermute | solution.py:45
  35.8 0.6 shard_map.90.refs_1_
  36.4 0.3 collective-permute-start.5
  36.8 2.9 %collective-permute-start.7 = (f32[96,512]{1,0:T(8,128)S(1)}, f32[96,512]{1,0:T(8,128)S(1)}, u32[]{:S(2)}, u32[]{:S(2)}) collective-permute-start(f32[96,512]{1,0:T(8,128)S(1)} %bitcast.16), channel_id=1, source_target_pairs={{0,1},{1,2},{2,3},{3,4},{4,5},{5,6},{6,7},{8,9},{9,10},{10,11},{11... | collective-permute-start | bytes 589832 | tf_op jit(solution)/shard_map/ppermute | solution.py:398
  39.7 3.2 %collective-permute-start.8 = (f32[96,512]{1,0:T(8,128)S(1)}, f32[96,512]{1,0:T(8,128)S(1)}, u32[]{:S(2)}, u32[]{:S(2)}) collective-permute-start(f32[96,512]{1,0:T(8,128)S(1)} %bitcast.15), channel_id=1, source_target_pairs={{1,0},{2,1},{3,2},{4,3},{5,4},{6,5},{7,6},{9,8},{10,9},{11,10},{12... | collective-permute-start | bytes 589832 | tf_op jit(solution)/shard_map/ppermute | solution.py:398
  43.0 0.0 collective-permute-done.5.refs_2_
  43.0 0.6 shard_map.91.refs_1_.refs_5_
  43.6 0.6 shard_map.92
  44.2 2.1 %collective-permute-start.6 = (f32[240,128]{1,0:T(8,128)S(1)}, f32[240,128]{1,0:T(8,128)S(1)}, u32[]{:S(2)}, u32[]{:S(2)}) collective-permute-start(f32[240,128]{1,0:T(8,128)S(1)} %shard_map.92), channel_id=1, source_target_pairs={{0,1},{1,0},{2,3},{3,2},{4,5},{5,4},{6,7},{7,6},{8,9},{9,8},{10,11... | collective-permute-start | bytes 368648 | tf_op jit(solution)/shard_map/ppermute | solution.py:45
  46.3 1.9 %collective-permute-start.1 = (f32[24,1024]{1,0:T(8,128)S(1)}, f32[24,1024]{1,0:T(8,128)S(1)}, u32[]{:S(2)}, u32[]{:S(2)}) collective-permute-start(f32[24,1024]{1,0:T(8,128)S(1)} %get-tuple-element.10), channel_id=1, source_target_pairs={{1,0},{2,1},{3,2},{4,3},{5,4},{6,5},{7,6},{9,8},{10,9},{11,10},{12... | collective-permute-start | bytes 294920 | tf_op jit(solution)/shard_map/ppermute | solution.py:398
  48.2 3.4 %collective-permute-start = (f32[24,1024]{1,0:T(8,128)S(1)}, f32[24,1024]{1,0:T(8,128)S(1)}, u32[]{:S(2)}, u32[]{:S(2)}) collective-permute-start(f32[24,1024]{1,0:T(8,128)S(1)} %get-tuple-element.11), channel_id=1, source_target_pairs={{0,1},{1,2},{2,3},{3,4},{4,5},{5,6},{6,7},{8,9},{9,10},{10,11},{11... | collective-permute-start | bytes 294920 | tf_op jit(solution)/shard_map/ppermute | solution.py:398
  51.6 8.2 %collective-permute-done.1.refs_6_ = f32[24,1024]{1,0:T(8,128)S(1)} collective-permute-done((f32[24,1024]{1,0:T(8,128)S(1)}, f32[24,1024]{1,0:T(8,128)S(1)}, u32[]{:S(2)}, u32[]{:S(2)}) %collective-permute-start.1) | collective-permute-done | bytes 98336 | tf_op jit(solution)/shard_map/ppermute | solution.py:398
  59.8 3.5 %shard_map.89 = f32[384,1024]{1,0:T(8,128)} custom-call(f32[24]{0:T(128)S(1)} %copy-done.7, f32[2,24]{1,0:T(2,128)S(1)} %copy-done.5, f32[2,8]{1,0:T(2,128)S(1)} %copy-done.6, f32[3]{0:T(128)S(1)} %copy-done.8, f32[384,1024]{1,0:T(8,128)S(1)} %bitcast.11, f32[24,1024]{1,0:T(8,128)S(1)} %collective-permute-done.refs_5_, ...), custom_call_target="tpu_custom_call" | custom-call | flops 11796480 | bytes 3145728 | tf_op jit(solution)/shard_map/pallas_call | solution.py:433
  63.4 9.4 %shard_map.93 = f32[384,512]{1,0:T(8,128)} custom-call(s32[4,4]{1,0:T(4,128)S(1)} %copy-done.4, f32[24]{0:T(128)S(1)} %copy-done.7, f32[2,24]{1,0:T(2,128)S(1)} %copy-done.5, f32[2,8]{1,0:T(2,128)S(1)} %copy-done.6, f32[3]{0:T(128)S(1)} %copy-done.8, f32[408,128]{1,0:T(8,128)S(1)} %shard_map.91.refs_1_.refs_5_, ...), custom_call_target="tpu_custom_call" | custom-call | flops 23592960 | bytes 3145728 | tf_op jit(solution)/shard_map/pallas_call | solution.py:448
  (22 shorter events, 0.2 us)
Async XLA Ops:
  0.6 1.4 %copy-start = (f32[16,24,1024]{2,1,0:T(8,128)S(1)}, f32[16,24,1024]{2,1,0:T(8,128)}, u32[]{:S(2)}) copy-start(f32[16,24,1024]{2,1,0:T(8,128)} %param.7) | copy-start | bytes 4718596
  2.0 0.7 copy-start.3
  2.7 33.1 %copy-start.4 = (s32[4,4]{1,0:T(4,128)S(1)}, s32[4,4]{1,0:T(4,128)}, u32[]{:S(2)}) copy-start(s32[4,4]{1,0:T(4,128)} %refs_0_.11) | copy-start | bytes 196
  2.7 34.0 %copy-start.2 = (f32[1,16,24,512]{3,2,1,0:T(8,128)S(1)}, f32[1,16,24,512]{3,2,1,0:T(8,128)}, u32[]{:S(2)}) copy-start(f32[1,16,24,512]{3,2,1,0:T(8,128)} %param.8) | copy-start | bytes 2359300
  15.5 2.1 %collective-permute-start.2 = (f32[2,408,128]{2,1,0:T(8,128)S(1)}, f32[2,408,128]{2,1,0:T(8,128)S(1)}, u32[]{:S(2)}, u32[]{:S(2)}) collective-permute-start(f32[2,408,128]{2,1,0:T(8,128)S(1)} %get-tuple-element.7), channel_id=1, source_target_pairs={{0,8},{8,0},{16,24},{24,16},{1,9},{9,1},{17,25},{25,17},{2,10},{10... | collective-permute-start | bytes 1253384 | tf_op jit(solution)/shard_map/ppermute | solution.py:45
  17.7 28.5 %copy-start.1 = (f32[16,24,1024]{2,1,0:T(8,128)S(1)}, f32[16,24,1024]{2,1,0:T(8,128)}, u32[]{:S(2)}) copy-start(f32[16,24,1024]{2,1,0:T(8,128)} %param.7) | copy-start | bytes 4718596
  17.7 6.4 %collective-permute-start.3 = (f32[1,408,128]{2,1,0:T(8,128)S(1)}, f32[1,408,128]{2,1,0:T(8,128)S(1)}, u32[]{:S(2)}, u32[]{:S(2)}) collective-permute-start(f32[1,408,128]{2,1,0:T(8,128)S(1)} %get-tuple-element.9), channel_id=1, source_target_pairs={{0,16},{8,24},{16,0},{24,8},{1,17},{9,25},{17,1},{25,9},{2,18},{10... | collective-permute-start | bytes 626696 | tf_op jit(solution)/shard_map/ppermute | solution.py:45
  24.2 35.6 %copy-start.5 = (f32[2,24]{1,0:T(2,128)S(1)}, f32[2,24]{1,0:T(2,128)}, u32[]{:S(2)}) copy-start(f32[2,24]{1,0:T(2,128)} %refs_2_.3) | copy-start | bytes 580
  24.2 35.6 %copy-start.6 = (f32[2,8]{1,0:T(2,128)S(1)}, f32[2,8]{1,0:T(2,128)}, u32[]{:S(2)}) copy-start(f32[2,8]{1,0:T(2,128)} %refs_3_.3) | copy-start | bytes 196
  24.2 35.6 %copy-start.7 = (f32[24]{0:T(128)S(1)}, f32[24]{0:T(128)}, u32[]{:S(2)}) copy-start(f32[24]{0:T(128)} %refs_1_.3) | copy-start | bytes 292
  24.2 35.7 %copy-start.8 = (f32[3]{0:T(128)S(1)}, f32[3]{0:T(128)}, u32[]{:S(2)}) copy-start(f32[3]{0:T(128)} %refs_4_.1) | copy-start | bytes 40
  24.2 11.6 %collective-permute-start.4 = (f32[408,128]{1,0:T(8,128)S(1)}, f32[408,128]{1,0:T(8,128)S(1)}, u32[]{:S(2)}, u32[]{:S(2)}) collective-permute-start(f32[408,128]{1,0:T(8,128)S(1)} %shard_map.88.refs_7_.refs_1_), channel_id=1, source_target_pairs={{0,4},{1,5},{2,6},{3,7},{4,0},{5,1},{6,2},{7,3},{8,12},{9,13},{10,... | collective-permute-start | bytes 626696 | tf_op jit(solution)/shard_map/ppermute | solution.py:45
  36.4 6.5 %collective-permute-start.5 = (f32[408,128]{1,0:T(8,128)S(1)}, f32[408,128]{1,0:T(8,128)S(1)}, u32[]{:S(2)}, u32[]{:S(2)}) collective-permute-start(f32[408,128]{1,0:T(8,128)S(1)} %shard_map.90.refs_1_), channel_id=1, source_target_pairs={{0,2},{1,3},{2,0},{3,1},{4,6},{5,7},{6,4},{7,5},{8,10},{9,11},{10,... | collective-permute-start | bytes 626696 | tf_op jit(solution)/shard_map/ppermute | solution.py:45
  36.8 26.6 %collective-permute-start.7 = (f32[96,512]{1,0:T(8,128)S(1)}, f32[96,512]{1,0:T(8,128)S(1)}, u32[]{:S(2)}, u32[]{:S(2)}) collective-permute-start(f32[96,512]{1,0:T(8,128)S(1)} %bitcast.16), channel_id=1, source_target_pairs={{0,1},{1,2},{2,3},{3,4},{4,5},{5,6},{6,7},{8,9},{9,10},{10,11},{11... | collective-permute-start | bytes 589832 | tf_op jit(solution)/shard_map/ppermute | solution.py:398
  39.7 23.7 %collective-permute-start.8 = (f32[96,512]{1,0:T(8,128)S(1)}, f32[96,512]{1,0:T(8,128)S(1)}, u32[]{:S(2)}, u32[]{:S(2)}) collective-permute-start(f32[96,512]{1,0:T(8,128)S(1)} %bitcast.15), channel_id=1, source_target_pairs={{1,0},{2,1},{3,2},{4,3},{5,4},{6,5},{7,6},{9,8},{10,9},{11,10},{12... | collective-permute-start | bytes 589832 | tf_op jit(solution)/shard_map/ppermute | solution.py:398
  44.2 19.2 %collective-permute-start.6 = (f32[240,128]{1,0:T(8,128)S(1)}, f32[240,128]{1,0:T(8,128)S(1)}, u32[]{:S(2)}, u32[]{:S(2)}) collective-permute-start(f32[240,128]{1,0:T(8,128)S(1)} %shard_map.92), channel_id=1, source_target_pairs={{0,1},{1,0},{2,3},{3,2},{4,5},{5,4},{6,7},{7,6},{8,9},{9,8},{10,11... | collective-permute-start | bytes 368648 | tf_op jit(solution)/shard_map/ppermute | solution.py:45
  46.3 13.5 %collective-permute-start.1 = (f32[24,1024]{1,0:T(8,128)S(1)}, f32[24,1024]{1,0:T(8,128)S(1)}, u32[]{:S(2)}, u32[]{:S(2)}) collective-permute-start(f32[24,1024]{1,0:T(8,128)S(1)} %get-tuple-element.10), channel_id=1, source_target_pairs={{1,0},{2,1},{3,2},{4,3},{5,4},{6,5},{7,6},{9,8},{10,9},{11,10},{12... | collective-permute-start | bytes 294920 | tf_op jit(solution)/shard_map/ppermute | solution.py:398
  48.2 11.6 %collective-permute-start = (f32[24,1024]{1,0:T(8,128)S(1)}, f32[24,1024]{1,0:T(8,128)S(1)}, u32[]{:S(2)}, u32[]{:S(2)}) collective-permute-start(f32[24,1024]{1,0:T(8,128)S(1)} %get-tuple-element.11), channel_id=1, source_target_pairs={{0,1},{1,2},{2,3},{3,4},{4,5},{5,6},{6,7},{8,9},{9,10},{10,11},{11... | collective-permute-start | bytes 294920 | tf_op jit(solution)/shard_map/ppermute | solution.py:398

commit v2 on v1

v2 whole, which is shorter than its diff:
```python
import jax
import jax.numpy as jnp
from jax import lax
from jax.experimental import pallas as pl
from jax.experimental.pallas import tpu as pltpu
from jax.sharding import PartitionSpec as P

NSTEP = 4
RATIO = 4
LANES = 128
F32 = jnp.float32
VMEM = pl.BlockSpec(memory_space=pltpu.VMEM)
SMEM = pl.BlockSpec(memory_space=pltpu.SMEM)
ANY = pl.BlockSpec(memory_space=pl.ANY)


def call(kernel, outs, args, specs, scratch=(), limit=16, cost=0, out_specs=None, same=None):
    return pl.pallas_call(
        kernel,
        out_shape=list(outs),
        in_specs=list(specs),
        out_specs=[VMEM] * len(outs) if out_specs is None else out_specs,
        scratch_shapes=list(scratch),
        input_output_aliases=same or {},
        compiler_params=pltpu.CompilerParams(vmem_limit_bytes=limit << 20),
        cost_estimate=pl.CostEstimate(flops=0, bytes_accessed=cost, transcendentals=0),
    )(*args)


def shape(*dims, dtype=F32):
    return jax.ShapeDtypeStruct(dims, dtype)


def lane_ids():
    return lax.broadcasted_iota(jnp.int32, (8, LANES), 1)


def sublane_ids():
    return lax.broadcasted_iota(jnp.int32, (8, LANES), 0)


def one_if(condition):
    return jnp.where(condition, 1.0, 0.0).astype(F32)


def aligned(start, step):
    return pl.multiple_of(start, step)


def edge_rows(deep, chan, nest, parent, near, far, sems):
    odd = lax.rem(lax.axis_index("tile"), 2)
    cols = nest.shape[1]
    copies = []
    for k, (dest, last) in enumerate(((near, 1 - odd), (far, odd))):
        size = deep * chan
        at = aligned(last * (nest.shape[0] - size), 8)
        copies.append((nest.at[pl.ds(at, size), :], dest.at[pl.ds(0, size), :]))
        at = aligned(last * (parent.shape[0] - chan), 8)
        for part in range(parent.shape[1] // cols):
            source = parent.at[pl.ds(at, chan), pl.ds(part * cols, cols)]
            copies.append((source, dest.at[pl.ds(size + part * chan, chan), :]))
    made = [pltpu.make_async_copy(a, b, sems.at[i]) for i, (a, b) in enumerate(copies)]
    for copy in made:
        copy.start()
    for copy in made:
        copy.wait()


def extract(rows, chan, box, parent, keep, send, anchor):
    cols = parent.shape[1]
    blocks = cols // LANES
    groups = chan // 8
    sec = lax.axis_index("sec")
    half = lax.rem(sec, 2)
    lane = lane_ids()
    anchor[...] = jnp.full((8, LANES), box[sec, 0], jnp.int32)

    def at(row, g):
        return pl.ds(aligned(row * chan + 8 * g, 8), 8)

    lane_row = lax.div(lane, 2)
    together = 4

    def outer(step, packed):
        packed = list(packed)
        for k in range(together):
            row = step * together + k
            for g in range(groups):
                ends = jnp.where(
                    lane < LANES // 2,
                    parent[at(row, g), pl.ds(0, LANES)],
                    parent[at(row, g), pl.ds(cols - LANES, LANES)],
                )
                ends = pltpu.roll(ends, 2 * rows + 2 * row + 1, axis=1)
                packed[g] = jnp.where(lane_row == rows + row, ends, packed[g])
        return tuple(packed)

    zeros = (jnp.zeros((8, LANES), F32),) * groups
    halo = lax.fori_loop(0, rows // together, outer, zeros)

    for which, dest in ((1 - half, send), (half, keep)):

        @pl.loop(0, dest.shape[0])
        def _(i):
            nest = 2 * i + which
            offset = box[nest, 1] - sec * cols
            shift = lax.bitwise_and(offset, LANES - 1)
            back = lax.bitwise_and(LANES - shift, LANES - 1)

            def place(k):
                start = aligned(jnp.clip(k, 0, blocks - 1) * LANES, LANES)
                return pl.ds(start, LANES), one_if((k >= 0) & (k < blocks))

            first = lax.shift_right_arithmetic(offset, 7)
            at_a, on_a = place(first)
            at_b, on_b = place(first + 1)
            at_c, on_c = place(lax.shift_right_arithmetic(offset - 1, 7))
            before = lax.bitwise_and(lane - shift, LANES - 1) >= LANES // 2
            sent = jnp.where(lax.rem(lane, 2) == 0, one_if(nest == sec + 1), one_if(nest == sec - 1))

            def inner(step, packed):
                packed = list(packed)
                shifted = []
                for k in range(together):
                    row = step * together + k
                    turn = lax.bitwise_and(back + 2 * row + 1, LANES - 1)
                    for g in range(groups):
                        a = parent[at(row, g), at_a] * on_a
                        b = parent[at(row, g), at_b] * on_b
                        c = parent[at(row, g), at_c] * on_c
                        main = pltpu.roll(jnp.where(lane < shift, b, a), back, axis=1)
                        shifted.append((at(row, g), main))
                        side = pltpu.roll(jnp.where(before, c, b), turn, axis=1)
                        packed[g] = jnp.where(lane_row == row, side, packed[g])
                for where, main in shifted:
                    dest[i, where, :] = main
                return tuple(packed)

            packed = lax.fori_loop(0, rows // together, inner, tuple(h * sent for h in halo))
            for g in range(groups):
                dest[i, pl.ds(rows * chan + 8 * g, 8), :] = packed[g]


def combine(bit, own, got, keep, send):
    mine = lax.rem(lax.axis_index("sec") // bit, 2)
    for i in range(keep.shape[0]):
        send[i] = own[2 * i + 1 - mine] + got[2 * i + 1 - mine]
        keep[i] = own[2 * i + mine] + got[2 * i + mine]


def split(rows, chan, own, got, mine, to_sec, to_tile, to_both):
    sec = lax.div(lax.axis_index("sec"), lax.axis_size("sec") // 2)
    part = lax.rem(lax.div(lax.axis_index("tile"), 2), 2)
    size = rows // 2 * chan
    for dest, nest, half in (
        (to_sec, 1 - sec, part),
        (to_both, 1 - sec, 1 - part),
        (to_tile, sec, 1 - part),
        (mine, sec, part),
    ):
        at = pl.ds(aligned(half * size, 8), size)
        dest[pl.ds(0, size), :] = own[nest, at, :] + got[nest, at, :]
        at = pl.ds(rows * chan, chan)
        dest[pl.ds(size, chan), :] = own[nest, at, :] + got[nest, at, :]


def gathered(mine, from_sec, from_tile, from_both, out):
    out[0] = mine[...] + from_sec[...]
    out[1] = from_tile[...] + from_both[...]


def held_block(anchor, tile, rows, own_rows, group):
    first = lax.div(tile, group) * group
    low = jnp.maximum(anchor + (own_rows * first - 2), 0)
    base = lax.shift_right_arithmetic(low, rows.bit_length() - 1)
    return base + lax.bitwise_and(tile - base, group - 1)


def held(anchor, tile, rows, own_rows, group, tiles):
    if group == tiles:
        return jnp.full((8, LANES), tile, jnp.int32)
    return held_block(anchor, tile, rows, own_rows, group)


def choose(rows, own_rows, group, tiles, anchor, own, got, out):
    start = anchor[...]
    for k in range(2):
        tile = lax.bitwise_xor(lax.axis_index("tile"), 2 * k)
        keep = held(start, tile, rows, own_rows, 2 * group, tiles) == held_block(
            start, tile, rows, own_rows, group
        )
        for r in range(0, out.shape[1], 8):
            at = pl.ds(r, 8)
            out[k, at, :] = jnp.where(keep, own[k, at, :], got[k, at, :])


def wanted(anchor, row, tile, group, own_rows):
    first = lax.div(tile, group) * group
    low = anchor + (own_rows * first - 2)
    return (row >= low) & (row <= low + own_rows * group + 4)


def slot_rows(rows, own_rows, tiles, anchor):
    tile = lax.axis_index("tile")
    return [
        rows * held(anchor, lax.bitwise_xor(tile, 2 * k), rows, own_rows, 8, tiles) for k in range(2)
    ]


def select(rows, chan, own_rows, tiles, anchor, both, mine, sent):
    start = anchor[...]
    tile = lax.axis_index("tile")
    part = lax.rem(lax.div(tile, 2), 2)
    size = rows // 2 * chan
    base = slot_rows(rows, own_rows, tiles, start)
    lane_row = lax.div(lane_ids(), 2)
    for dest, owner in ((sent, lax.bitwise_xor(tile, 4)), (mine, tile)):
        for j in range(rows // 2 + 1):
            row = lane_row if j == rows // 2 else part * (rows // 2) + j
            second = wanted(start, base[1] + row, owner, 4, own_rows)
            for g in range(chan // 8):
                at = pl.ds(j * chan + 8 * g, 8)
                dest[at, :] = jnp.where(second, both[1, at, :], both[0, at, :])


def settle(rows, chan, own_rows, tiles, anchor, mine, got, near, nest, parent, out):
    start = anchor[...]
    tile = lax.axis_index("tile")
    part = lax.rem(lax.div(tile, 2), 2)
    base = slot_rows(rows, own_rows, tiles, start)
    lane_row = lax.div(lane_ids(), 2)
    for j in range(rows // 2 + 1):
        row = lane_row if j == rows // 2 else part * (rows // 2) + j
        keep = wanted(start, base[0] + row, tile, 4, own_rows)
        keep = keep | wanted(start, base[1] + row, tile, 4, own_rows)
        for g in range(chan // 8):
            at = pl.ds(j * chan + 8 * g, 8)
            out[at, :] = jnp.where(keep, mine[at, :], got[at, :])


def table_rows(chan, levels):
    return 4 * chan + 2 * levels + 6 * levels + 3


def make_table(diff, wind, conv, mix, table):
    chan, levels = diff.shape[0], conv.shape[1]

    def put(i, value):
        table[pl.ds(i, 1), :] = jnp.full((1, LANES), value, F32)

    for c in range(chan):
        d, wx, wy = diff[c], wind[0, c], wind[1, c]
        for k, value in enumerate((1.0 - 4.0 * d - wx - wy, d + wx, d + wy, d)):
            put(4 * c + k, value)
    base = 4 * chan
    for f in range(2):
        for l in range(levels):
            put(base + f * levels + l, conv[f, l])
    base += 2 * levels
    for f in range(3):
        m = jnp.full((1, LANES), mix[f], F32)
        ratio = None
        for l in range(levels):
            pivot = 1.0 + (1.0 if l in (0, levels - 1) else 2.0) * m
            if l:
                pivot = pivot - m * ratio
            inverse = 1.0 / pivot
            ratio = m * inverse
            table[pl.ds(base + 2 * (f * levels + l), 1), :] = inverse
            table[pl.ds(base + 2 * (f * levels + l) + 1, 1), :] = ratio
        put(base + 6 * levels + f, mix[f])


def rows_of(table):
    def coef(i):
        return jnp.broadcast_to(table[pl.ds(i, 1), :], (8, LANES))

    return coef


def step_blocks(chan, table, loads, stores):
    coef = rows_of(table)

    def horizontal(c):
        center, above, left, spread = (coef(4 * c + k) for k in range(4))
        out = []
        for load in loads:
            v, n, s, w, e = load(c)
            out.append(center * v + above * n + left * w + spread * (s + e))
        return out

    mix_blocks(chan, table, horizontal, stores)


def mix_blocks(chan, table, fields, stores):
    levels = chan // 3
    count = len(stores)
    coef = rows_of(table)
    conv = 4 * chan
    solve = conv + 2 * levels
    passed = None
    for f in range(3):
        ys, carry = [], []
        for l in range(levels):
            c = f * levels + l
            given = fields(c)
            rate = coef(conv + f * levels + l) if f < 2 else None
            ratio = coef(solve + 2 * (c - 1) + 1) if l else None
            row, moved = [], []
            for b in range(count):
                h = given[b]
                if passed is not None:
                    h = h + passed[l][b]
                if f < 2:
                    moved.append(rate * h)
                    h = h - moved[b]
                if l:
                    h = h + ratio * ys[-1][b]
                row.append(h)
            ys.append(row)
            carry.append(moved)
        passed = carry
        m = coef(solve + 6 * levels + f)
        x = [None] * count
        for l in range(levels - 1, -1, -1):
            c = f * levels + l
            inverse = coef(solve + 2 * c)
            for b in range(count):
                x[b] = inverse * (ys[l][b] if x[b] is None else ys[l][b] + m * x[b])
                stores[b](c, x[b])


def sides(lane, west, v, east):
    w = pltpu.roll(jnp.where(lane == LANES - 1, west, v), 1, axis=1)
    e = pltpu.roll(jnp.where(lane == 0, east, v), LANES - 1, axis=1)
    return w, e


def parent_step(rows, chan, table, parent, strip, out, edges, ext, done, sems):
    blocks = parent.shape[1] // LANES
    groups = chan // 8
    lane = lane_ids()
    packed_at = strip.shape[1] - chan

    def columns(j):
        return pl.ds(aligned(j * LANES, LANES), LANES)

    packed = [strip[0, pl.ds(packed_at + 8 * g, 8), :] for g in range(groups)]

    @pl.loop(0, rows)
    def _(row):
        for g in range(groups):
            at = pl.ds(aligned((row + 1) * chan + 8 * g, 8), 8)
            turn = LANES - 1 - 2 * rows - 2 * row
            turned = pltpu.roll(packed[g], turn, axis=1)
            ext[0, at, :] = turned
            ext[blocks + 1, at, :] = turned

    @pl.loop(0, blocks)
    def _(j):
        ext[j + 1, pl.ds(chan, rows * chan), :] = parent[:, columns(j)]
        ext[j + 1, pl.ds(0, chan), :] = jnp.zeros((chan, LANES), F32)
        ext[j + 1, pl.ds((rows + 1) * chan, chan), :] = jnp.zeros((chan, LANES), F32)

    @pl.loop(0, blocks)
    def _(j):
        def block(first):
            def loads(c):
                def at(r):
                    return pl.ds((first + r) * chan + c, 8, stride=chan)

                v = ext[j + 1, at(1), :]
                w, e = sides(lane, ext[j, at(1), :], v, ext[j + 2, at(1), :])
                return v, ext[j + 1, at(0), :], ext[j + 1, at(2), :], w, e

            def store(c, x):
                done[j, pl.ds(first * chan + c, 8, stride=chan), :] = x

            return loads, store

        loads, stores = zip(*(block(first) for first in range(0, rows, 8)))
        step_blocks(chan, table, loads, stores)
        at = pl.ds(aligned(j * chan, 8), chan)
        edges[0, at, :] = done[j, pl.ds(0, chan), :]
        edges[1, at, :] = done[j, pl.ds((rows - 1) * chan, chan), :]
        pltpu.make_async_copy(done.at[j], out.at[:, columns(j)], sems.at[j]).start()

    @pl.loop(0, blocks)
    def _(j):
        pltpu.make_async_copy(done.at[j], out.at[:, columns(j)], sems.at[j]).wait()


def parent_edges(rows, chan, deep, table, near, far, edges, given, out, beside, done, sems):
    blocks = edges.shape[1] // chan
    per = near.shape[1] // LANES
    odd = lax.rem(lax.axis_index("tile"), 2) == 1
    for j in range(blocks):
        for g in range(chan // 8):
            at = pl.ds((deep + j // per) * chan + 8 * g, 8)
            a, b = (ref[at, pl.ds(j % per * LANES, LANES)] for ref in (near, far))
            at = pl.ds(j * chan + 8 * g, 8)
            beside[0, at, :] = jnp.where(odd, a, b)
            beside[1, at, :] = jnp.where(odd, b, a)
    coef = rows_of(table)
    pieces = [(k, b) for k in range(2) for b in range(0, blocks, 8)]

    def at(b, c):
        return pl.ds(b * chan + c, 8, stride=chan)

    def fields(c):
        return [coef(4 * c + (1, 3)[k]) * beside[k, at(b, c), :] for k, b in pieces]

    def storing(k, b):
        def store(c, x):
            done[k, at(b, c), :] = edges[k, at(b, c), :] + x

        return store

    mix_blocks(chan, table, fields, [storing(k, b) for k, b in pieces])
    copies = []
    for k, row in enumerate((0, rows - 1)):
        for j in range(blocks):
            copies.append(
                pltpu.make_async_copy(
                    done.at[k, pl.ds(j * chan, chan), :],
                    out.at[pl.ds(row * chan, chan), pl.ds(j * LANES, LANES)],
                    sems.at[k * blocks + j],
                )
            )
    for copy in copies:
        copy.start()
    for copy in copies:
        copy.wait()


def dealing(cols, back):
    first = lax.broadcasted_iota(jnp.int32, (cols, cols), 0)
    second = lax.broadcasted_iota(jnp.int32, (cols, cols), 1)
    planes = cols // LANES
    natural, dealt = (second, first) if back else (first, second)
    hit = natural == planes * lax.bitwise_and(dealt, LANES - 1) + lax.shift_right_arithmetic(dealt, 7)
    return jnp.where(hit, 1.0, 0.0).astype(jnp.bfloat16)


def dealt(x, matrix):
    out = None
    for _ in range(3):
        part = x.astype(jnp.bfloat16)
        x = x - part.astype(F32)
        term = jnp.dot(part, matrix, preferred_element_type=F32)
        out = term if out is None else out + term
    return out


def plane_blocks(chan, table, planes, lane, load, store):
    cache = {}

    def center(k, c):
        if (k, c) not in cache:
            cache[k, c] = load(0, k, c)
        return cache[k, c]

    def block(k):
        def loads(c):
            if k == 0:
                w = jnp.where(lane == 0, 0.0, pltpu.roll(center(planes - 1, c), 1, axis=1))
            else:
                w = center(k - 1, c)
            if k == planes - 1:
                e = jnp.where(lane == LANES - 1, 0.0, pltpu.roll(center(0, c), LANES - 1, axis=1))
            else:
                e = center(k + 1, c)
            return center(k, c), load(-1, k, c), load(1, k, c), w, e

        def put(c, x):
            store(k, c, x)

        return loads, put

    loads, stores = zip(*(block(k) for k in range(planes)))
    step_blocks(chan, table, loads, stores)


def nest_first(chan, deep, box, table, nest, moved, nudge, back, matrix, ext):
    nest_rows = nest.shape[0] // chan
    planes = nest.shape[1] // LANES
    ext_rows = nest_rows + 2 * deep
    groups = chan // 8
    sec, tile = lax.axis_index("sec"), lax.axis_index("tile")
    extent_x, extent_y = box[sec, 2], box[sec, 3]
    lane, sub = lane_ids(), sublane_ids()
    first_row = nest_rows * tile - deep
    matrix[...] = dealing(nest.shape[1], False)
    back[...] = dealing(nest.shape[1], True)
    for k in range(planes):
        col = planes * lane + k
        for rb in range(0, ext_rows, 8):
            i = first_row + rb + sub
            live = one_if((i >= 0) & (i < extent_x) & (col < extent_y))
            dist = jnp.minimum(jnp.minimum(i, col), jnp.minimum(extent_x - 1 - i, extent_y - 1 - col))
            dist = jnp.maximum(dist, 0).astype(F32)
            rate = 0.1 + 0.4 * jnp.exp(-dist / 3.0)
            nudge[0, k, pl.ds(rb, 8), :] = live * (1.0 - rate)
            nudge[1, k, pl.ds(rb, 8), :] = live * rate
            nudge[2, k, pl.ds(rb, 8), :] = live

    together = 4

    @pl.loop(0, nest_rows // together)
    def _(step):
        size = together * chan
        x = dealt(nest[pl.ds(aligned(step * size, 8), size), :], matrix[...])
        for r in range(together):
            row = step * together + r
            for k in range(planes):
                live = jnp.broadcast_to(nudge[2, k, pl.ds(deep + row, 1), :], (8, LANES))
                for g in range(groups):
                    piece = x[r * chan + 8 * g : r * chan + 8 * g + 8, k * LANES : (k + 1) * LANES]
                    ext[k, pl.ds(aligned((row + 1) * chan + 8 * g, 8), 8), :] = piece * live

    for row in (0, nest_rows + 1):
        ext[:, pl.ds(row * chan, chan), :] = jnp.zeros((planes, chan, LANES), F32)
    for rb in range(0, nest_rows, 8):

        def load(shift, k, c):
            return ext[k, pl.ds((rb + 1 + shift) * chan + c, 8, stride=chan), :]

        def store(k, c, x):
            at = pl.ds(deep + rb, 8)
            moved[k, c, at, :] = x * nudge[0, k, at, :]

        plane_blocks(chan, table, planes, lane, load, store)


def nest_edges(chan, deep, table, nest, near, far, nudge, given, moved, matrix, natural, ext):
    nest_rows = nest.shape[0] // chan
    planes = nest.shape[1] // LANES
    ext_rows = nest_rows + 2 * deep
    size = deep * chan
    lane, sub = lane_ids(), sublane_ids()
    odd = lax.rem(lax.axis_index("tile"), 2) == 1
    matrix[...] = dealing(nest.shape[1], False)
    edge = (deep + 2) * chan
    a, b = near[pl.ds(0, size), :], far[pl.ds(0, size), :]
    natural[pl.ds(0, size), :] = jnp.where(odd, a, b)
    natural[pl.ds(size, 2 * chan), :] = nest[pl.ds(0, 2 * chan), :]
    natural[pl.ds(edge, 2 * chan), :] = nest[pl.ds((nest_rows - 2) * chan, 2 * chan), :]
    natural[pl.ds(edge + 2 * chan, size), :] = jnp.where(odd, b, a)
    for half in range(2):

        def rows_at(r):
            return r if half == 0 else ext_rows - deep - 2 + r

        x = dealt(natural[pl.ds(half * edge, edge), :], matrix[...])
        for r in range(deep + 2):
            for k in range(planes):
                live = jnp.broadcast_to(nudge[2, k, pl.ds(rows_at(r), 1), :], (8, LANES))
                for g in range(chan // 8):
                    piece = x[r * chan + 8 * g : r * chan + 8 * g + 8, k * LANES : (k + 1) * LANES]
                    ext[k, pl.ds(half * edge + r * chan + 8 * g, 8), :] = piece * live

    def load(shift, k, c):
        upper = ext[k, pl.ds((1 + shift) * chan + c, 8, stride=chan), :]
        lower = ext[k, pl.ds((3 + shift) * chan + c, 8, stride=chan), :]
        return jnp.where(sub < deep, upper, lower)

    def store(k, c, x):
        low, high = pl.ds(1, deep), pl.ds(ext_rows - 1 - deep, deep)
        moved[k, c, low, :] = x[:deep] * nudge[0, k, low, :]
        moved[k, c, high, :] = x[deep:] * nudge[0, k, high, :]

    plane_blocks(chan, table, planes, lane, load, store)


def nest_rest(
    rows, chan, deep, own_rows, tiles,
    anchor, table, own, got_a, got_b, got_c, moved, nudge, back, out,
    slots, foot, coarse, state, force, done, final, sems,
):
    planes, _, ext_rows, _ = moved.shape
    nest_rows = ext_rows - 2 * deep
    groups = chan // 8
    tile = lax.axis_index("tile")
    lane, sub = lane_ids(), sublane_ids()
    first_row = nest_rows * tile - deep
    start = jnp.max(anchor[...]) + own_rows * tile - 2
    span = foot.shape[1] // chan - 1
    size = rows // 2 * chan
    part = lax.rem(lax.div(tile, 2), 2)
    side = lax.rem(tile, 2)

    for k, ref in enumerate((own, got_a, got_b, got_c)):
        slots[k] = ref[...]

    for m in range(span):
        row = start + m
        local = lax.bitwise_and(row, rows - 1)
        upper = lax.div(local, rows // 2)
        other = lax.bitwise_and(lax.shift_right_arithmetic(row, rows.bit_length() - 1), 1)
        k = 2 * lax.bitwise_xor(upper, part) + lax.bitwise_xor(other, side)
        inside = one_if((row >= 0) & (row < rows * tiles))
        slot = (local - upper * (rows // 2)) * chan
        turn = LANES - 1 - 2 * local
        for g in range(groups):
            at = pl.ds(m * chan + 8 * g, 8)
            foot[0, at, :] = pltpu.roll(slots[k, pl.ds(size + 8 * g, 8), :] * inside, turn, axis=1)
            foot[1, at, :] = slots[k, pl.ds(aligned(slot + 8 * g, 8), 8), :] * inside

    for k in range(2):
        foot[k, pl.ds(span * chan, chan), :] = jnp.zeros((chan, LANES), F32)

    def foot_loads(c):
        def at(r):
            return pl.ds(r * chan + c, 8, stride=chan)

        v = foot[1, at(1), :]
        edge = foot[0, at(1), :]
        w, e = sides(lane, edge, v, edge)
        return v, foot[1, at(0), :], foot[1, at(2), :], w, e

    def foot_store(c, x):
        old = foot[1, pl.ds(chan + c, 8, stride=chan), :]
        coarse[0, c] = old
        coarse[1, c] = x - old

    step_blocks(chan, table, [foot_loads], [foot_store])

    share = []
    for rb in range(0, ext_rows, 8):
        p = lax.rem(sub, RATIO).astype(F32) / RATIO
        share.append(jnp.where(first_row + rb + sub >= RATIO * (own_rows * tiles - 1), 0.0, p))

    @pl.loop(0, chan)
    def _(c):
        for rb in range(0, ext_rows, 8):
            u = rb // RATIO
            at = pl.ds(rb, 8)
            lines = []
            for t in range(2):
                r0, r1, r2 = (
                    jnp.broadcast_to(coarse[t, c, pl.ds(u + i, 1), :], (8, LANES)) for i in range(3)
                )
                a0 = jnp.where(sub < RATIO, r0, r1)
                a1 = jnp.where(sub < RATIO, r1, r2)
                line = a0 + share[rb // 8] * (a1 - a0)
                beside = jnp.where(lane == LANES - 1, line, pltpu.roll(line, LANES - 1, axis=1))
                lines.append((line, (beside - line) * (1.0 / RATIO)))
            for k in range(planes):
                b = nudge[1, k, at, :]
                old, new = (b * (line + float(k) * slope if k else line) for line, slope in lines)
                force[0, k, c, at, :] = old
                force[1, k, c, at, :] = new
                state[0, k, c, pl.ds(8 + rb, 8), :] = moved[k, c, at, :] + (old + new * (1.0 / NSTEP))

    def advance(step, src, rb, put):
        weight = jnp.float32(step + 1) / NSTEP

        def load(shift, k, c):
            return state[src, k, c, pl.ds(8 + rb + shift, 8), :]

        def store(k, c, x):
            at = pl.ds(rb, 8)
            g = force[0, k, c, at, :] + weight * force[1, k, c, at, :]
            put(k, c, nudge[0, k, at, :] * x + g)

        plane_blocks(chan, table, planes, lane, load, store)

    @pl.loop(1, NSTEP - 1)
    def _(step):
        src = lax.rem(step + 1, 2)

        @pl.loop(0, ext_rows // 8)
        def _(block):
            rb = aligned(block * 8, 8)

            def put(k, c, x):
                state[1 - src, k, c, pl.ds(8 + rb, 8), :] = x

            advance(step, src, rb, put)

    copies = []
    for n, rb in enumerate(range(0, nest_rows, 8)):

        def put(k, c, x):
            done[n, k, pl.ds(c, 8, stride=chan), :] = x

        advance(NSTEP - 1, NSTEP % 2, deep + rb, put)
        whole = jnp.concatenate([done[n, k] for k in range(planes)], axis=1)
        final[n] = dealt(whole, back[...])
        copies.append(
            pltpu.make_async_copy(final.at[n], out.at[pl.ds(rb * chan, 8 * chan), :], sems.at[n])
        )
        copies[n].start()
    for copy in copies:
        copy.wait()


def bound(kernel, *static):
    def run(*refs):
        return kernel(*static, *refs)

    return run


def exchange(block, axis, bit):
    return lax.ppermute(block, axis, [(i, i ^ bit) for i in range(lax.axis_size(axis))])


def exchange_both(block, sec_bit, tile_bit):
    secs, tiles = lax.axis_size("sec"), lax.axis_size("tile")
    route = [
        (s * tiles + t, (s ^ sec_bit) * tiles + (t ^ tile_bit)) for s in range(secs) for t in range(tiles)
    ]
    return lax.ppermute(block, ("sec", "tile"), route)


def body(parent_old, nest_state, diffusion, wind_speed, conversion, vert_mix, nest_box):
    rows, chan, cols = parent_old.shape
    nest_rows, nest_cols = nest_state.shape[1], nest_state.shape[3]
    secs, tiles = lax.axis_size("sec"), lax.axis_size("tile")
    own_rows = nest_rows // RATIO
    levels = conversion.shape[1]
    deep = NSTEP
    ext_rows = nest_rows + 2 * deep
    col_blocks = nest_cols // LANES
    blocks = cols // LANES
    span = (ext_rows // RATIO + 1) + 2
    strip_rows = (rows + 1) * chan
    half_rows = (rows // 2 + 1) * chan
    parent = parent_old.reshape(rows * chan, cols)
    nest = nest_state.reshape(nest_rows * chan, nest_cols)
    half = shape(half_rows, LANES)

    halo = shape((deep + cols // nest_cols) * chan, nest_cols)
    near, far = call(
        bound(edge_rows, deep, chan), [halo] * 2, (nest, parent), (ANY, ANY),
        scratch=[pltpu.SemaphoreType.DMA((2 * (1 + cols // nest_cols),))], limit=4, cost=1 << 20,
    )
    near = exchange(near, "tile", 1)
    beside = [(i, i + 1) for i in range(1, tiles - 1, 2)]
    far = lax.ppermute(far, "tile", beside + [(j, i) for i, j in beside])

    (table,) = call(
        make_table, [shape(table_rows(chan, levels), LANES)],
        (diffusion, wind_speed, conversion, vert_mix), (SMEM,) * 4, limit=2, cost=1 << 20,
    )

    some = shape(secs // 2, strip_rows, LANES)
    keep, send, anchor = call(
        bound(extract, rows, chan), [some, some, shape(8, LANES, dtype=jnp.int32)],
        (nest_box, parent), (SMEM, VMEM), cost=4 << 20,
    )
    got = exchange(send, "sec", 1)
    bit = 2
    while bit < secs // 2:
        some = shape(secs // (2 * bit), strip_rows, LANES)
        keep, send = call(bound(combine, bit), [some, some], (keep, got), (VMEM, VMEM), cost=1 << 20)
        got = exchange(send, "sec", bit)
        bit *= 2
    mine, to_sec, to_tile, to_both = call(
        bound(split, rows, chan), [half] * 4, (keep, got), (VMEM, VMEM), cost=1 << 18,
    )
    from_sec = exchange_both(to_sec, secs // 2, 0)
    from_tile = exchange_both(to_tile, 0, 2)
    from_both = exchange_both(to_both, secs // 2, 2)
    two = shape(2, half_rows, LANES)
    (strip,) = call(
        gathered, [two], (mine, from_sec, from_tile, from_both), (VMEM,) * 4, cost=1 << 18,
    )
    pair = strip
    group = tiles // 2
    while group > 4:
        got = exchange(pair, "tile", group)
        (pair,) = call(
            bound(choose, rows, own_rows, group, tiles), [two], (anchor, pair, got), (VMEM,) * 3, cost=1 << 18,
        )
        group //= 2
    mine, sent = call(
        bound(select, rows, chan, own_rows, tiles), [half] * 2, (anchor, pair), (VMEM,) * 2, cost=1 << 18,
    )
    got = exchange(sent, "tile", 4)
    edge = shape(2, blocks * chan, LANES)
    parent_new, edges = call(
        bound(parent_step, rows, chan), [shape(rows * chan, cols), edge],
        (table, parent, strip), (VMEM,) * 3, cost=8 << 20, out_specs=[ANY, VMEM],
        scratch=[
            pltpu.VMEM((blocks + 2, (rows + 2) * chan, LANES), F32),
            pltpu.VMEM((blocks, rows * chan, LANES), F32),
            pltpu.SemaphoreType.DMA((blocks,)),
        ],
    )

    moved_shape = shape(col_blocks, chan, ext_rows, LANES)
    square = (nest_cols, nest_cols)
    moved, nudge, back = call(
        bound(nest_first, chan, deep),
        [moved_shape, shape(3, col_blocks, ext_rows, LANES), shape(*square, dtype=jnp.bfloat16)],
        (nest_box, table, nest), (SMEM, VMEM, VMEM), cost=6 << 20,
        scratch=[
            pltpu.VMEM(square, jnp.bfloat16),
            pltpu.VMEM((col_blocks, (nest_rows + 2) * chan, LANES), F32),
        ],
    )

    (own,) = call(
        bound(settle, rows, chan, own_rows, tiles), [half], (anchor, mine, got, near, moved, edges), (VMEM,) * 6, cost=1 << 18,
    )
    got_a, got_b, got_c = (exchange(own, "tile", k) for k in (1, 2, 3))

    (parent_new,) = call(
        bound(parent_edges, rows, chan, deep), [shape(rows * chan, cols)],
        (table, near, far, edges, parent_new), (VMEM,) * 4 + (ANY,), cost=1 << 20, out_specs=[ANY], same={4: 0},
        scratch=[
            pltpu.VMEM((2, blocks * chan, LANES), F32),
            pltpu.VMEM((2, blocks * chan, LANES), F32),
            pltpu.SemaphoreType.DMA((2 * blocks,)),
        ],
    )
    (moved,) = call(
        bound(nest_edges, chan, deep), [moved_shape],
        (table, nest, near, far, nudge, moved), (VMEM,) * 6, cost=3 << 20, same={5: 0},
        scratch=[
            pltpu.VMEM(square, jnp.bfloat16),
            pltpu.VMEM((2 * (deep + 2) * chan, nest_cols), F32),
            pltpu.VMEM((col_blocks, 2 * (deep + 2) * chan, LANES), F32),
        ],
    )

    (nest_new,) = call(
        bound(nest_rest, rows, chan, deep, own_rows, tiles), [shape(nest_rows * chan, nest_cols)],
        (anchor, table, own, got_a, got_b, got_c, moved, nudge, back), (VMEM,) * 9, cost=16 << 20, out_specs=[ANY],
        limit=32,
        scratch=[
            pltpu.VMEM((4, half_rows, LANES), F32),
            pltpu.VMEM((2, (span + 1) * chan, LANES), F32),
            pltpu.VMEM((2, chan, 8, LANES), F32),
            pltpu.VMEM((2, col_blocks, chan, ext_rows + 16, LANES), F32),
            pltpu.VMEM((2, col_blocks, chan, ext_rows, LANES), F32),
            pltpu.VMEM((nest_rows // 8, col_blocks, 8 * chan, LANES), F32),
            pltpu.VMEM((nest_rows // 8, 8 * chan, nest_cols), F32),
            pltpu.SemaphoreType.DMA((nest_rows // 8,)),
        ],
    )

    return parent_new.reshape(parent_old.shape), nest_new.reshape(nest_state.shape)


def solution(mesh):
    placed = (P("tile", None, "sec"), P("sec", "tile", None, None), P(), P(), P(), P(), P())
    return jax.shard_map(
        body,
        mesh=mesh,
        in_specs=placed,
        out_specs=(P("tile", None, "sec"), P("sec", "tile", None, None)),
        check_vma=False,
    )
```

time: 73.1 us -> 43.5 us (0.60)
  the two profiles are of different devices: /device:TPU:9 before, /device:TPU:0 now
where the time goes in v2:
time: 43.5 us; the launch traced here: 43.3 us
  Pallas kernels  20.7 us (48%)
  starting transfers between devices  13.5 us (31%)
  waiting for transfers between devices  6.19 us (14%)
  local copies, waits for them, and re-layouts  2.12 us (5%)
  between operations  0.78 us (2%)
    pallas_call x12, Pallas kernels, call(): pl.pallas_call(kernel, out_shape=list(outs), in_specs=list(specs), out_sp...  20.7 us
    ppermute x6, starting transfers between devices, exchange(): lax.ppermute(block, axis, [(i, i ^ bit) for i in range(lax.axis_size(axis...  9.32 us
    ppermute x3, waiting for transfers between devices, exchange_both(): return lax.ppermute(block, ('sec', 'tile'), route)  4.75 us
    ppermute x3, starting transfers between devices, exchange_both(): return lax.ppermute(block, ('sec', 'tile'), route)  3.55 us
    unnamed x18, local copies, waits for them, and re-layouts  2.12 us
    ppermute x6, waiting for transfers between devices, exchange(): lax.ppermute(block, axis, [(i, i ^ bit) for i in range(lax.axis_size(axis...  1.44 us
  transfers between devices with their start and end apart: 10, of which 6 were waited for; matrix products, arithmetic and copies ran while one was open for 0% of the time, Pallas kernels for 25%

profile of v2, /device:TPU:0, one launch (start us, length us, event | category | flops | bytes accessed | tf_op | source)
XLA Modules:
  0.0 43.3 jit_solution(16562781134089294665)
XLA Ops:
  0.6 1.4 %copy-done = f32[16,24,1024]{2,1,0:T(8,128)S(1)} copy-done((f32[16,24,1024]{2,1,0:T(8,128)S(1)}, f32[16,24,1024]{2,1,0:T(8,128)}, u32[]{:S(2)}) %copy-start) | copy-done | bytes 1572888
  2.0 0.7 %copy-done.3 = s32[4,4]{1,0:T(4,128)S(1)} copy-done((s32[4,4]{1,0:T(4,128)S(1)}, s32[4,4]{1,0:T(4,128)}, u32[]{:S(2)}) %copy-start.3) | copy-done | bytes 88
  2.7 2.8 %shard_map.88 = (f32[2,408,128]{2,1,0:T(8,128)S(1)}, f32[2,408,128]{2,1,0:T(8,128)S(1)}, s32[8,128]{1,0:T(8,128)S(1)}) custom-call(s32[4,4]{1,0:T(4,128)S(1)} %copy-done.3, f32[384,1024]{1,0:T(8,128)S(1)} %bitcast.4), custom_call_target="tpu_custom_call" | custom-call | bytes 4194304 | tf_op jit(solution)/shard_map/pallas_call | solution.py:18
  5.5 0.5 %collective-permute-start.2 = (f32[2,408,128]{2,1,0:T(8,128)S(1)}, f32[2,408,128]{2,1,0:T(8,128)S(1)}, u32[]{:S(2)}, u32[]{:S(2)}) collective-permute-start(f32[2,408,128]{2,1,0:T(8,128)S(1)} %get-tuple-element.21), channel_id=1, source_target_pairs={{0,8},{8,0},{16,24},{24,16},{1,9},{9,1},{17,25},{25,17},{2,10},{10... | collective-permute-start | bytes 1253384 | tf_op jit(solution)/shard_map/ppermute | solution.py:706
  6.1 0.7 %shard_map.87 = (f32[144,512]{1,0:T(8,128)S(1)}, f32[144,512]{1,0:T(8,128)S(1)}) custom-call(f32[384,512]{1,0:T(8,128)S(1)} %bitcast.7, f32[384,1024]{1,0:T(8,128)S(1)} %bitcast.5), custom_call_target="tpu_custom_call" | custom-call | bytes 1048576 | tf_op jit(solution)/shard_map/pallas_call | solution.py:18
  6.8 2.6 %collective-permute-start = (f32[144,512]{1,0:T(8,128)S(1)}, f32[144,512]{1,0:T(8,128)S(1)}, u32[]{:S(2)}, u32[]{:S(2)}) collective-permute-start(f32[144,512]{1,0:T(8,128)S(1)} %get-tuple-element.18), channel_id=1, source_target_pairs={{0,1},{1,0},{2,3},{3,2},{4,5},{5,4},{6,7},{7,6},{8,9},{9,8},{10,11... | collective-permute-start | bytes 884744 | tf_op jit(solution)/shard_map/ppermute | solution.py:706
  9.4 1.6 %collective-permute-start.3 = (f32[216,128]{1,0:T(8,128)S(1)}, f32[216,128]{1,0:T(8,128)S(1)}, u32[]{:S(2)}, u32[]{:S(2)}) collective-permute-start(f32[216,128]{1,0:T(8,128)S(1)} %get-tuple-element.23), channel_id=1, source_target_pairs={{0,16},{1,17},{2,18},{3,19},{4,20},{5,21},{6,22},{7,23},{8,24},{9,... | collective-permute-start | bytes 331784 | tf_op jit(solution)/shard_map/ppermute | solution.py:714
  11.0 1.6 %collective-permute-start.4 = (f32[216,128]{1,0:T(8,128)S(1)}, f32[216,128]{1,0:T(8,128)S(1)}, u32[]{:S(2)}, u32[]{:S(2)}) collective-permute-start(f32[216,128]{1,0:T(8,128)S(1)} %get-tuple-element.24), channel_id=1, source_target_pairs={{0,2},{1,3},{2,0},{3,1},{4,6},{5,7},{6,4},{7,5},{8,10},{9,11},{10,... | collective-permute-start | bytes 331784 | tf_op jit(solution)/shard_map/ppermute | solution.py:714
  13.0 0.7 %collective-permute-start.1 = (f32[144,512]{1,0:T(8,128)S(1)}, f32[144,512]{1,0:T(8,128)S(1)}, u32[]{:S(2)}, u32[]{:S(2)}) collective-permute-start(f32[144,512]{1,0:T(8,128)S(1)} %get-tuple-element.19), channel_id=1, source_target_pairs={{1,2},{3,4},{5,6},{2,1},{4,3},{6,5},{9,10},{11,12},{13,14},{10,9},... | collective-permute-start | bytes 884744 | tf_op jit(solution)/shard_map/ppermute | solution.py:741
  13.7 1.0 %collective-permute-done.3.from_sec = f32[216,128]{1,0:T(8,128)S(1)} collective-permute-done((f32[216,128]{1,0:T(8,128)S(1)}, f32[216,128]{1,0:T(8,128)S(1)}, u32[]{:S(2)}, u32[]{:S(2)}) %collective-permute-start.3) | collective-permute-done | bytes 110624 | tf_op jit(solution)/shard_map/ppermute | solution.py:714
  14.6 2.3 %collective-permute-done.4.from_tile = f32[216,128]{1,0:T(8,128)S(1)} collective-permute-done((f32[216,128]{1,0:T(8,128)S(1)}, f32[216,128]{1,0:T(8,128)S(1)}, u32[]{:S(2)}, u32[]{:S(2)}) %collective-permute-start.4) | collective-permute-done | bytes 110624 | tf_op jit(solution)/shard_map/ppermute | solution.py:714
  17.0 1.5 %collective-permute-done.5.from_both = f32[216,128]{1,0:T(8,128)S(1)} collective-permute-done((f32[216,128]{1,0:T(8,128)S(1)}, f32[216,128]{1,0:T(8,128)S(1)}, u32[]{:S(2)}, u32[]{:S(2)}) %collective-permute-start.5) | collective-permute-done | bytes 110624 | tf_op jit(solution)/shard_map/ppermute | solution.py:714
  18.5 2.7 %collective-permute-start.6 = (f32[216,128]{1,0:T(8,128)S(1)}, f32[216,128]{1,0:T(8,128)S(1)}, u32[]{:S(2)}, u32[]{:S(2)}) collective-permute-start(f32[216,128]{1,0:T(8,128)S(1)} %get-tuple-element.30), channel_id=1, source_target_pairs={{0,4},{1,5},{2,6},{3,7},{4,0},{5,1},{6,2},{7,3},{8,12},{9,13},{10,... | collective-permute-start | bytes 331784 | tf_op jit(solution)/shard_map/ppermute | solution.py:706
  21.2 0.7 %shard_map.86.refs_0_.refs_1_ = f32[163,128]{1,0:T(8,128)S(1)} custom-call(f32[24]{0:T(128)S(1)} %copy-done.7, f32[2,24]{1,0:T(2,128)S(1)} %copy-done.5, f32[2,8]{1,0:T(2,128)S(1)} %copy-done.6, f32[3]{0:T(128)S(1)} %copy-done.8), custom_call_target="tpu_custom_call" | custom-call | bytes 1048576 | tf_op jit(solution)/shard_map/pallas_call | solution.py:18
  21.9 3.1 %shard_map.94 = (f32[4,24,24,128]{3,2,1,0:T(8,128)S(1)}, f32[3,4,24,128]{3,2,1,0:T(8,128)S(1)}, bf16[512,512]{1,0:T(8,128)(2,1)S(1)}) custom-call(s32[4,4]{1,0:T(4,128)S(1)} %copy-done.4, f32[163,128]{1,0:T(8,128)S(1)} %shard_map.86.refs_0_.refs_1_, f32[384,512]{1,0:T(8,128)S(1)} %bitcast.8), custom_call_target="tpu_custom_call" | custom-call | bytes 6291456 | tf_op jit(solution)/shard_map/pallas_call | solution.py:18
  25.0 4.0 %shard_map.91 = (f32[384,1024]{1,0:T(8,128)}, f32[2,192,128]{2,1,0:T(8,128)S(1)}) custom-call(f32[163,128]{1,0:T(8,128)S(1)} %shard_map.86.refs_0_.refs_1_, f32[384,1024]{1,0:T(8,128)S(1)} %bitcast.6, f32[2,216,128]{2,1,0:T(8,128)S(1)} %shard_map.90.refs_2_.refs_1_), custom_call_target="tpu_custom_call" | custom-call | bytes 8388608 | tf_op jit(solution)/shard_map/pallas_call | solution.py:18
  29.3 1.5 %collective-permute-start.9 = (f32[216,128]{1,0:T(8,128)S(1)}, f32[216,128]{1,0:T(8,128)S(1)}, u32[]{:S(2)}, u32[]{:S(2)}) collective-permute-start(f32[216,128]{1,0:T(8,128)S(1)} %shard_map.95.refs_2_), channel_id=1, source_target_pairs={{0,3},{1,2},{2,1},{3,0},{4,7},{5,6},{6,5},{7,4},{8,11},{9,10},{10,... | collective-permute-start | bytes 331784 | tf_op jit(solution)/shard_map/ppermute | solution.py:706
  30.8 0.5 %collective-permute-start.8 = (f32[216,128]{1,0:T(8,128)S(1)}, f32[216,128]{1,0:T(8,128)S(1)}, u32[]{:S(2)}, u32[]{:S(2)}) collective-permute-start(f32[216,128]{1,0:T(8,128)S(1)} %shard_map.95.refs_2_), channel_id=1, source_target_pairs={{0,2},{1,3},{2,0},{3,1},{4,6},{5,7},{6,4},{7,5},{8,10},{9,11},{10,... | collective-permute-start | bytes 331784 | tf_op jit(solution)/shard_map/ppermute | solution.py:706
  31.3 1.5 %collective-permute-start.7 = (f32[216,128]{1,0:T(8,128)S(1)}, f32[216,128]{1,0:T(8,128)S(1)}, u32[]{:S(2)}, u32[]{:S(2)}) collective-permute-start(f32[216,128]{1,0:T(8,128)S(1)} %shard_map.95.refs_2_), channel_id=1, source_target_pairs={{0,1},{1,0},{2,3},{3,2},{4,5},{5,4},{6,7},{7,6},{8,9},{9,8},{10,11... | collective-permute-start | bytes 331784 | tf_op jit(solution)/shard_map/ppermute | solution.py:706
  32.8 0.9 %shard_map.92 = f32[384,1024]{1,0:T(8,128)} custom-call(f32[163,128]{1,0:T(8,128)S(1)} %shard_map.86.refs_0_.refs_1_, f32[144,512]{1,0:T(8,128)S(1)} %collective-permute-done.refs_1_.refs_3_.refs_2_, f32[144,512]{1,0:T(8,128)S(1)} %collective-permute-done.1.refs_2_.refs_3_, ...), custom_call_target="tpu_custom_call", output_to_operand_aliasing={{}: (4, {})} | custom-call | bytes 1048576 | tf_op jit(solution)/shard_map/pallas_call | solution.py:18
  33.8 1.2 %shard_map.96.refs_6_ = f32[4,24,24,128]{3,2,1,0:T(8,128)S(1)} custom-call(f32[163,128]{1,0:T(8,128)S(1)} %shard_map.86.refs_0_.refs_1_, f32[384,512]{1,0:T(8,128)S(1)} %bitcast.9, f32[144,512]{1,0:T(8,128)S(1)} %collective-permute-done.refs_1_.refs_3_.refs_2_, ...), custom_call_target="tpu_custom_call", output_to_operand_aliasing={{}: (5, {})} | custom-call | bytes 3145728 | tf_op jit(solution)/shard_map/pallas_call | solution.py:18
  35.0 0.5 %collective-permute-done.8.refs_4_ = f32[216,128]{1,0:T(8,128)S(1)} collective-permute-done((f32[216,128]{1,0:T(8,128)S(1)}, f32[216,128]{1,0:T(8,128)S(1)}, u32[]{:S(2)}, u32[]{:S(2)}) %collective-permute-start.8) | collective-permute-done | bytes 110624 | tf_op jit(solution)/shard_map/ppermute | solution.py:706
  35.5 0.6 %collective-permute-done.7.refs_3_ = f32[216,128]{1,0:T(8,128)S(1)} collective-permute-done((f32[216,128]{1,0:T(8,128)S(1)}, f32[216,128]{1,0:T(8,128)S(1)}, u32[]{:S(2)}, u32[]{:S(2)}) %collective-permute-start.7) | collective-permute-done | bytes 110624 | tf_op jit(solution)/shard_map/ppermute | solution.py:706
  36.2 7.1 %shard_map.97 = f32[384,512]{1,0:T(8,128)} custom-call(s32[8,128]{1,0:T(8,128)S(1)} %get-tuple-element.28.refs_0_, f32[163,128]{1,0:T(8,128)S(1)} %shard_map.86.refs_0_.refs_1_, f32[216,128]{1,0:T(8,128)S(1)} %shard_map.95.refs_2_, f32[216,128]{1,0:T(8,128)S(1)} %collective-permute-done.7.refs_3_, f32[216,128]{1,0:T(8,128)S(1)} %collective-permute-done.8.refs_4_, ...), custom_call_target="tpu_custom_call" | custom-call | bytes 16777216 | tf_op jit(solution)/shard_map/pallas_call | solution.py:18
  (26 shorter events, 0.8 us)
Async XLA Ops:
  0.6 1.4 %copy-start = (f32[16,24,1024]{2,1,0:T(8,128)S(1)}, f32[16,24,1024]{2,1,0:T(8,128)}, u32[]{:S(2)}) copy-start(f32[16,24,1024]{2,1,0:T(8,128)} %param.7) | copy-start | bytes 4718596
  2.0 0.7 %copy-start.3 = (s32[4,4]{1,0:T(4,128)S(1)}, s32[4,4]{1,0:T(4,128)}, u32[]{:S(2)}) copy-start(s32[4,4]{1,0:T(4,128)} %refs_0_.3) | copy-start | bytes 196
  2.7 3.3 %copy-start.2 = (f32[1,16,24,512]{3,2,1,0:T(8,128)S(1)}, f32[1,16,24,512]{3,2,1,0:T(8,128)}, u32[]{:S(2)}) copy-start(f32[1,16,24,512]{3,2,1,0:T(8,128)} %param.8) | copy-start | bytes 2359300
  5.5 3.8 %collective-permute-start.2 = (f32[2,408,128]{2,1,0:T(8,128)S(1)}, f32[2,408,128]{2,1,0:T(8,128)S(1)}, u32[]{:S(2)}, u32[]{:S(2)}) collective-permute-start(f32[2,408,128]{2,1,0:T(8,128)S(1)} %get-tuple-element.21), channel_id=1, source_target_pairs={{0,8},{8,0},{16,24},{24,16},{1,9},{9,1},{17,25},{25,17},{2,10},{10... | collective-permute-start | bytes 1253384 | tf_op jit(solution)/shard_map/ppermute | solution.py:706
  6.1 15.1 %copy-start.5 = (f32[2,24]{1,0:T(2,128)S(1)}, f32[2,24]{1,0:T(2,128)}, u32[]{:S(2)}) copy-start(f32[2,24]{1,0:T(2,128)} %wind.1) | copy-start | bytes 580
  6.1 15.1 %copy-start.6 = (f32[2,8]{1,0:T(2,128)S(1)}, f32[2,8]{1,0:T(2,128)}, u32[]{:S(2)}) copy-start(f32[2,8]{1,0:T(2,128)} %conv.1) | copy-start | bytes 196
  6.1 15.1 %copy-start.7 = (f32[24]{0:T(128)S(1)}, f32[24]{0:T(128)}, u32[]{:S(2)}) copy-start(f32[24]{0:T(128)} %diff.1) | copy-start | bytes 292
  6.1 15.1 %copy-start.8 = (f32[3]{0:T(128)S(1)}, f32[3]{0:T(128)}, u32[]{:S(2)}) copy-start(f32[3]{0:T(128)} %mix.1) | copy-start | bytes 40
  6.1 15.8 %copy-start.4 = (s32[4,4]{1,0:T(4,128)S(1)}, s32[4,4]{1,0:T(4,128)}, u32[]{:S(2)}) copy-start(s32[4,4]{1,0:T(4,128)} %refs_0_.3) | copy-start | bytes 196
  6.8 18.2 %copy-start.1 = (f32[16,24,1024]{2,1,0:T(8,128)S(1)}, f32[16,24,1024]{2,1,0:T(8,128)}, u32[]{:S(2)}) copy-start(f32[16,24,1024]{2,1,0:T(8,128)} %param.7) | copy-start | bytes 4718596
  6.8 22.2 %collective-permute-start = (f32[144,512]{1,0:T(8,128)S(1)}, f32[144,512]{1,0:T(8,128)S(1)}, u32[]{:S(2)}, u32[]{:S(2)}) collective-permute-start(f32[144,512]{1,0:T(8,128)S(1)} %get-tuple-element.18), channel_id=1, source_target_pairs={{0,1},{1,0},{2,3},{3,2},{4,5},{5,4},{6,7},{7,6},{8,9},{9,8},{10,11... | collective-permute-start | bytes 884744 | tf_op jit(solution)/shard_map/ppermute | solution.py:706
  9.4 5.2 %collective-permute-start.3 = (f32[216,128]{1,0:T(8,128)S(1)}, f32[216,128]{1,0:T(8,128)S(1)}, u32[]{:S(2)}, u32[]{:S(2)}) collective-permute-start(f32[216,128]{1,0:T(8,128)S(1)} %get-tuple-element.23), channel_id=1, source_target_pairs={{0,16},{1,17},{2,18},{3,19},{4,20},{5,21},{6,22},{7,23},{8,24},{9,... | collective-permute-start | bytes 331784 | tf_op jit(solution)/shard_map/ppermute | solution.py:714
  11.0 5.9 %collective-permute-start.4 = (f32[216,128]{1,0:T(8,128)S(1)}, f32[216,128]{1,0:T(8,128)S(1)}, u32[]{:S(2)}, u32[]{:S(2)}) collective-permute-start(f32[216,128]{1,0:T(8,128)S(1)} %get-tuple-element.24), channel_id=1, source_target_pairs={{0,2},{1,3},{2,0},{3,1},{4,6},{5,7},{6,4},{7,5},{8,10},{9,11},{10,... | collective-permute-start | bytes 331784 | tf_op jit(solution)/shard_map/ppermute | solution.py:714
  12.6 5.8 %collective-permute-start.5 = (f32[216,128]{1,0:T(8,128)S(1)}, f32[216,128]{1,0:T(8,128)S(1)}, u32[]{:S(2)}, u32[]{:S(2)}) collective-permute-start(f32[216,128]{1,0:T(8,128)S(1)} %get-tuple-element.25), channel_id=1, source_target_pairs={{0,18},{1,19},{2,16},{3,17},{4,22},{5,23},{6,20},{7,21},{8,26},{9,... | collective-permute-start | bytes 331784 | tf_op jit(solution)/shard_map/ppermute | solution.py:714
  13.0 19.8 %collective-permute-start.1 = (f32[144,512]{1,0:T(8,128)S(1)}, f32[144,512]{1,0:T(8,128)S(1)}, u32[]{:S(2)}, u32[]{:S(2)}) collective-permute-start(f32[144,512]{1,0:T(8,128)S(1)} %get-tuple-element.19), channel_id=1, source_target_pairs={{1,2},{3,4},{5,6},{2,1},{4,3},{6,5},{9,10},{11,12},{13,14},{10,9},... | collective-permute-start | bytes 884744 | tf_op jit(solution)/shard_map/ppermute | solution.py:741
  18.5 10.7 %collective-permute-start.6 = (f32[216,128]{1,0:T(8,128)S(1)}, f32[216,128]{1,0:T(8,128)S(1)}, u32[]{:S(2)}, u32[]{:S(2)}) collective-permute-start(f32[216,128]{1,0:T(8,128)S(1)} %get-tuple-element.30), channel_id=1, source_target_pairs={{0,4},{1,5},{2,6},{3,7},{4,0},{5,1},{6,2},{7,3},{8,12},{9,13},{10,... | collective-permute-start | bytes 331784 | tf_op jit(solution)/shard_map/ppermute | solution.py:706
  29.3 5.7 %collective-permute-start.9 = (f32[216,128]{1,0:T(8,128)S(1)}, f32[216,128]{1,0:T(8,128)S(1)}, u32[]{:S(2)}, u32[]{:S(2)}) collective-permute-start(f32[216,128]{1,0:T(8,128)S(1)} %shard_map.95.refs_2_), channel_id=1, source_target_pairs={{0,3},{1,2},{2,1},{3,0},{4,7},{5,6},{6,5},{7,4},{8,11},{9,10},{10,... | collective-permute-start | bytes 331784 | tf_op jit(solution)/shard_map/ppermute | solution.py:706
  30.8 4.7 %collective-permute-start.8 = (f32[216,128]{1,0:T(8,128)S(1)}, f32[216,128]{1,0:T(8,128)S(1)}, u32[]{:S(2)}, u32[]{:S(2)}) collective-permute-start(f32[216,128]{1,0:T(8,128)S(1)} %shard_map.95.refs_2_), channel_id=1, source_target_pairs={{0,2},{1,3},{2,0},{3,1},{4,6},{5,7},{6,4},{7,5},{8,10},{9,11},{10,... | collective-permute-start | bytes 331784 | tf_op jit(solution)/shard_map/ppermute | solution.py:706
  31.3 4.8 %collective-permute-start.7 = (f32[216,128]{1,0:T(8,128)S(1)}, f32[216,128]{1,0:T(8,128)S(1)}, u32[]{:S(2)}, u32[]{:S(2)}) collective-permute-start(f32[216,128]{1,0:T(8,128)S(1)} %shard_map.95.refs_2_), channel_id=1, source_target_pairs={{0,1},{1,0},{2,3},{3,2},{4,5},{5,4},{6,7},{7,6},{8,9},{9,8},{10,11... | collective-permute-start | bytes 331784 | tf_op jit(solution)/shard_map/ppermute | solution.py:706

commit v3 on v2

--- a/solution.py
+++ b/solution.py
@@ -12,6 +12,8 @@
 VMEM = pl.BlockSpec(memory_space=pltpu.VMEM)
 SMEM = pl.BlockSpec(memory_space=pltpu.SMEM)
 ANY = pl.BlockSpec(memory_space=pl.ANY)
+HBM = pl.BlockSpec(memory_space=pltpu.HBM)
+TOGETHER = 8
 
 
 def call(kernel, outs, args, specs, scratch=(), limit=16, cost=0, out_specs=None, same=None):
@@ -66,7 +68,15 @@
         copy.wait()
 
 
-def extract(rows, chan, box, parent, keep, send, anchor):
+def extract(rows, chan, box_in, parent_in, keep, send, anchor, box, parent, sems):
+    copies = [
+        pltpu.make_async_copy(box_in, box, sems.at[0]),
+        pltpu.make_async_copy(parent_in, parent, sems.at[1]),
+    ]
+    for copy in copies:
+        copy.start()
+    for copy in copies:
+        copy.wait()
     cols = parent.shape[1]
     blocks = cols // LANES
     groups = chan // 8
@@ -79,7 +89,7 @@
         return pl.ds(aligned(row * chan + 8 * g, 8), 8)
 
     lane_row = lax.div(lane, 2)
-    together = 4
+    together = TOGETHER
 
     def outer(step, packed):
         packed = list(packed)
@@ -136,9 +146,19 @@
                     dest[i, where, :] = main
                 return tuple(packed)
 
-            packed = lax.fori_loop(0, rows // together, inner, tuple(h * sent for h in halo))
-            for g in range(groups):
-                dest[i, pl.ds(rows * chan + 8 * g, 8), :] = packed[g]
+            here = (offset >= -LANES) & (offset <= cols)
+
+            @pl.when(here)
+            def _():
+                packed = lax.fori_loop(0, rows // together, inner, tuple(h * sent for h in halo))
+                for g in range(groups):
+                    dest[i, pl.ds(rows * chan + 8 * g, 8), :] = packed[g]
+
+            @pl.when(jnp.logical_not(here))
+            def _():
+                dest[i, pl.ds(0, rows * chan), :] = jnp.zeros((rows * chan, LANES), F32)
+                for g in range(groups):
+                    dest[i, pl.ds(rows * chan + 8 * g, 8), :] = halo[g] * sent
 
 
 def combine(bit, own, got, keep, send):
@@ -164,7 +184,7 @@
         dest[pl.ds(size, chan), :] = own[nest, at, :] + got[nest, at, :]
 
 
-def gathered(mine, from_sec, from_tile, from_both, out):
+def gathered(mine, from_sec, from_tile, from_both, moved, out):
     out[0] = mine[...] + from_sec[...]
     out[1] = from_tile[...] + from_both[...]
 
@@ -223,7 +243,7 @@
                 dest[at, :] = jnp.where(second, both[1, at, :], both[0, at, :])
 
 
-def settle(rows, chan, own_rows, tiles, anchor, mine, got, near, nest, parent, out):
+def settle(rows, chan, own_rows, tiles, anchor, mine, got, near, parent, out):
     start = anchor[...]
     tile = lax.axis_index("tile")
     part = lax.rem(lax.div(tile, 2), 2)
@@ -239,36 +259,37 @@
 
 
 def table_rows(chan, levels):
-    return 4 * chan + 2 * levels + 6 * levels + 3
+    return 4 * chan + 2 * levels + chan
 
 
 def make_table(diff, wind, conv, mix, table):
     chan, levels = diff.shape[0], conv.shape[1]
 
+    def line(value):
+        return jnp.full((1, LANES), value, F32)
+
     def put(i, value):
-        table[pl.ds(i, 1), :] = jnp.full((1, LANES), value, F32)
-
-    for c in range(chan):
-        d, wx, wy = diff[c], wind[0, c], wind[1, c]
-        for k, value in enumerate((1.0 - 4.0 * d - wx - wy, d + wx, d + wy, d)):
-            put(4 * c + k, value)
-    base = 4 * chan
-    for f in range(2):
-        for l in range(levels):
-            put(base + f * levels + l, conv[f, l])
-    base += 2 * levels
+        table[pl.ds(i, 1), :] = value
+
+    scale = {}
     for f in range(3):
-        m = jnp.full((1, LANES), mix[f], F32)
+        m = line(mix[f])
         ratio = None
         for l in range(levels):
+            c = f * levels + l
             pivot = 1.0 + (1.0 if l in (0, levels - 1) else 2.0) * m
             if l:
                 pivot = pivot - m * ratio
             inverse = 1.0 / pivot
             ratio = m * inverse
-            table[pl.ds(base + 2 * (f * levels + l), 1), :] = inverse
-            table[pl.ds(base + 2 * (f * levels + l) + 1, 1), :] = ratio
-        put(base + 6 * levels + f, mix[f])
+            put(4 * chan + 2 * levels + c, ratio)
+            scale[c] = inverse * (1.0 - line(conv[f, l])) if f < 2 else inverse
+            d, wx, wy = diff[c], wind[0, c], wind[1, c]
+            for k, value in enumerate((1.0 - 4.0 * d - wx - wy, d + wx, d + wy, d)):
+                put(4 * c + k, scale[c] * line(value))
+            if f:
+                before = c - levels
+                put(4 * chan + before, scale[c] * line(conv[f - 1, l]) / scale[before])
 
 
 def rows_of(table):
@@ -294,40 +315,30 @@
 
 def mix_blocks(chan, table, fields, stores):
     levels = chan // 3
-    count = len(stores)
+    blocks = range(len(stores))
     coef = rows_of(table)
-    conv = 4 * chan
-    solve = conv + 2 * levels
-    passed = None
-    for f in range(3):
-        ys, carry = [], []
-        for l in range(levels):
+    ys = {}
+    for l in range(levels):
+        for f in range(3):
             c = f * levels + l
-            given = fields(c)
-            rate = coef(conv + f * levels + l) if f < 2 else None
-            ratio = coef(solve + 2 * (c - 1) + 1) if l else None
-            row, moved = [], []
-            for b in range(count):
-                h = given[b]
-                if passed is not None:
-                    h = h + passed[l][b]
-                if f < 2:
-                    moved.append(rate * h)
-                    h = h - moved[b]
-                if l:
-                    h = h + ratio * ys[-1][b]
-                row.append(h)
-            ys.append(row)
-            carry.append(moved)
-        passed = carry
-        m = coef(solve + 6 * levels + f)
-        x = [None] * count
-        for l in range(levels - 1, -1, -1):
+            row = fields(c)
+            if f:
+                rate = coef(4 * chan + c - levels)
+                row = [row[b] + rate * given[b] for b in blocks]
+            given = row
+            if l:
+                ratio = coef(4 * chan + 2 * levels + c)
+                row = [row[b] + ratio * ys[c - 1][b] for b in blocks]
+            ys[c] = row
+    xs = {}
+    for l in range(levels - 1, -1, -1):
+        for f in range(3):
             c = f * levels + l
-            inverse = coef(solve + 2 * c)
-            for b in range(count):
-                x[b] = inverse * (ys[l][b] if x[b] is None else ys[l][b] + m * x[b])
-                stores[b](c, x[b])
+            xs[f] = ys[c] if l == levels - 1 else [
+                ys[c][b] + coef(4 * chan + 2 * levels + c) * xs[f][b] for b in blocks
+            ]
+            for b in blocks:
+                stores[b](c, xs[f][b])
 
 
 def sides(lane, west, v, east):
@@ -481,7 +492,8 @@
     step_blocks(chan, table, loads, stores)
 
 
-def nest_first(chan, deep, box, table, nest, moved, nudge, back, matrix, ext):
+def nest_first(chan, deep, box, diff, wind, conv, mix, nest, moved, nudge, back, table, matrix, ext):
+    make_table(diff, wind, conv, mix, table)
     nest_rows = nest.shape[0] // chan
     planes = nest.shape[1] // LANES
     ext_rows = nest_rows + 2 * deep
@@ -630,38 +642,46 @@
         p = lax.rem(sub, RATIO).astype(F32) / RATIO
         share.append(jnp.where(first_row + rb + sub >= RATIO * (own_rows * tiles - 1), 0.0, p))
 
-    @pl.loop(0, chan)
-    def _(c):
-        for rb in range(0, ext_rows, 8):
-            u = rb // RATIO
-            at = pl.ds(rb, 8)
-            lines = []
-            for t in range(2):
-                r0, r1, r2 = (
-                    jnp.broadcast_to(coarse[t, c, pl.ds(u + i, 1), :], (8, LANES)) for i in range(3)
-                )
-                a0 = jnp.where(sub < RATIO, r0, r1)
-                a1 = jnp.where(sub < RATIO, r1, r2)
-                line = a0 + share[rb // 8] * (a1 - a0)
-                beside = jnp.where(lane == LANES - 1, line, pltpu.roll(line, LANES - 1, axis=1))
-                lines.append((line, (beside - line) * (1.0 / RATIO)))
-            for k in range(planes):
-                b = nudge[1, k, at, :]
-                old, new = (b * (line + float(k) * slope if k else line) for line, slope in lines)
-                force[0, k, c, at, :] = old
-                force[1, k, c, at, :] = new
-                state[0, k, c, pl.ds(8 + rb, 8), :] = moved[k, c, at, :] + (old + new * (1.0 / NSTEP))
+    together = 3
+
+    @pl.loop(0, chan // together)
+    def _(i):
+        for c in (together * i + t for t in range(together)):
+            for rb in range(0, ext_rows, 8):
+                u = rb // RATIO
+                at = pl.ds(rb, 8)
+                lines = []
+                for t in range(2):
+                    r0, r1, r2 = (
+                        jnp.broadcast_to(coarse[t, c, pl.ds(u + n, 1), :], (8, LANES)) for n in range(3)
+                    )
+                    a0 = jnp.where(sub < RATIO, r0, r1)
+                    a1 = jnp.where(sub < RATIO, r1, r2)
+                    level = a0 + share[rb // 8] * (a1 - a0)
+                    beside = jnp.where(lane == LANES - 1, level, pltpu.roll(level, LANES - 1, axis=1))
+                    slope = (beside - level) * (1.0 / RATIO)
+                    force[t, c, at, :] = level
+                    force[2 + t, c, at, :] = slope
+                    lines.append((level, slope))
+                level, slope = (old + new * (1.0 / NSTEP) for old, new in zip(*lines))
+                for k in range(planes):
+                    g = level + float(k) * slope if k else level
+                    state[0, k, c, pl.ds(8 + rb, 8), :] = moved[k, c, at, :] + nudge[1, k, at, :] * g
 
     def advance(step, src, rb, put):
         weight = jnp.float32(step + 1) / NSTEP
+        at = pl.ds(rb, 8)
+        lines = {}
 
         def load(shift, k, c):
             return state[src, k, c, pl.ds(8 + rb + shift, 8), :]
 
         def store(k, c, x):
-            at = pl.ds(rb, 8)
-            g = force[0, k, c, at, :] + weight * force[1, k, c, at, :]
-            put(k, c, nudge[0, k, at, :] * x + g)
+            if c not in lines:
+                lines[c] = [force[t, c, at, :] + weight * force[t + 1, c, at, :] for t in (0, 2)]
+            level, slope = lines[c]
+            g = level + float(k) * slope if k else level
+            put(k, c, nudge[0, k, at, :] * x + nudge[1, k, at, :] * g)
 
         plane_blocks(chan, table, planes, lane, load, store)
 
@@ -740,15 +760,15 @@
     beside = [(i, i + 1) for i in range(1, tiles - 1, 2)]
     far = lax.ppermute(far, "tile", beside + [(j, i) for i, j in beside])
 
-    (table,) = call(
-        make_table, [shape(table_rows(chan, levels), LANES)],
-        (diffusion, wind_speed, conversion, vert_mix), (SMEM,) * 4, limit=2, cost=1 << 20,
-    )
-
     some = shape(secs // 2, strip_rows, LANES)
     keep, send, anchor = call(
         bound(extract, rows, chan), [some, some, shape(8, LANES, dtype=jnp.int32)],
-        (nest_box, parent), (SMEM, VMEM), cost=4 << 20,
+        (nest_box, parent), (HBM, HBM), cost=4 << 20,
+        scratch=[
+            pltpu.SMEM(nest_box.shape, jnp.int32),
+            pltpu.VMEM(parent.shape, F32),
+            pltpu.SemaphoreType.DMA((2,)),
+        ],
     )
     got = exchange(send, "sec", 1)
     bit = 2
@@ -763,9 +783,22 @@
     from_sec = exchange_both(to_sec, secs // 2, 0)
     from_tile = exchange_both(to_tile, 0, 2)
     from_both = exchange_both(to_both, secs // 2, 2)
+    moved_shape = shape(col_blocks, chan, ext_rows, LANES)
+    square = (nest_cols, nest_cols)
+    moved, nudge, back, table = call(
+        bound(nest_first, chan, deep),
+        [moved_shape, shape(3, col_blocks, ext_rows, LANES), shape(*square, dtype=jnp.bfloat16),
+         shape(table_rows(chan, levels), LANES)],
+        (nest_box, diffusion, wind_speed, conversion, vert_mix, nest), (SMEM,) * 5 + (VMEM,), cost=6 << 20,
+        scratch=[
+            pltpu.VMEM(square, jnp.bfloat16),
+            pltpu.VMEM((col_blocks, (nest_rows + 2) * chan, LANES), F32),
+        ],
+    )
+
     two = shape(2, half_rows, LANES)
     (strip,) = call(
-        gathered, [two], (mine, from_sec, from_tile, from_both), (VMEM,) * 4, cost=1 << 18,
+        gathered, [two], (mine, from_sec, from_tile, from_both, moved), (VMEM,) * 5, cost=1 << 18,
     )
     pair = strip
     group = tiles // 2
@@ -790,20 +823,8 @@
         ],
     )
 
-    moved_shape = shape(col_blocks, chan, ext_rows, LANES)
-    square = (nest_cols, nest_cols)
-    moved, nudge, back = call(
-        bound(nest_first, chan, deep),
-        [moved_shape, shape(3, col_blocks, ext_rows, LANES), shape(*square, dtype=jnp.bfloat16)],
-        (nest_box, table, nest), (SMEM, VMEM, VMEM), cost=6 << 20,
-        scratch=[
-            pltpu.VMEM(square, jnp.bfloat16),
-            pltpu.VMEM((col_blocks, (nest_rows + 2) * chan, LANES), F32),
-        ],
-    )
-
     (own,) = call(
-        bound(settle, rows, chan, own_rows, tiles), [half], (anchor, mine, got, near, moved, edges), (VMEM,) * 6, cost=1 << 18,
+        bound(settle, rows, chan, own_rows, tiles), [half], (anchor, mine, got, near, edges), (VMEM,) * 5, cost=1 << 18,
     )
     got_a, got_b, got_c = (exchange(own, "tile", k) for k in (1, 2, 3))
 
@@ -835,7 +856,7 @@
             pltpu.VMEM((2, (span + 1) * chan, LANES), F32),
             pltpu.VMEM((2, chan, 8, LANES), F32),
             pltpu.VMEM((2, col_blocks, chan, ext_rows + 16, LANES), F32),
-            pltpu.VMEM((2, col_blocks, chan, ext_rows, LANES), F32),
+            pltpu.VMEM((4, chan, ext_rows, LANES), F32),
             pltpu.VMEM((nest_rows // 8, col_blocks, 8 * chan, LANES), F32),
             pltpu.VMEM((nest_rows // 8, 8 * chan, nest_cols), F32),
             pltpu.SemaphoreType.DMA((nest_rows // 8,)),

time: 43.5 us -> 41.1 us (0.945)
  Pallas kernels: 20.7 us -> 17.2 us
  waiting for transfers between devices: 6.19 us -> 7.47 us
    ppermute x6, waiting for transfers between devices: 1.44 us -> 5.26 us  [exchange(): lax.ppermute(block, axis, [(i, i ^ bit) for i in range(lax.axis_size(axis...]
    pallas_call x12 -> x11, Pallas kernels: 20.7 us -> 17.2 us  [call(): pl.pallas_call(kernel, out_shape=list(outs), in_specs=list(specs), out_sp...]
    ppermute x3, waiting for transfers between devices: 4.75 us -> 2.21 us  [exchange_both(): return lax.ppermute(block, ('sec', 'tile'), route)]
    unnamed x18 -> x16, local copies, waits for them, and re-layouts: 2.12 us -> 2.12 us
  transfers between devices with their start and end apart: 10 -> 10, of which waited for: 6 -> 3; matrix products, arithmetic and copies ran while one was open for 0% -> 0% of each run, Pallas kernels for 25% -> 24%
where the time goes in v3:
time: 41.1 us
  Pallas kernels  17.2 us (42%)
  starting transfers between devices  13.5 us (33%)
  waiting for transfers between devices  7.47 us (18%)
  local copies, waits for them, and re-layouts  2.12 us (5%)
  between operations  0.85 us (2%)
    pallas_call x11, Pallas kernels, call(): pl.pallas_call(kernel, out_shape=list(outs), in_specs=list(specs), out_sp...  17.2 us
    ppermute x6, starting transfers between devices, exchange(): lax.ppermute(block, axis, [(i, i ^ bit) for i in range(lax.axis_size(axis...  9.27 us
    ppermute x6, waiting for transfers between devices, exchange(): lax.ppermute(block, axis, [(i, i ^ bit) for i in range(lax.axis_size(axis...  5.26 us
    ppermute x3, starting transfers between devices, exchange_both(): return lax.ppermute(block, ('sec', 'tile'), route)  3.55 us
    ppermute x3, waiting for transfers between devices, exchange_both(): return lax.ppermute(block, ('sec', 'tile'), route)  2.21 us
    unnamed x16, local copies, waits for them, and re-layouts  2.12 us
  transfers between devices with their start and end apart: 10, of which 3 were waited for; matrix products, arithmetic and copies ran while one was open for 0% of the time, Pallas kernels for 24%

profile of v3, /device:TPU:0, one launch (start us, length us, event | category | flops | bytes accessed | tf_op | source)
XLA Modules:
  0.0 41.1 jit_solution(13379996606614118691)
XLA Ops:
  0.6 0.0 copy-start
  0.6 1.4 %copy-done = f32[16,24,1024]{2,1,0:T(8,128)S(1)} copy-done((f32[16,24,1024]{2,1,0:T(8,128)S(1)}, f32[16,24,1024]{2,1,0:T(8,128)}, u32[]{:S(2)}) %copy-start) | copy-done | bytes 1572888
  2.0 0.7 %copy-done.3 = s32[4,4]{1,0:T(4,128)S(1)} copy-done((s32[4,4]{1,0:T(4,128)S(1)}, s32[4,4]{1,0:T(4,128)}, u32[]{:S(2)}) %copy-start.3) | copy-done | bytes 88
  2.7 1.9 %shard_map.88 = (f32[2,408,128]{2,1,0:T(8,128)S(1)}, f32[2,408,128]{2,1,0:T(8,128)S(1)}, s32[8,128]{1,0:T(8,128)S(1)}) custom-call(s32[4,4]{1,0:T(4,128)S(1)} %copy-done.3, f32[384,1024]{1,0:T(8,128)S(1)} %bitcast.4), custom_call_target="tpu_custom_call" | custom-call | bytes 4194304 | tf_op jit(solution)/shard_map/pallas_call | solution.py:20
  4.6 0.1 collective-permute-start.2
  4.8 0.7 %shard_map.87 = (f32[144,512]{1,0:T(8,128)S(1)}, f32[144,512]{1,0:T(8,128)S(1)}) custom-call(f32[384,512]{1,0:T(8,128)S(1)} %bitcast.7, f32[384,1024]{1,0:T(8,128)S(1)} %bitcast.5), custom_call_target="tpu_custom_call" | custom-call | bytes 1048576 | tf_op jit(solution)/shard_map/pallas_call | solution.py:20
  5.5 3.0 %collective-permute-start = (f32[144,512]{1,0:T(8,128)S(1)}, f32[144,512]{1,0:T(8,128)S(1)}, u32[]{:S(2)}, u32[]{:S(2)}) collective-permute-start(f32[144,512]{1,0:T(8,128)S(1)} %get-tuple-element.20), channel_id=1, source_target_pairs={{0,1},{1,0},{2,3},{3,2},{4,5},{5,4},{6,7},{7,6},{8,9},{9,8},{10,11... | collective-permute-start | bytes 884744 | tf_op jit(solution)/shard_map/ppermute | solution.py:726
  8.5 0.1 shard_map.89
  8.5 0.8 %collective-permute-start.3 = (f32[216,128]{1,0:T(8,128)S(1)}, f32[216,128]{1,0:T(8,128)S(1)}, u32[]{:S(2)}, u32[]{:S(2)}) collective-permute-start(f32[216,128]{1,0:T(8,128)S(1)} %get-tuple-element.25), channel_id=1, source_target_pairs={{0,16},{1,17},{2,18},{3,19},{4,20},{5,21},{6,22},{7,23},{8,24},{9,... | collective-permute-start | bytes 331784 | tf_op jit(solution)/shard_map/ppermute | solution.py:734
  9.3 1.6 %collective-permute-start.4 = (f32[216,128]{1,0:T(8,128)S(1)}, f32[216,128]{1,0:T(8,128)S(1)}, u32[]{:S(2)}, u32[]{:S(2)}) collective-permute-start(f32[216,128]{1,0:T(8,128)S(1)} %get-tuple-element.26), channel_id=1, source_target_pairs={{0,2},{1,3},{2,0},{3,1},{4,6},{5,7},{6,4},{7,5},{8,10},{9,11},{10,... | collective-permute-start | bytes 331784 | tf_op jit(solution)/shard_map/ppermute | solution.py:734
  10.9 1.2 %collective-permute-start.5 = (f32[216,128]{1,0:T(8,128)S(1)}, f32[216,128]{1,0:T(8,128)S(1)}, u32[]{:S(2)}, u32[]{:S(2)}) collective-permute-start(f32[216,128]{1,0:T(8,128)S(1)} %get-tuple-element.27), channel_id=1, source_target_pairs={{0,18},{1,19},{2,16},{3,17},{4,22},{5,23},{6,20},{7,21},{8,26},{9,... | collective-permute-start | bytes 331784 | tf_op jit(solution)/shard_map/ppermute | solution.py:734
  12.1 0.7 %collective-permute-start.1 = (f32[144,512]{1,0:T(8,128)S(1)}, f32[144,512]{1,0:T(8,128)S(1)}, u32[]{:S(2)}, u32[]{:S(2)}) collective-permute-start(f32[144,512]{1,0:T(8,128)S(1)} %get-tuple-element.21), channel_id=1, source_target_pairs={{1,2},{3,4},{5,6},{2,1},{4,3},{6,5},{9,10},{11,12},{13,14},{10,9},... | collective-permute-start | bytes 884744 | tf_op jit(solution)/shard_map/ppermute | solution.py:761
  12.8 3.2 %shard_map.86 = (f32[4,24,24,128]{3,2,1,0:T(8,128)S(1)}, f32[3,4,24,128]{3,2,1,0:T(8,128)S(1)}, bf16[512,512]{1,0:T(8,128)(2,1)S(1)}, f32[136,128]{1,0:T(8,128)S(1)}) custom-call(s32[4,4]{1,0:T(4,128)S(1)} %copy-done.3, f32[24]{0:T(128)S(1)} %copy-done.6, f32[2,24]{1,0:T(2,128)S(1)} %copy-done.4, f32[2,8]{1,0:T(2,128)S(1)} %copy-done.5, f32[3]{0:T(128)S(1)} %copy-done.7, ...), custom_call_target="tpu_custom_call" | custom-call | bytes 6291456 | tf_op jit(solution)/shard_map/pallas_call | solution.py:20
  16.0 2.2 %collective-permute-done.5.from_both = f32[216,128]{1,0:T(8,128)S(1)} collective-permute-done((f32[216,128]{1,0:T(8,128)S(1)}, f32[216,128]{1,0:T(8,128)S(1)}, u32[]{:S(2)}, u32[]{:S(2)}) %collective-permute-start.5) | collective-permute-done | bytes 110624 | tf_op jit(solution)/shard_map/ppermute | solution.py:734
  18.3 2.7 %collective-permute-start.6 = (f32[216,128]{1,0:T(8,128)S(1)}, f32[216,128]{1,0:T(8,128)S(1)}, u32[]{:S(2)}, u32[]{:S(2)}) collective-permute-start(f32[216,128]{1,0:T(8,128)S(1)} %get-tuple-element.33), channel_id=1, source_target_pairs={{0,4},{1,5},{2,6},{3,7},{4,0},{5,1},{6,2},{7,3},{8,12},{9,13},{10,... | collective-permute-start | bytes 331784 | tf_op jit(solution)/shard_map/ppermute | solution.py:726
  21.0 3.9 %shard_map.91 = (f32[384,1024]{1,0:T(8,128)}, f32[2,192,128]{2,1,0:T(8,128)S(1)}) custom-call(f32[136,128]{1,0:T(8,128)S(1)} %get-tuple-element.19.refs_0_.refs_1_, f32[384,1024]{1,0:T(8,128)S(1)} %bitcast.6, f32[2,216,128]{2,1,0:T(8,128)S(1)} %shard_map.90.refs_2_.refs_1_), custom_call_target="tpu_custom_call" | custom-call | bytes 8388608 | tf_op jit(solution)/shard_map/pallas_call | solution.py:20
  24.9 3.5 %collective-permute-done.6.refs_2_ = f32[216,128]{1,0:T(8,128)S(1)} collective-permute-done((f32[216,128]{1,0:T(8,128)S(1)}, f32[216,128]{1,0:T(8,128)S(1)}, u32[]{:S(2)}, u32[]{:S(2)}) %collective-permute-start.6) | collective-permute-done | bytes 110624 | tf_op jit(solution)/shard_map/ppermute | solution.py:726
  28.4 0.1 collective-permute-start.7
  28.5 0.7 %collective-permute-start.8 = (f32[216,128]{1,0:T(8,128)S(1)}, f32[216,128]{1,0:T(8,128)S(1)}, u32[]{:S(2)}, u32[]{:S(2)}) collective-permute-start(f32[216,128]{1,0:T(8,128)S(1)} %shard_map.94.refs_2_), channel_id=1, source_target_pairs={{0,2},{1,3},{2,0},{3,1},{4,6},{5,7},{6,4},{7,5},{8,10},{9,11},{10,... | collective-permute-start | bytes 331784 | tf_op jit(solution)/shard_map/ppermute | solution.py:726
  29.2 2.8 %collective-permute-start.9 = (f32[216,128]{1,0:T(8,128)S(1)}, f32[216,128]{1,0:T(8,128)S(1)}, u32[]{:S(2)}, u32[]{:S(2)}) collective-permute-start(f32[216,128]{1,0:T(8,128)S(1)} %shard_map.94.refs_2_), channel_id=1, source_target_pairs={{0,3},{1,2},{2,1},{3,0},{4,7},{5,6},{6,5},{7,4},{8,11},{9,10},{10,... | collective-permute-start | bytes 331784 | tf_op jit(solution)/shard_map/ppermute | solution.py:726
  32.0 1.2 %shard_map.95.refs_6_ = f32[4,24,24,128]{3,2,1,0:T(8,128)S(1)} custom-call(f32[136,128]{1,0:T(8,128)S(1)} %get-tuple-element.19.refs_0_.refs_1_, f32[384,512]{1,0:T(8,128)S(1)} %bitcast.9, f32[144,512]{1,0:T(8,128)S(1)} %collective-permute-done.refs_1_.refs_3_.refs_2_, ...), custom_call_target="tpu_custom_call", output_to_operand_aliasing={{}: (5, {})} | custom-call | bytes 3145728 | tf_op jit(solution)/shard_map/pallas_call | solution.py:20
  33.1 0.9 %shard_map.92 = f32[384,1024]{1,0:T(8,128)} custom-call(f32[136,128]{1,0:T(8,128)S(1)} %get-tuple-element.19.refs_0_.refs_1_, f32[144,512]{1,0:T(8,128)S(1)} %collective-permute-done.refs_1_.refs_3_.refs_2_, f32[144,512]{1,0:T(8,128)S(1)} %collective-permute-done.1.refs_2_.refs_3_, ...), custom_call_target="tpu_custom_call", output_to_operand_aliasing={{}: (4, {})} | custom-call | bytes 1048576 | tf_op jit(solution)/shard_map/pallas_call | solution.py:20
  34.1 1.8 %collective-permute-done.9.refs_5_ = f32[216,128]{1,0:T(8,128)S(1)} collective-permute-done((f32[216,128]{1,0:T(8,128)S(1)}, f32[216,128]{1,0:T(8,128)S(1)}, u32[]{:S(2)}, u32[]{:S(2)}) %collective-permute-start.9) | collective-permute-done | bytes 110624 | tf_op jit(solution)/shard_map/ppermute | solution.py:726
  35.9 5.2 %shard_map.96 = f32[384,512]{1,0:T(8,128)} custom-call(s32[8,128]{1,0:T(8,128)S(1)} %get-tuple-element.31.refs_0_, f32[136,128]{1,0:T(8,128)S(1)} %get-tuple-element.19.refs_0_.refs_1_, f32[216,128]{1,0:T(8,128)S(1)} %shard_map.94.refs_2_, f32[216,128]{1,0:T(8,128)S(1)} %collective-permute-done.7.refs_3_, f32[216,128]{1,0:T(8,128)S(1)} %collective-permute-done.8.refs_4_, ...), custom_call_target="tpu_custom_call" | custom-call | bytes 16777216 | tf_op jit(solution)/shard_map/pallas_call | solution.py:20
  (23 shorter events, 0.2 us)
Async XLA Ops:
  0.6 1.4 %copy-start = (f32[16,24,1024]{2,1,0:T(8,128)S(1)}, f32[16,24,1024]{2,1,0:T(8,128)}, u32[]{:S(2)}) copy-start(f32[16,24,1024]{2,1,0:T(8,128)} %param.7) | copy-start | bytes 4718596
  2.0 0.7 %copy-start.3 = (s32[4,4]{1,0:T(4,128)S(1)}, s32[4,4]{1,0:T(4,128)}, u32[]{:S(2)}) copy-start(s32[4,4]{1,0:T(4,128)} %refs_0_.3) | copy-start | bytes 196
  2.7 2.0 %copy-start.2 = (f32[1,16,24,512]{3,2,1,0:T(8,128)S(1)}, f32[1,16,24,512]{3,2,1,0:T(8,128)}, u32[]{:S(2)}) copy-start(f32[1,16,24,512]{3,2,1,0:T(8,128)} %param.8) | copy-start | bytes 2359300
  4.6 3.8 %collective-permute-start.2 = (f32[2,408,128]{2,1,0:T(8,128)S(1)}, f32[2,408,128]{2,1,0:T(8,128)S(1)}, u32[]{:S(2)}, u32[]{:S(2)}) collective-permute-start(f32[2,408,128]{2,1,0:T(8,128)S(1)} %get-tuple-element.23), channel_id=1, source_target_pairs={{0,8},{8,0},{16,24},{24,16},{1,9},{9,1},{17,25},{25,17},{2,10},{10... | collective-permute-start | bytes 1253384 | tf_op jit(solution)/shard_map/ppermute | solution.py:726
  4.7 8.0 %copy-start.4 = (f32[2,24]{1,0:T(2,128)S(1)}, f32[2,24]{1,0:T(2,128)}, u32[]{:S(2)}) copy-start(f32[2,24]{1,0:T(2,128)} %refs_2_.1) | copy-start | bytes 580
  4.7 8.0 %copy-start.5 = (f32[2,8]{1,0:T(2,128)S(1)}, f32[2,8]{1,0:T(2,128)}, u32[]{:S(2)}) copy-start(f32[2,8]{1,0:T(2,128)} %refs_3_.1) | copy-start | bytes 196
  4.8 8.0 %copy-start.6 = (f32[24]{0:T(128)S(1)}, f32[24]{0:T(128)}, u32[]{:S(2)}) copy-start(f32[24]{0:T(128)} %refs_1_.1) | copy-start | bytes 292
  4.8 8.0 %copy-start.7 = (f32[3]{0:T(128)S(1)}, f32[3]{0:T(128)}, u32[]{:S(2)}) copy-start(f32[3]{0:T(128)} %refs_4_.1) | copy-start | bytes 40
  5.5 19.4 %collective-permute-start = (f32[144,512]{1,0:T(8,128)S(1)}, f32[144,512]{1,0:T(8,128)S(1)}, u32[]{:S(2)}, u32[]{:S(2)}) collective-permute-start(f32[144,512]{1,0:T(8,128)S(1)} %get-tuple-element.20), channel_id=1, source_target_pairs={{0,1},{1,0},{2,3},{3,2},{4,5},{5,4},{6,7},{7,6},{8,9},{9,8},{10,11... | collective-permute-start | bytes 884744 | tf_op jit(solution)/shard_map/ppermute | solution.py:726
  8.5 12.5 %copy-start.1 = (f32[16,24,1024]{2,1,0:T(8,128)S(1)}, f32[16,24,1024]{2,1,0:T(8,128)}, u32[]{:S(2)}) copy-start(f32[16,24,1024]{2,1,0:T(8,128)} %param.7) | copy-start | bytes 4718596
  8.5 7.5 %collective-permute-start.3 = (f32[216,128]{1,0:T(8,128)S(1)}, f32[216,128]{1,0:T(8,128)S(1)}, u32[]{:S(2)}, u32[]{:S(2)}) collective-permute-start(f32[216,128]{1,0:T(8,128)S(1)} %get-tuple-element.25), channel_id=1, source_target_pairs={{0,16},{1,17},{2,18},{3,19},{4,20},{5,21},{6,22},{7,23},{8,24},{9,... | collective-permute-start | bytes 331784 | tf_op jit(solution)/shard_map/ppermute | solution.py:734
  9.3 6.7 %collective-permute-start.4 = (f32[216,128]{1,0:T(8,128)S(1)}, f32[216,128]{1,0:T(8,128)S(1)}, u32[]{:S(2)}, u32[]{:S(2)}) collective-permute-start(f32[216,128]{1,0:T(8,128)S(1)} %get-tuple-element.26), channel_id=1, source_target_pairs={{0,2},{1,3},{2,0},{3,1},{4,6},{5,7},{6,4},{7,5},{8,10},{9,11},{10,... | collective-permute-start | bytes 331784 | tf_op jit(solution)/shard_map/ppermute | solution.py:734
  10.9 7.4 %collective-permute-start.5 = (f32[216,128]{1,0:T(8,128)S(1)}, f32[216,128]{1,0:T(8,128)S(1)}, u32[]{:S(2)}, u32[]{:S(2)}) collective-permute-start(f32[216,128]{1,0:T(8,128)S(1)} %get-tuple-element.27), channel_id=1, source_target_pairs={{0,18},{1,19},{2,16},{3,17},{4,22},{5,23},{6,20},{7,21},{8,26},{9,... | collective-permute-start | bytes 331784 | tf_op jit(solution)/shard_map/ppermute | solution.py:734
  12.1 19.9 %collective-permute-start.1 = (f32[144,512]{1,0:T(8,128)S(1)}, f32[144,512]{1,0:T(8,128)S(1)}, u32[]{:S(2)}, u32[]{:S(2)}) collective-permute-start(f32[144,512]{1,0:T(8,128)S(1)} %get-tuple-element.21), channel_id=1, source_target_pairs={{1,2},{3,4},{5,6},{2,1},{4,3},{6,5},{9,10},{11,12},{13,14},{10,9},... | collective-permute-start | bytes 884744 | tf_op jit(solution)/shard_map/ppermute | solution.py:761
  18.3 10.0 %collective-permute-start.6 = (f32[216,128]{1,0:T(8,128)S(1)}, f32[216,128]{1,0:T(8,128)S(1)}, u32[]{:S(2)}, u32[]{:S(2)}) collective-permute-start(f32[216,128]{1,0:T(8,128)S(1)} %get-tuple-element.33), channel_id=1, source_target_pairs={{0,4},{1,5},{2,6},{3,7},{4,0},{5,1},{6,2},{7,3},{8,12},{9,13},{10,... | collective-permute-start | bytes 331784 | tf_op jit(solution)/shard_map/ppermute | solution.py:726
  28.4 5.7 %collective-permute-start.7 = (f32[216,128]{1,0:T(8,128)S(1)}, f32[216,128]{1,0:T(8,128)S(1)}, u32[]{:S(2)}, u32[]{:S(2)}) collective-permute-start(f32[216,128]{1,0:T(8,128)S(1)} %shard_map.94.refs_2_), channel_id=1, source_target_pairs={{0,1},{1,0},{2,3},{3,2},{4,5},{5,4},{6,7},{7,6},{8,9},{9,8},{10,11... | collective-permute-start | bytes 331784 | tf_op jit(solution)/shard_map/ppermute | solution.py:726
  28.5 5.6 %collective-permute-start.8 = (f32[216,128]{1,0:T(8,128)S(1)}, f32[216,128]{1,0:T(8,128)S(1)}, u32[]{:S(2)}, u32[]{:S(2)}) collective-permute-start(f32[216,128]{1,0:T(8,128)S(1)} %shard_map.94.refs_2_), channel_id=1, source_target_pairs={{0,2},{1,3},{2,0},{3,1},{4,6},{5,7},{6,4},{7,5},{8,10},{9,11},{10,... | collective-permute-start | bytes 331784 | tf_op jit(solution)/shard_map/ppermute | solution.py:726
  29.2 6.7 %collective-permute-start.9 = (f32[216,128]{1,0:T(8,128)S(1)}, f32[216,128]{1,0:T(8,128)S(1)}, u32[]{:S(2)}, u32[]{:S(2)}) collective-permute-start(f32[216,128]{1,0:T(8,128)S(1)} %shard_map.94.refs_2_), channel_id=1, source_target_pairs={{0,3},{1,2},{2,1},{3,0},{4,7},{5,6},{6,5},{7,4},{8,11},{9,10},{10,... | collective-permute-start | bytes 331784 | tf_op jit(solution)/shard_map/ppermute | solution.py:726

commit v4 on v3

--- a/solution.py
+++ b/solution.py
@@ -178,8 +178,9 @@
         (to_tile, sec, 1 - part),
         (mine, sec, part),
     ):
-        at = pl.ds(aligned(half * size, 8), size)
-        dest[pl.ds(0, size), :] = own[nest, at, :] + got[nest, at, :]
+        for j in range(rows // 2):
+            at = pl.ds(aligned((2 * j + half) * chan, 8), chan)
+            dest[pl.ds(j * chan, chan), :] = own[nest, at, :] + got[nest, at, :]
         at = pl.ds(rows * chan, chan)
         dest[pl.ds(size, chan), :] = own[nest, at, :] + got[nest, at, :]
 
@@ -236,26 +237,43 @@
     lane_row = lax.div(lane_ids(), 2)
     for dest, owner in ((sent, lax.bitwise_xor(tile, 4)), (mine, tile)):
         for j in range(rows // 2 + 1):
-            row = lane_row if j == rows // 2 else part * (rows // 2) + j
+            row = lane_row if j == rows // 2 else 2 * j + part
             second = wanted(start, base[1] + row, owner, 4, own_rows)
             for g in range(chan // 8):
                 at = pl.ds(j * chan + 8 * g, 8)
                 dest[at, :] = jnp.where(second, both[1, at, :], both[0, at, :])
 
 
-def settle(rows, chan, own_rows, tiles, anchor, mine, got, near, parent, out):
+def settle(rows, chan, own_rows, tiles, anchor, mine, got, near, parent, out, *sent):
     start = anchor[...]
     tile = lax.axis_index("tile")
     part = lax.rem(lax.div(tile, 2), 2)
     base = slot_rows(rows, own_rows, tiles, start)
     lane_row = lax.div(lane_ids(), 2)
-    for j in range(rows // 2 + 1):
-        row = lane_row if j == rows // 2 else part * (rows // 2) + j
+    groups = range(chan // 8)
+    slots = rows // 2
+    held_rows = {}
+    for j in range(slots + 1):
+        row = lane_row if j == slots else 2 * j + part
         keep = wanted(start, base[0] + row, tile, 4, own_rows)
         keep = keep | wanted(start, base[1] + row, tile, 4, own_rows)
-        for g in range(chan // 8):
+        for g in groups:
             at = pl.ds(j * chan + 8 * g, 8)
-            out[at, :] = jnp.where(keep, mine[at, :], got[at, :])
+            held_rows[j, g] = jnp.where(keep, mine[at, :], got[at, :])
+            out[at, :] = held_rows[j, g]
+    for k, dest in enumerate(sent):
+        count = dest.shape[0] // chan - 1
+        first = start + (own_rows * lax.bitwise_xor(tile, k + 1) - 2)
+        first = lax.shift_right_arithmetic(first + lax.bitwise_and(lax.bitwise_xor(first, part), 1), 1)
+        for i in range(count):
+            slot = lax.bitwise_and(first + i, slots - 1)
+            row = [held_rows[0, g] for g in groups]
+            for j in range(1, slots):
+                row = [jnp.where(slot == j, held_rows[j, g], row[g]) for g in groups]
+            for g in groups:
+                dest[pl.ds(i * chan + 8 * g, 8), :] = row[g]
+        for g in groups:
+            dest[pl.ds(count * chan + 8 * g, 8), :] = held_rows[slots, g]
 
 
 def table_rows(chan, levels):
@@ -492,7 +510,7 @@
     step_blocks(chan, table, loads, stores)
 
 
-def nest_first(chan, deep, box, diff, wind, conv, mix, nest, moved, nudge, back, table, matrix, ext):
+def nest_first(chan, deep, box, diff, wind, conv, mix, nest, moved, nudge, back, matrix, table, ext):
     make_table(diff, wind, conv, mix, table)
     nest_rows = nest.shape[0] // chan
     planes = nest.shape[1] // LANES
@@ -544,14 +562,13 @@
         plane_blocks(chan, table, planes, lane, load, store)
 
 
-def nest_edges(chan, deep, table, nest, near, far, nudge, given, moved, matrix, natural, ext):
+def nest_edges(chan, deep, table, nest, near, far, nudge, matrix, given, moved, natural, ext):
     nest_rows = nest.shape[0] // chan
     planes = nest.shape[1] // LANES
     ext_rows = nest_rows + 2 * deep
     size = deep * chan
     lane, sub = lane_ids(), sublane_ids()
     odd = lax.rem(lax.axis_index("tile"), 2) == 1
-    matrix[...] = dealing(nest.shape[1], False)
     edge = (deep + 2) * chan
     a, b = near[pl.ds(0, size), :], far[pl.ds(0, size), :]
     natural[pl.ds(0, size), :] = jnp.where(odd, a, b)
@@ -601,17 +618,19 @@
     part = lax.rem(lax.div(tile, 2), 2)
     side = lax.rem(tile, 2)
 
-    for k, ref in enumerate((own, got_a, got_b, got_c)):
-        slots[k] = ref[...]
+    slots[0] = own[...]
+    for k, ref in enumerate((got_a, got_b, got_c)):
+        count = ref.shape[0] - chan
+        slots[k + 1, pl.ds(0, count), :] = ref[pl.ds(0, count), :]
+        slots[k + 1, pl.ds(size, chan), :] = ref[pl.ds(count, chan), :]
 
     for m in range(span):
         row = start + m
         local = lax.bitwise_and(row, rows - 1)
-        upper = lax.div(local, rows // 2)
         other = lax.bitwise_and(lax.shift_right_arithmetic(row, rows.bit_length() - 1), 1)
-        k = 2 * lax.bitwise_xor(upper, part) + lax.bitwise_xor(other, side)
+        k = 2 * lax.bitwise_xor(lax.bitwise_and(row, 1), part) + lax.bitwise_xor(other, side)
         inside = one_if((row >= 0) & (row < rows * tiles))
-        slot = (local - upper * (rows // 2)) * chan
+        slot = jnp.where(k == 0, lax.shift_right_arithmetic(local, 1), m // 2) * chan
         turn = LANES - 1 - 2 * local
         for g in range(groups):
             at = pl.ds(m * chan + 8 * g, 8)
@@ -642,7 +661,7 @@
         p = lax.rem(sub, RATIO).astype(F32) / RATIO
         share.append(jnp.where(first_row + rb + sub >= RATIO * (own_rows * tiles - 1), 0.0, p))
 
-    together = 3
+    together = 6
 
     @pl.loop(0, chan // together)
     def _(i):
@@ -785,13 +804,12 @@
     from_both = exchange_both(to_both, secs // 2, 2)
     moved_shape = shape(col_blocks, chan, ext_rows, LANES)
     square = (nest_cols, nest_cols)
-    moved, nudge, back, table = call(
+    moved, nudge, back, matrix, table = call(
         bound(nest_first, chan, deep),
         [moved_shape, shape(3, col_blocks, ext_rows, LANES), shape(*square, dtype=jnp.bfloat16),
-         shape(table_rows(chan, levels), LANES)],
+         shape(*square, dtype=jnp.bfloat16), shape(table_rows(chan, levels), LANES)],
         (nest_box, diffusion, wind_speed, conversion, vert_mix, nest), (SMEM,) * 5 + (VMEM,), cost=6 << 20,
         scratch=[
-            pltpu.VMEM(square, jnp.bfloat16),
             pltpu.VMEM((col_blocks, (nest_rows + 2) * chan, LANES), F32),
         ],
     )
@@ -823,10 +841,12 @@
         ],
     )
 
-    (own,) = call(
-        bound(settle, rows, chan, own_rows, tiles), [half], (anchor, mine, got, near, edges), (VMEM,) * 5, cost=1 << 18,
-    )
-    got_a, got_b, got_c = (exchange(own, "tile", k) for k in (1, 2, 3))
+    message = shape(((span + 1) // 2 + 1) * chan, LANES)
+    own, *sent = call(
+        bound(settle, rows, chan, own_rows, tiles), [half] + [message] * 3,
+        (anchor, mine, got, near, edges), (VMEM,) * 5, cost=1 << 18,
+    )
+    got_a, got_b, got_c = (exchange(block, "tile", k + 1) for k, block in enumerate(sent))
 
     (parent_new,) = call(
         bound(parent_edges, rows, chan, deep), [shape(rows * chan, cols)],
@@ -839,9 +859,8 @@
     )
     (moved,) = call(
         bound(nest_edges, chan, deep), [moved_shape],
-        (table, nest, near, far, nudge, moved), (VMEM,) * 6, cost=3 << 20, same={5: 0},
+        (table, nest, near, far, nudge, matrix, moved), (VMEM,) * 7, cost=3 << 20, same={6: 0},
         scratch=[
-            pltpu.VMEM(square, jnp.bfloat16),
             pltpu.VMEM((2 * (deep + 2) * chan, nest_cols), F32),
             pltpu.VMEM((col_blocks, 2 * (deep + 2) * chan, LANES), F32),
         ],

time: 41.1 us -> 39.4 us (0.959); the launches traced: 41.1 us -> 38.7 us
  waiting for transfers between devices: 7.47 us -> 5.99 us
  Pallas kernels: 17.2 us -> 16 us
    pallas_call x11, Pallas kernels: 17.2 us -> 16 us  [call(): pl.pallas_call(kernel, out_shape=list(outs), in_specs=list(specs), out_sp...]
    ppermute x6, waiting for transfers between devices: 5.26 us -> 4.15 us  [exchange(): lax.ppermute(block, axis, [(i, i ^ bit) for i in range(lax.axis_size(axis...]
  transfers between devices with their start and end apart: 10 -> 10, of which waited for: 3 -> 4; matrix products, arithmetic and copies ran while one was open for 0% -> 0% of each run, Pallas kernels for 24% -> 26%
where the time goes in v4:
time: 39.4 us; the launch traced here: 38.7 us
  Pallas kernels  16 us (41%)
  starting transfers between devices  13.8 us (35%)
  waiting for transfers between devices  5.99 us (15%)
  local copies, waits for them, and re-layouts  2.11 us (5%)
  between operations  0.8 us (2%)
    pallas_call x11, Pallas kernels, call(): pl.pallas_call(kernel, out_shape=list(outs), in_specs=list(specs), out_sp...  16 us
    ppermute x6, starting transfers between devices, exchange(): lax.ppermute(block, axis, [(i, i ^ bit) for i in range(lax.axis_size(axis...  9.57 us
    ppermute x6, waiting for transfers between devices, exchange(): lax.ppermute(block, axis, [(i, i ^ bit) for i in range(lax.axis_size(axis...  4.15 us
    ppermute x3, starting transfers between devices, exchange_both(): return lax.ppermute(block, ('sec', 'tile'), route)  3.55 us
    unnamed x16, local copies, waits for them, and re-layouts  2.11 us
    ppermute x3, waiting for transfers between devices, exchange_both(): return lax.ppermute(block, ('sec', 'tile'), route)  1.83 us
  transfers between devices with their start and end apart: 10, of which 4 were waited for; matrix products, arithmetic and copies ran while one was open for 0% of the time, Pallas kernels for 26%

profile of v4, /device:TPU:0, one launch (start us, length us, event | category | flops | bytes accessed | tf_op | source)
XLA Modules:
  0.0 38.7 jit_solution(5786741556028338208)
XLA Ops:
  0.6 1.4 %copy-done = f32[16,24,1024]{2,1,0:T(8,128)S(1)} copy-done((f32[16,24,1024]{2,1,0:T(8,128)S(1)}, f32[16,24,1024]{2,1,0:T(8,128)}, u32[]{:S(2)}) %copy-start) | copy-done | bytes 1572888
  2.0 0.7 %copy-done.3 = s32[4,4]{1,0:T(4,128)S(1)} copy-done((s32[4,4]{1,0:T(4,128)S(1)}, s32[4,4]{1,0:T(4,128)}, u32[]{:S(2)}) %copy-start.3) | copy-done | bytes 88
  2.7 1.0 %shard_map.88 = (f32[2,408,128]{2,1,0:T(8,128)S(1)}, f32[2,408,128]{2,1,0:T(8,128)S(1)}, s32[8,128]{1,0:T(8,128)S(1)}) custom-call(s32[4,4]{1,0:T(4,128)S(1)} %copy-done.3, f32[384,1024]{1,0:T(8,128)S(1)} %bitcast.4), custom_call_target="tpu_custom_call" | custom-call | bytes 4194304 | tf_op jit(solution)/shard_map/pallas_call | solution.py:20
  3.7 0.8 %collective-permute-start.2 = (f32[2,408,128]{2,1,0:T(8,128)S(1)}, f32[2,408,128]{2,1,0:T(8,128)S(1)}, u32[]{:S(2)}, u32[]{:S(2)}) collective-permute-start(f32[2,408,128]{2,1,0:T(8,128)S(1)} %get-tuple-element.28), channel_id=1, source_target_pairs={{0,8},{8,0},{16,24},{24,16},{1,9},{9,1},{17,25},{25,17},{2,10},{10... | collective-permute-start | bytes 1253384 | tf_op jit(solution)/shard_map/ppermute | solution.py:745
  4.6 0.7 %shard_map.87 = (f32[144,512]{1,0:T(8,128)S(1)}, f32[144,512]{1,0:T(8,128)S(1)}) custom-call(f32[384,512]{1,0:T(8,128)S(1)} %bitcast.7, f32[384,1024]{1,0:T(8,128)S(1)} %bitcast.5), custom_call_target="tpu_custom_call" | custom-call | bytes 1048576 | tf_op jit(solution)/shard_map/pallas_call | solution.py:20
  5.2 2.4 %collective-permute-start = (f32[144,512]{1,0:T(8,128)S(1)}, f32[144,512]{1,0:T(8,128)S(1)}, u32[]{:S(2)}, u32[]{:S(2)}) collective-permute-start(f32[144,512]{1,0:T(8,128)S(1)} %get-tuple-element.25), channel_id=1, source_target_pairs={{0,1},{1,0},{2,3},{3,2},{4,5},{5,4},{6,7},{7,6},{8,9},{9,8},{10,11... | collective-permute-start | bytes 884744 | tf_op jit(solution)/shard_map/ppermute | solution.py:745
  7.7 1.9 %collective-permute-start.3 = (f32[216,128]{1,0:T(8,128)S(1)}, f32[216,128]{1,0:T(8,128)S(1)}, u32[]{:S(2)}, u32[]{:S(2)}) collective-permute-start(f32[216,128]{1,0:T(8,128)S(1)} %get-tuple-element.30), channel_id=1, source_target_pairs={{0,16},{1,17},{2,18},{3,19},{4,20},{5,21},{6,22},{7,23},{8,24},{9,... | collective-permute-start | bytes 331784 | tf_op jit(solution)/shard_map/ppermute | solution.py:753
  9.6 1.6 %collective-permute-start.4 = (f32[216,128]{1,0:T(8,128)S(1)}, f32[216,128]{1,0:T(8,128)S(1)}, u32[]{:S(2)}, u32[]{:S(2)}) collective-permute-start(f32[216,128]{1,0:T(8,128)S(1)} %get-tuple-element.31), channel_id=1, source_target_pairs={{0,2},{1,3},{2,0},{3,1},{4,6},{5,7},{6,4},{7,5},{8,10},{9,11},{10,... | collective-permute-start | bytes 331784 | tf_op jit(solution)/shard_map/ppermute | solution.py:753
  11.2 0.1 collective-permute-start.5
  11.3 0.7 %collective-permute-start.1 = (f32[144,512]{1,0:T(8,128)S(1)}, f32[144,512]{1,0:T(8,128)S(1)}, u32[]{:S(2)}, u32[]{:S(2)}) collective-permute-start(f32[144,512]{1,0:T(8,128)S(1)} %get-tuple-element.26), channel_id=1, source_target_pairs={{1,2},{3,4},{5,6},{2,1},{4,3},{6,5},{9,10},{11,12},{13,14},{10,9},... | collective-permute-start | bytes 884744 | tf_op jit(solution)/shard_map/ppermute | solution.py:780
  12.0 3.3 %shard_map.86 = (f32[4,24,24,128]{3,2,1,0:T(8,128)S(1)}, f32[3,4,24,128]{3,2,1,0:T(8,128)S(1)}, bf16[512,512]{1,0:T(8,128)(2,1)S(1)}, bf16[512,512]{1,0:T(8,128)(2,1)S(1)}, f32[136,128]{1,0:T(8,128)S(1)}) custom-call(s32[4,4]{1,0:T(4,128)S(1)} %copy-done.3, f32[24]{0:T(128)S(1)} %copy-done.6, f32[2,24]{1,0:T(2,128)S(1)} %copy-done.4, f32[2,8]{1,0:T(2,128)S(1)} %copy-done.5, ...), custom_call_target="tpu_custom_call" | custom-call | bytes 6291456 | tf_op jit(solution)/shard_map/pallas_call | solution.py:20
  15.3 0.3 collective-permute-done.4.from_tile
  15.6 1.5 %collective-permute-done.5.from_both = f32[216,128]{1,0:T(8,128)S(1)} collective-permute-done((f32[216,128]{1,0:T(8,128)S(1)}, f32[216,128]{1,0:T(8,128)S(1)}, u32[]{:S(2)}, u32[]{:S(2)}) %collective-permute-start.5) | collective-permute-done | bytes 110624 | tf_op jit(solution)/shard_map/ppermute | solution.py:753
  17.2 2.8 %collective-permute-start.6 = (f32[216,128]{1,0:T(8,128)S(1)}, f32[216,128]{1,0:T(8,128)S(1)}, u32[]{:S(2)}, u32[]{:S(2)}) collective-permute-start(f32[216,128]{1,0:T(8,128)S(1)} %get-tuple-element.38), channel_id=1, source_target_pairs={{0,4},{1,5},{2,6},{3,7},{4,0},{5,1},{6,2},{7,3},{8,12},{9,13},{10,... | collective-permute-start | bytes 331784 | tf_op jit(solution)/shard_map/ppermute | solution.py:745
  20.0 3.9 %shard_map.91 = (f32[384,1024]{1,0:T(8,128)}, f32[2,192,128]{2,1,0:T(8,128)S(1)}) custom-call(f32[136,128]{1,0:T(8,128)S(1)} %get-tuple-element.24.refs_0_.refs_1_, f32[384,1024]{1,0:T(8,128)S(1)} %bitcast.6, f32[2,216,128]{2,1,0:T(8,128)S(1)} %shard_map.90.refs_2_.refs_1_), custom_call_target="tpu_custom_call" | custom-call | bytes 8388608 | tf_op jit(solution)/shard_map/pallas_call | solution.py:20
  23.9 2.5 %collective-permute-done.6.refs_2_ = f32[216,128]{1,0:T(8,128)S(1)} collective-permute-done((f32[216,128]{1,0:T(8,128)S(1)}, f32[216,128]{1,0:T(8,128)S(1)}, u32[]{:S(2)}, u32[]{:S(2)}) %collective-permute-start.6) | collective-permute-done | bytes 110624 | tf_op jit(solution)/shard_map/ppermute | solution.py:745
  26.4 0.1 shard_map.94
  26.5 0.7 %collective-permute-start.7 = (f32[144,128]{1,0:T(8,128)S(1)}, f32[144,128]{1,0:T(8,128)S(1)}, u32[]{:S(2)}, u32[]{:S(2)}) collective-permute-start(f32[144,128]{1,0:T(8,128)S(1)} %get-tuple-element.40), channel_id=1, source_target_pairs={{0,1},{1,0},{2,3},{3,2},{4,5},{5,4},{6,7},{7,6},{8,9},{9,8},{10,11... | collective-permute-start | bytes 221192 | tf_op jit(solution)/shard_map/ppermute | solution.py:745
  27.2 1.3 %collective-permute-start.8 = (f32[144,128]{1,0:T(8,128)S(1)}, f32[144,128]{1,0:T(8,128)S(1)}, u32[]{:S(2)}, u32[]{:S(2)}) collective-permute-start(f32[144,128]{1,0:T(8,128)S(1)} %get-tuple-element.41), channel_id=1, source_target_pairs={{0,2},{1,3},{2,0},{3,1},{4,6},{5,7},{6,4},{7,5},{8,10},{9,11},{10,... | collective-permute-start | bytes 221192 | tf_op jit(solution)/shard_map/ppermute | solution.py:745
  28.5 1.5 %collective-permute-start.9 = (f32[144,128]{1,0:T(8,128)S(1)}, f32[144,128]{1,0:T(8,128)S(1)}, u32[]{:S(2)}, u32[]{:S(2)}) collective-permute-start(f32[144,128]{1,0:T(8,128)S(1)} %get-tuple-element.42), channel_id=1, source_target_pairs={{0,3},{1,2},{2,1},{3,0},{4,7},{5,6},{6,5},{7,4},{8,11},{9,10},{10,... | collective-permute-start | bytes 221192 | tf_op jit(solution)/shard_map/ppermute | solution.py:745
  30.0 0.9 %shard_map.92 = f32[384,1024]{1,0:T(8,128)} custom-call(f32[136,128]{1,0:T(8,128)S(1)} %get-tuple-element.24.refs_0_.refs_1_, f32[144,512]{1,0:T(8,128)S(1)} %collective-permute-done.refs_1_.refs_3_.refs_2_, f32[144,512]{1,0:T(8,128)S(1)} %collective-permute-done.1.refs_2_.refs_3_, ...), custom_call_target="tpu_custom_call", output_to_operand_aliasing={{}: (4, {})} | custom-call | bytes 1048576 | tf_op jit(solution)/shard_map/pallas_call | solution.py:20
  31.0 1.1 %shard_map.95.refs_6_ = f32[4,24,24,128]{3,2,1,0:T(8,128)S(1)} custom-call(f32[136,128]{1,0:T(8,128)S(1)} %get-tuple-element.24.refs_0_.refs_1_, f32[384,512]{1,0:T(8,128)S(1)} %bitcast.9, f32[144,512]{1,0:T(8,128)S(1)} %collective-permute-done.refs_1_.refs_3_.refs_2_, ...), custom_call_target="tpu_custom_call", output_to_operand_aliasing={{}: (6, {})} | custom-call | bytes 3145728 | tf_op jit(solution)/shard_map/pallas_call | solution.py:20
  32.1 1.7 %collective-permute-done.9.refs_5_ = f32[144,128]{1,0:T(8,128)S(1)} collective-permute-done((f32[144,128]{1,0:T(8,128)S(1)}, f32[144,128]{1,0:T(8,128)S(1)}, u32[]{:S(2)}, u32[]{:S(2)}) %collective-permute-start.9) | collective-permute-done | bytes 73760 | tf_op jit(solution)/shard_map/ppermute | solution.py:745
  33.8 4.9 %shard_map.96 = f32[384,512]{1,0:T(8,128)} custom-call(s32[8,128]{1,0:T(8,128)S(1)} %get-tuple-element.36.refs_0_, f32[136,128]{1,0:T(8,128)S(1)} %get-tuple-element.24.refs_0_.refs_1_, f32[216,128]{1,0:T(8,128)S(1)} %get-tuple-element.39.refs_2_, f32[144,128]{1,0:T(8,128)S(1)} %collective-permute-done.7.refs_3_, ...), custom_call_target="tpu_custom_call" | custom-call | bytes 16777216 | tf_op jit(solution)/shard_map/pallas_call | solution.py:20
  (23 shorter events, 0.2 us)
Async XLA Ops:
  0.6 1.4 %copy-start = (f32[16,24,1024]{2,1,0:T(8,128)S(1)}, f32[16,24,1024]{2,1,0:T(8,128)}, u32[]{:S(2)}) copy-start(f32[16,24,1024]{2,1,0:T(8,128)} %param.7) | copy-start | bytes 4718596
  2.0 0.7 %copy-start.3 = (s32[4,4]{1,0:T(4,128)S(1)}, s32[4,4]{1,0:T(4,128)}, u32[]{:S(2)}) copy-start(s32[4,4]{1,0:T(4,128)} %refs_0_.3) | copy-start | bytes 196
  2.7 1.8 %copy-start.2 = (f32[1,16,24,512]{3,2,1,0:T(8,128)S(1)}, f32[1,16,24,512]{3,2,1,0:T(8,128)}, u32[]{:S(2)}) copy-start(f32[1,16,24,512]{3,2,1,0:T(8,128)} %param.8) | copy-start | bytes 2359300
  3.7 3.9 %collective-permute-start.2 = (f32[2,408,128]{2,1,0:T(8,128)S(1)}, f32[2,408,128]{2,1,0:T(8,128)S(1)}, u32[]{:S(2)}, u32[]{:S(2)}) collective-permute-start(f32[2,408,128]{2,1,0:T(8,128)S(1)} %get-tuple-element.28), channel_id=1, source_target_pairs={{0,8},{8,0},{16,24},{24,16},{1,9},{9,1},{17,25},{25,17},{2,10},{10... | collective-permute-start | bytes 1253384 | tf_op jit(solution)/shard_map/ppermute | solution.py:745
  4.5 7.4 %copy-start.4 = (f32[2,24]{1,0:T(2,128)S(1)}, f32[2,24]{1,0:T(2,128)}, u32[]{:S(2)}) copy-start(f32[2,24]{1,0:T(2,128)} %refs_2_.1) | copy-start | bytes 580
  4.6 7.4 %copy-start.5 = (f32[2,8]{1,0:T(2,128)S(1)}, f32[2,8]{1,0:T(2,128)}, u32[]{:S(2)}) copy-start(f32[2,8]{1,0:T(2,128)} %refs_3_.1) | copy-start | bytes 196
  4.6 7.4 %copy-start.6 = (f32[24]{0:T(128)S(1)}, f32[24]{0:T(128)}, u32[]{:S(2)}) copy-start(f32[24]{0:T(128)} %refs_1_.1) | copy-start | bytes 292
  4.6 7.4 %copy-start.7 = (f32[3]{0:T(128)S(1)}, f32[3]{0:T(128)}, u32[]{:S(2)}) copy-start(f32[3]{0:T(128)} %refs_4_.1) | copy-start | bytes 40
  5.2 18.6 %collective-permute-start = (f32[144,512]{1,0:T(8,128)S(1)}, f32[144,512]{1,0:T(8,128)S(1)}, u32[]{:S(2)}, u32[]{:S(2)}) collective-permute-start(f32[144,512]{1,0:T(8,128)S(1)} %get-tuple-element.25), channel_id=1, source_target_pairs={{0,1},{1,0},{2,3},{3,2},{4,5},{5,4},{6,7},{7,6},{8,9},{9,8},{10,11... | collective-permute-start | bytes 884744 | tf_op jit(solution)/shard_map/ppermute | solution.py:745
  7.7 12.3 %copy-start.1 = (f32[16,24,1024]{2,1,0:T(8,128)S(1)}, f32[16,24,1024]{2,1,0:T(8,128)}, u32[]{:S(2)}) copy-start(f32[16,24,1024]{2,1,0:T(8,128)} %param.7) | copy-start | bytes 4718596
  7.7 7.5 %collective-permute-start.3 = (f32[216,128]{1,0:T(8,128)S(1)}, f32[216,128]{1,0:T(8,128)S(1)}, u32[]{:S(2)}, u32[]{:S(2)}) collective-permute-start(f32[216,128]{1,0:T(8,128)S(1)} %get-tuple-element.30), channel_id=1, source_target_pairs={{0,16},{1,17},{2,18},{3,19},{4,20},{5,21},{6,22},{7,23},{8,24},{9,... | collective-permute-start | bytes 331784 | tf_op jit(solution)/shard_map/ppermute | solution.py:753
  9.6 6.0 %collective-permute-start.4 = (f32[216,128]{1,0:T(8,128)S(1)}, f32[216,128]{1,0:T(8,128)S(1)}, u32[]{:S(2)}, u32[]{:S(2)}) collective-permute-start(f32[216,128]{1,0:T(8,128)S(1)} %get-tuple-element.31), channel_id=1, source_target_pairs={{0,2},{1,3},{2,0},{3,1},{4,6},{5,7},{6,4},{7,5},{8,10},{9,11},{10,... | collective-permute-start | bytes 331784 | tf_op jit(solution)/shard_map/ppermute | solution.py:753
  11.2 5.9 %collective-permute-start.5 = (f32[216,128]{1,0:T(8,128)S(1)}, f32[216,128]{1,0:T(8,128)S(1)}, u32[]{:S(2)}, u32[]{:S(2)}) collective-permute-start(f32[216,128]{1,0:T(8,128)S(1)} %get-tuple-element.32), channel_id=1, source_target_pairs={{0,18},{1,19},{2,16},{3,17},{4,22},{5,23},{6,20},{7,21},{8,26},{9,... | collective-permute-start | bytes 331784 | tf_op jit(solution)/shard_map/ppermute | solution.py:753
  11.3 18.8 %collective-permute-start.1 = (f32[144,512]{1,0:T(8,128)S(1)}, f32[144,512]{1,0:T(8,128)S(1)}, u32[]{:S(2)}, u32[]{:S(2)}) collective-permute-start(f32[144,512]{1,0:T(8,128)S(1)} %get-tuple-element.26), channel_id=1, source_target_pairs={{1,2},{3,4},{5,6},{2,1},{4,3},{6,5},{9,10},{11,12},{13,14},{10,9},... | collective-permute-start | bytes 884744 | tf_op jit(solution)/shard_map/ppermute | solution.py:780
  17.2 9.2 %collective-permute-start.6 = (f32[216,128]{1,0:T(8,128)S(1)}, f32[216,128]{1,0:T(8,128)S(1)}, u32[]{:S(2)}, u32[]{:S(2)}) collective-permute-start(f32[216,128]{1,0:T(8,128)S(1)} %get-tuple-element.38), channel_id=1, source_target_pairs={{0,4},{1,5},{2,6},{3,7},{4,0},{5,1},{6,2},{7,3},{8,12},{9,13},{10,... | collective-permute-start | bytes 331784 | tf_op jit(solution)/shard_map/ppermute | solution.py:745
  26.5 5.6 %collective-permute-start.7 = (f32[144,128]{1,0:T(8,128)S(1)}, f32[144,128]{1,0:T(8,128)S(1)}, u32[]{:S(2)}, u32[]{:S(2)}) collective-permute-start(f32[144,128]{1,0:T(8,128)S(1)} %get-tuple-element.40), channel_id=1, source_target_pairs={{0,1},{1,0},{2,3},{3,2},{4,5},{5,4},{6,7},{7,6},{8,9},{9,8},{10,11... | collective-permute-start | bytes 221192 | tf_op jit(solution)/shard_map/ppermute | solution.py:745
  27.2 4.9 %collective-permute-start.8 = (f32[144,128]{1,0:T(8,128)S(1)}, f32[144,128]{1,0:T(8,128)S(1)}, u32[]{:S(2)}, u32[]{:S(2)}) collective-permute-start(f32[144,128]{1,0:T(8,128)S(1)} %get-tuple-element.41), channel_id=1, source_target_pairs={{0,2},{1,3},{2,0},{3,1},{4,6},{5,7},{6,4},{7,5},{8,10},{9,11},{10,... | collective-permute-start | bytes 221192 | tf_op jit(solution)/shard_map/ppermute | solution.py:745
  28.5 5.3 %collective-permute-start.9 = (f32[144,128]{1,0:T(8,128)S(1)}, f32[144,128]{1,0:T(8,128)S(1)}, u32[]{:S(2)}, u32[]{:S(2)}) collective-permute-start(f32[144,128]{1,0:T(8,128)S(1)} %get-tuple-element.42), channel_id=1, source_target_pairs={{0,3},{1,2},{2,1},{3,0},{4,7},{5,6},{6,5},{7,4},{8,11},{9,10},{10,... | collective-permute-start | bytes 221192 | tf_op jit(solution)/shard_map/ppermute | solution.py:745

commit v5 on v4

--- a/solution.py
+++ b/solution.py
@@ -534,7 +534,7 @@
             nudge[1, k, pl.ds(rb, 8), :] = live * rate
             nudge[2, k, pl.ds(rb, 8), :] = live
 
-    together = 4
+    together = nest_rows
 
     @pl.loop(0, nest_rows // together)
     def _(step):
@@ -661,7 +661,7 @@
         p = lax.rem(sub, RATIO).astype(F32) / RATIO
         share.append(jnp.where(first_row + rb + sub >= RATIO * (own_rows * tiles - 1), 0.0, p))
 
-    together = 6
+    together = 12
 
     @pl.loop(0, chan // together)
     def _(i):

time: 39.4 us -> 39.2 us (level); the launches traced: 38.7 us -> 39.2 us
  waiting for transfers between devices: 5.99 us -> 7.63 us
  Pallas kernels: 16 us -> 15.1 us
    ppermute x6, waiting for transfers between devices: 4.15 us -> 5.01 us  [exchange(): lax.ppermute(block, axis, [(i, i ^ bit) for i in range(lax.axis_size(axis...]
    pallas_call x11, Pallas kernels: 16 us -> 15.1 us  [call(): pl.pallas_call(kernel, out_shape=list(outs), in_specs=list(specs), out_sp...]
    ppermute x3, waiting for transfers between devices: 1.83 us -> 2.61 us  [exchange_both(): return lax.ppermute(block, ('sec', 'tile'), route)]
  transfers between devices with their start and end apart: 10 -> 10, of which waited for: 4 -> 4; matrix products, arithmetic and copies ran while one was open for 0% -> 0% of each run, Pallas kernels for 26% -> 23%
where the time goes in v5:
time: 39.2 us
  Pallas kernels  15.1 us (39%)
  starting transfers between devices  13.5 us (34%)
  waiting for transfers between devices  7.63 us (19%)
  local copies, waits for them, and re-layouts  2.11 us (5%)
  between operations  0.81 us (2%)
    pallas_call x11, Pallas kernels, call(): pl.pallas_call(kernel, out_shape=list(outs), in_specs=list(specs), out_sp...  15.1 us
    ppermute x6, starting transfers between devices, exchange(): lax.ppermute(block, axis, [(i, i ^ bit) for i in range(lax.axis_size(axis...  9.32 us
    ppermute x6, waiting for transfers between devices, exchange(): lax.ppermute(block, axis, [(i, i ^ bit) for i in range(lax.axis_size(axis...  5.01 us
    ppermute x3, starting transfers between devices, exchange_both(): return lax.ppermute(block, ('sec', 'tile'), route)  3.55 us
    ppermute x3, waiting for transfers between devices, exchange_both(): return lax.ppermute(block, ('sec', 'tile'), route)  2.61 us
    unnamed x16, local copies, waits for them, and re-layouts  2.11 us
  transfers between devices with their start and end apart: 10, of which 4 were waited for; matrix products, arithmetic and copies ran while one was open for 0% of the time, Pallas kernels for 23%

profile of v5, /device:TPU:0, one launch (start us, length us, event | category | flops | bytes accessed | tf_op | source)
XLA Modules:
  0.0 39.2 jit_solution(16030795401373020762)
XLA Ops:
  0.6 1.4 %copy-done = f32[16,24,1024]{2,1,0:T(8,128)S(1)} copy-done((f32[16,24,1024]{2,1,0:T(8,128)S(1)}, f32[16,24,1024]{2,1,0:T(8,128)}, u32[]{:S(2)}) %copy-start) | copy-done | bytes 1572888
  2.0 0.7 %copy-done.3 = s32[4,4]{1,0:T(4,128)S(1)} copy-done((s32[4,4]{1,0:T(4,128)S(1)}, s32[4,4]{1,0:T(4,128)}, u32[]{:S(2)}) %copy-start.3) | copy-done | bytes 88
  2.7 1.3 %shard_map.88 = (f32[2,408,128]{2,1,0:T(8,128)S(1)}, f32[2,408,128]{2,1,0:T(8,128)S(1)}, s32[8,128]{1,0:T(8,128)S(1)}) custom-call(s32[4,4]{1,0:T(4,128)S(1)} %copy-done.3, f32[384,1024]{1,0:T(8,128)S(1)} %bitcast.4), custom_call_target="tpu_custom_call" | custom-call | bytes 4194304 | tf_op jit(solution)/shard_map/pallas_call | solution.py:20
  4.0 0.5 %collective-permute-start.2 = (f32[2,408,128]{2,1,0:T(8,128)S(1)}, f32[2,408,128]{2,1,0:T(8,128)S(1)}, u32[]{:S(2)}, u32[]{:S(2)}) collective-permute-start(f32[2,408,128]{2,1,0:T(8,128)S(1)} %get-tuple-element.28), channel_id=1, source_target_pairs={{0,8},{8,0},{16,24},{24,16},{1,9},{9,1},{17,25},{25,17},{2,10},{10... | collective-permute-start | bytes 1253384 | tf_op jit(solution)/shard_map/ppermute | solution.py:745
  4.6 0.7 %shard_map.87 = (f32[144,512]{1,0:T(8,128)S(1)}, f32[144,512]{1,0:T(8,128)S(1)}) custom-call(f32[384,512]{1,0:T(8,128)S(1)} %bitcast.7, f32[384,1024]{1,0:T(8,128)S(1)} %bitcast.5), custom_call_target="tpu_custom_call" | custom-call | bytes 1048576 | tf_op jit(solution)/shard_map/pallas_call | solution.py:20
  5.2 2.6 %collective-permute-start = (f32[144,512]{1,0:T(8,128)S(1)}, f32[144,512]{1,0:T(8,128)S(1)}, u32[]{:S(2)}, u32[]{:S(2)}) collective-permute-start(f32[144,512]{1,0:T(8,128)S(1)} %get-tuple-element.25), channel_id=1, source_target_pairs={{0,1},{1,0},{2,3},{3,2},{4,5},{5,4},{6,7},{7,6},{8,9},{9,8},{10,11... | collective-permute-start | bytes 884744 | tf_op jit(solution)/shard_map/ppermute | solution.py:745
  7.9 1.7 %collective-permute-start.3 = (f32[216,128]{1,0:T(8,128)S(1)}, f32[216,128]{1,0:T(8,128)S(1)}, u32[]{:S(2)}, u32[]{:S(2)}) collective-permute-start(f32[216,128]{1,0:T(8,128)S(1)} %get-tuple-element.30), channel_id=1, source_target_pairs={{0,16},{1,17},{2,18},{3,19},{4,20},{5,21},{6,22},{7,23},{8,24},{9,... | collective-permute-start | bytes 331784 | tf_op jit(solution)/shard_map/ppermute | solution.py:753
  9.6 1.6 %collective-permute-start.4 = (f32[216,128]{1,0:T(8,128)S(1)}, f32[216,128]{1,0:T(8,128)S(1)}, u32[]{:S(2)}, u32[]{:S(2)}) collective-permute-start(f32[216,128]{1,0:T(8,128)S(1)} %get-tuple-element.31), channel_id=1, source_target_pairs={{0,2},{1,3},{2,0},{3,1},{4,6},{5,7},{6,4},{7,5},{8,10},{9,11},{10,... | collective-permute-start | bytes 331784 | tf_op jit(solution)/shard_map/ppermute | solution.py:753
  11.2 0.3 collective-permute-start.5
  11.5 0.7 %collective-permute-start.1 = (f32[144,512]{1,0:T(8,128)S(1)}, f32[144,512]{1,0:T(8,128)S(1)}, u32[]{:S(2)}, u32[]{:S(2)}) collective-permute-start(f32[144,512]{1,0:T(8,128)S(1)} %get-tuple-element.26), channel_id=1, source_target_pairs={{1,2},{3,4},{5,6},{2,1},{4,3},{6,5},{9,10},{11,12},{13,14},{10,9},... | collective-permute-start | bytes 884744 | tf_op jit(solution)/shard_map/ppermute | solution.py:780
  12.2 2.3 %shard_map.86 = (f32[4,24,24,128]{3,2,1,0:T(8,128)S(1)}, f32[3,4,24,128]{3,2,1,0:T(8,128)S(1)}, bf16[512,512]{1,0:T(8,128)(2,1)S(1)}, bf16[512,512]{1,0:T(8,128)(2,1)S(1)}, f32[136,128]{1,0:T(8,128)S(1)}) custom-call(s32[4,4]{1,0:T(4,128)S(1)} %copy-done.3, f32[24]{0:T(128)S(1)} %copy-done.6, f32[2,24]{1,0:T(2,128)S(1)} %copy-done.4, f32[2,8]{1,0:T(2,128)S(1)} %copy-done.5, ...), custom_call_target="tpu_custom_call" | custom-call | bytes 6291456 | tf_op jit(solution)/shard_map/pallas_call | solution.py:20
  14.5 1.0 %collective-permute-done.4.from_tile = f32[216,128]{1,0:T(8,128)S(1)} collective-permute-done((f32[216,128]{1,0:T(8,128)S(1)}, f32[216,128]{1,0:T(8,128)S(1)}, u32[]{:S(2)}, u32[]{:S(2)}) %collective-permute-start.4) | collective-permute-done | bytes 110624 | tf_op jit(solution)/shard_map/ppermute | solution.py:753
  15.5 1.6 %collective-permute-done.5.from_both = f32[216,128]{1,0:T(8,128)S(1)} collective-permute-done((f32[216,128]{1,0:T(8,128)S(1)}, f32[216,128]{1,0:T(8,128)S(1)}, u32[]{:S(2)}, u32[]{:S(2)}) %collective-permute-start.5) | collective-permute-done | bytes 110624 | tf_op jit(solution)/shard_map/ppermute | solution.py:753
  17.2 2.7 %collective-permute-start.6 = (f32[216,128]{1,0:T(8,128)S(1)}, f32[216,128]{1,0:T(8,128)S(1)}, u32[]{:S(2)}, u32[]{:S(2)}) collective-permute-start(f32[216,128]{1,0:T(8,128)S(1)} %get-tuple-element.38), channel_id=1, source_target_pairs={{0,4},{1,5},{2,6},{3,7},{4,0},{5,1},{6,2},{7,3},{8,12},{9,13},{10,... | collective-permute-start | bytes 331784 | tf_op jit(solution)/shard_map/ppermute | solution.py:745
  19.8 3.9 %shard_map.91 = (f32[384,1024]{1,0:T(8,128)}, f32[2,192,128]{2,1,0:T(8,128)S(1)}) custom-call(f32[136,128]{1,0:T(8,128)S(1)} %get-tuple-element.24.refs_0_.refs_1_, f32[384,1024]{1,0:T(8,128)S(1)} %bitcast.6, f32[2,216,128]{2,1,0:T(8,128)S(1)} %shard_map.90.refs_2_.refs_1_), custom_call_target="tpu_custom_call" | custom-call | bytes 8388608 | tf_op jit(solution)/shard_map/pallas_call | solution.py:20
  23.8 4.0 %collective-permute-done.6.refs_2_ = f32[216,128]{1,0:T(8,128)S(1)} collective-permute-done((f32[216,128]{1,0:T(8,128)S(1)}, f32[216,128]{1,0:T(8,128)S(1)}, u32[]{:S(2)}, u32[]{:S(2)}) %collective-permute-start.6) | collective-permute-done | bytes 110624 | tf_op jit(solution)/shard_map/ppermute | solution.py:745
  27.7 0.1 shard_map.94
  27.8 0.1 collective-permute-start.7
  27.9 0.7 %collective-permute-start.8 = (f32[144,128]{1,0:T(8,128)S(1)}, f32[144,128]{1,0:T(8,128)S(1)}, u32[]{:S(2)}, u32[]{:S(2)}) collective-permute-start(f32[144,128]{1,0:T(8,128)S(1)} %get-tuple-element.41), channel_id=1, source_target_pairs={{0,2},{1,3},{2,0},{3,1},{4,6},{5,7},{6,4},{7,5},{8,10},{9,11},{10,... | collective-permute-start | bytes 221192 | tf_op jit(solution)/shard_map/ppermute | solution.py:745
  28.6 2.7 %collective-permute-start.9 = (f32[144,128]{1,0:T(8,128)S(1)}, f32[144,128]{1,0:T(8,128)S(1)}, u32[]{:S(2)}, u32[]{:S(2)}) collective-permute-start(f32[144,128]{1,0:T(8,128)S(1)} %get-tuple-element.42), channel_id=1, source_target_pairs={{0,3},{1,2},{2,1},{3,0},{4,7},{5,6},{6,5},{7,4},{8,11},{9,10},{10,... | collective-permute-start | bytes 221192 | tf_op jit(solution)/shard_map/ppermute | solution.py:745
  31.4 0.9 %shard_map.92 = f32[384,1024]{1,0:T(8,128)} custom-call(f32[136,128]{1,0:T(8,128)S(1)} %get-tuple-element.24.refs_0_.refs_1_, f32[144,512]{1,0:T(8,128)S(1)} %collective-permute-done.refs_1_.refs_3_.refs_2_, f32[144,512]{1,0:T(8,128)S(1)} %collective-permute-done.1.refs_2_.refs_3_, ...), custom_call_target="tpu_custom_call", output_to_operand_aliasing={{}: (4, {})} | custom-call | bytes 1048576 | tf_op jit(solution)/shard_map/pallas_call | solution.py:20
  32.3 1.1 %shard_map.95.refs_6_ = f32[4,24,24,128]{3,2,1,0:T(8,128)S(1)} custom-call(f32[136,128]{1,0:T(8,128)S(1)} %get-tuple-element.24.refs_0_.refs_1_, f32[384,512]{1,0:T(8,128)S(1)} %bitcast.9, f32[144,512]{1,0:T(8,128)S(1)} %collective-permute-done.refs_1_.refs_3_.refs_2_, ...), custom_call_target="tpu_custom_call", output_to_operand_aliasing={{}: (6, {})} | custom-call | bytes 3145728 | tf_op jit(solution)/shard_map/pallas_call | solution.py:20
  33.5 1.0 %collective-permute-done.9.refs_5_ = f32[144,128]{1,0:T(8,128)S(1)} collective-permute-done((f32[144,128]{1,0:T(8,128)S(1)}, f32[144,128]{1,0:T(8,128)S(1)}, u32[]{:S(2)}, u32[]{:S(2)}) %collective-permute-start.9) | collective-permute-done | bytes 73760 | tf_op jit(solution)/shard_map/ppermute | solution.py:745
  34.5 4.7 %shard_map.96 = f32[384,512]{1,0:T(8,128)} custom-call(s32[8,128]{1,0:T(8,128)S(1)} %get-tuple-element.36.refs_0_, f32[136,128]{1,0:T(8,128)S(1)} %get-tuple-element.24.refs_0_.refs_1_, f32[216,128]{1,0:T(8,128)S(1)} %get-tuple-element.39.refs_2_, f32[144,128]{1,0:T(8,128)S(1)} %collective-permute-done.7.refs_3_, ...), custom_call_target="tpu_custom_call" | custom-call | bytes 16777216 | tf_op jit(solution)/shard_map/pallas_call | solution.py:20
  (23 shorter events, 0.2 us)
Async XLA Ops:
  0.6 1.4 %copy-start = (f32[16,24,1024]{2,1,0:T(8,128)S(1)}, f32[16,24,1024]{2,1,0:T(8,128)}, u32[]{:S(2)}) copy-start(f32[16,24,1024]{2,1,0:T(8,128)} %param.7) | copy-start | bytes 4718596
  2.0 0.7 %copy-start.3 = (s32[4,4]{1,0:T(4,128)S(1)}, s32[4,4]{1,0:T(4,128)}, u32[]{:S(2)}) copy-start(s32[4,4]{1,0:T(4,128)} %refs_0_.3) | copy-start | bytes 196
  2.7 1.8 %copy-start.2 = (f32[1,16,24,512]{3,2,1,0:T(8,128)S(1)}, f32[1,16,24,512]{3,2,1,0:T(8,128)}, u32[]{:S(2)}) copy-start(f32[1,16,24,512]{3,2,1,0:T(8,128)} %param.8) | copy-start | bytes 2359300
  4.0 3.8 %collective-permute-start.2 = (f32[2,408,128]{2,1,0:T(8,128)S(1)}, f32[2,408,128]{2,1,0:T(8,128)S(1)}, u32[]{:S(2)}, u32[]{:S(2)}) collective-permute-start(f32[2,408,128]{2,1,0:T(8,128)S(1)} %get-tuple-element.28), channel_id=1, source_target_pairs={{0,8},{8,0},{16,24},{24,16},{1,9},{9,1},{17,25},{25,17},{2,10},{10... | collective-permute-start | bytes 1253384 | tf_op jit(solution)/shard_map/ppermute | solution.py:745
  4.5 7.6 %copy-start.4 = (f32[2,24]{1,0:T(2,128)S(1)}, f32[2,24]{1,0:T(2,128)}, u32[]{:S(2)}) copy-start(f32[2,24]{1,0:T(2,128)} %refs_2_.1) | copy-start | bytes 580
  4.6 7.6 %copy-start.5 = (f32[2,8]{1,0:T(2,128)S(1)}, f32[2,8]{1,0:T(2,128)}, u32[]{:S(2)}) copy-start(f32[2,8]{1,0:T(2,128)} %refs_3_.1) | copy-start | bytes 196
  4.6 7.6 %copy-start.6 = (f32[24]{0:T(128)S(1)}, f32[24]{0:T(128)}, u32[]{:S(2)}) copy-start(f32[24]{0:T(128)} %refs_1_.1) | copy-start | bytes 292
  4.6 7.6 %copy-start.7 = (f32[3]{0:T(128)S(1)}, f32[3]{0:T(128)}, u32[]{:S(2)}) copy-start(f32[3]{0:T(128)} %refs_4_.1) | copy-start | bytes 40
  5.2 18.5 %collective-permute-start = (f32[144,512]{1,0:T(8,128)S(1)}, f32[144,512]{1,0:T(8,128)S(1)}, u32[]{:S(2)}, u32[]{:S(2)}) collective-permute-start(f32[144,512]{1,0:T(8,128)S(1)} %get-tuple-element.25), channel_id=1, source_target_pairs={{0,1},{1,0},{2,3},{3,2},{4,5},{5,4},{6,7},{7,6},{8,9},{9,8},{10,11... | collective-permute-start | bytes 884744 | tf_op jit(solution)/shard_map/ppermute | solution.py:745
  7.9 11.9 %copy-start.1 = (f32[16,24,1024]{2,1,0:T(8,128)S(1)}, f32[16,24,1024]{2,1,0:T(8,128)}, u32[]{:S(2)}) copy-start(f32[16,24,1024]{2,1,0:T(8,128)} %param.7) | copy-start | bytes 4718596
  7.9 6.6 %collective-permute-start.3 = (f32[216,128]{1,0:T(8,128)S(1)}, f32[216,128]{1,0:T(8,128)S(1)}, u32[]{:S(2)}, u32[]{:S(2)}) collective-permute-start(f32[216,128]{1,0:T(8,128)S(1)} %get-tuple-element.30), channel_id=1, source_target_pairs={{0,16},{1,17},{2,18},{3,19},{4,20},{5,21},{6,22},{7,23},{8,24},{9,... | collective-permute-start | bytes 331784 | tf_op jit(solution)/shard_map/ppermute | solution.py:753
  9.6 5.9 %collective-permute-start.4 = (f32[216,128]{1,0:T(8,128)S(1)}, f32[216,128]{1,0:T(8,128)S(1)}, u32[]{:S(2)}, u32[]{:S(2)}) collective-permute-start(f32[216,128]{1,0:T(8,128)S(1)} %get-tuple-element.31), channel_id=1, source_target_pairs={{0,2},{1,3},{2,0},{3,1},{4,6},{5,7},{6,4},{7,5},{8,10},{9,11},{10,... | collective-permute-start | bytes 331784 | tf_op jit(solution)/shard_map/ppermute | solution.py:753
  11.2 5.9 %collective-permute-start.5 = (f32[216,128]{1,0:T(8,128)S(1)}, f32[216,128]{1,0:T(8,128)S(1)}, u32[]{:S(2)}, u32[]{:S(2)}) collective-permute-start(f32[216,128]{1,0:T(8,128)S(1)} %get-tuple-element.32), channel_id=1, source_target_pairs={{0,18},{1,19},{2,16},{3,17},{4,22},{5,23},{6,20},{7,21},{8,26},{9,... | collective-permute-start | bytes 331784 | tf_op jit(solution)/shard_map/ppermute | solution.py:753
  11.5 19.9 %collective-permute-start.1 = (f32[144,512]{1,0:T(8,128)S(1)}, f32[144,512]{1,0:T(8,128)S(1)}, u32[]{:S(2)}, u32[]{:S(2)}) collective-permute-start(f32[144,512]{1,0:T(8,128)S(1)} %get-tuple-element.26), channel_id=1, source_target_pairs={{1,2},{3,4},{5,6},{2,1},{4,3},{6,5},{9,10},{11,12},{13,14},{10,9},... | collective-permute-start | bytes 884744 | tf_op jit(solution)/shard_map/ppermute | solution.py:780
  17.2 10.6 %collective-permute-start.6 = (f32[216,128]{1,0:T(8,128)S(1)}, f32[216,128]{1,0:T(8,128)S(1)}, u32[]{:S(2)}, u32[]{:S(2)}) collective-permute-start(f32[216,128]{1,0:T(8,128)S(1)} %get-tuple-element.38), channel_id=1, source_target_pairs={{0,4},{1,5},{2,6},{3,7},{4,0},{5,1},{6,2},{7,3},{8,12},{9,13},{10,... | collective-permute-start | bytes 331784 | tf_op jit(solution)/shard_map/ppermute | solution.py:745
  27.8 5.6 %collective-permute-start.7 = (f32[144,128]{1,0:T(8,128)S(1)}, f32[144,128]{1,0:T(8,128)S(1)}, u32[]{:S(2)}, u32[]{:S(2)}) collective-permute-start(f32[144,128]{1,0:T(8,128)S(1)} %get-tuple-element.40), channel_id=1, source_target_pairs={{0,1},{1,0},{2,3},{3,2},{4,5},{5,4},{6,7},{7,6},{8,9},{9,8},{10,11... | collective-permute-start | bytes 221192 | tf_op jit(solution)/shard_map/ppermute | solution.py:745
  27.9 5.6 %collective-permute-start.8 = (f32[144,128]{1,0:T(8,128)S(1)}, f32[144,128]{1,0:T(8,128)S(1)}, u32[]{:S(2)}, u32[]{:S(2)}) collective-permute-start(f32[144,128]{1,0:T(8,128)S(1)} %get-tuple-element.41), channel_id=1, source_target_pairs={{0,2},{1,3},{2,0},{3,1},{4,6},{5,7},{6,4},{7,5},{8,10},{9,11},{10,... | collective-permute-start | bytes 221192 | tf_op jit(solution)/shard_map/ppermute | solution.py:745
  28.6 5.9 %collective-permute-start.9 = (f32[144,128]{1,0:T(8,128)S(1)}, f32[144,128]{1,0:T(8,128)S(1)}, u32[]{:S(2)}, u32[]{:S(2)}) collective-permute-start(f32[144,128]{1,0:T(8,128)S(1)} %get-tuple-element.42), channel_id=1, source_target_pairs={{0,3},{1,2},{2,1},{3,0},{4,7},{5,6},{6,5},{7,4},{8,11},{9,10},{10,... | collective-permute-start | bytes 221192 | tf_op jit(solution)/shard_map/ppermute | solution.py:745

commit v6 on v5

--- a/solution.py
+++ b/solution.py
@@ -13,7 +13,7 @@
 SMEM = pl.BlockSpec(memory_space=pltpu.SMEM)
 ANY = pl.BlockSpec(memory_space=pl.ANY)
 HBM = pl.BlockSpec(memory_space=pltpu.HBM)
-TOGETHER = 8
+TOGETHER = 16
 
 
 def call(kernel, outs, args, specs, scratch=(), limit=16, cost=0, out_specs=None, same=None):

time: 39.2 us -> 39.1 us (level)
  no operation moved by 1% of the time
where the time goes in v6:
time: 39.1 us; the launch traced here: 39 us
  Pallas kernels  14.9 us (38%)
  starting transfers between devices  13.5 us (35%)
  waiting for transfers between devices  7.63 us (20%)
  local copies, waits for them, and re-layouts  2.11 us (5%)
  between operations  0.81 us (2%)
    pallas_call x11, Pallas kernels, call(): pl.pallas_call(kernel, out_shape=list(outs), in_specs=list(specs), out_sp...  14.9 us
    ppermute x6, starting transfers between devices, exchange(): lax.ppermute(block, axis, [(i, i ^ bit) for i in range(lax.axis_size(axis...  9.32 us
    ppermute x6, waiting for transfers between devices, exchange(): lax.ppermute(block, axis, [(i, i ^ bit) for i in range(lax.axis_size(axis...  5.24 us
    ppermute x3, starting transfers between devices, exchange_both(): return lax.ppermute(block, ('sec', 'tile'), route)  3.55 us
    ppermute x3, waiting for transfers between devices, exchange_both(): return lax.ppermute(block, ('sec', 'tile'), route)  2.39 us
    unnamed x16, local copies, waits for them, and re-layouts  2.11 us
  transfers between devices with their start and end apart: 10, of which 4 were waited for; matrix products, arithmetic and copies ran while one was open for 0% of the time, Pallas kernels for 23%

profile of v6, /device:TPU:0, one launch (start us, length us, event | category | flops | bytes accessed | tf_op | source)
XLA Modules:
  0.0 39.0 jit_solution(4106338648398554314)
XLA Ops:
  0.6 1.4 %copy-done = f32[16,24,1024]{2,1,0:T(8,128)S(1)} copy-done((f32[16,24,1024]{2,1,0:T(8,128)S(1)}, f32[16,24,1024]{2,1,0:T(8,128)}, u32[]{:S(2)}) %copy-start) | copy-done | bytes 1572888
  2.0 0.7 %copy-done.3 = s32[4,4]{1,0:T(4,128)S(1)} copy-done((s32[4,4]{1,0:T(4,128)S(1)}, s32[4,4]{1,0:T(4,128)}, u32[]{:S(2)}) %copy-start.3) | copy-done | bytes 88
  2.7 1.1 %shard_map.88 = (f32[2,408,128]{2,1,0:T(8,128)S(1)}, f32[2,408,128]{2,1,0:T(8,128)S(1)}, s32[8,128]{1,0:T(8,128)S(1)}) custom-call(s32[4,4]{1,0:T(4,128)S(1)} %copy-done.3, f32[384,1024]{1,0:T(8,128)S(1)} %bitcast.4), custom_call_target="tpu_custom_call" | custom-call | bytes 4194304 | tf_op jit(solution)/shard_map/pallas_call | solution.py:20
  3.8 0.5 %collective-permute-start.2 = (f32[2,408,128]{2,1,0:T(8,128)S(1)}, f32[2,408,128]{2,1,0:T(8,128)S(1)}, u32[]{:S(2)}, u32[]{:S(2)}) collective-permute-start(f32[2,408,128]{2,1,0:T(8,128)S(1)} %get-tuple-element.28), channel_id=1, source_target_pairs={{0,8},{8,0},{16,24},{24,16},{1,9},{9,1},{17,25},{25,17},{2,10},{10... | collective-permute-start | bytes 1253384 | tf_op jit(solution)/shard_map/ppermute | solution.py:745
  4.3 0.7 %shard_map.87 = (f32[144,512]{1,0:T(8,128)S(1)}, f32[144,512]{1,0:T(8,128)S(1)}) custom-call(f32[384,512]{1,0:T(8,128)S(1)} %bitcast.7, f32[384,1024]{1,0:T(8,128)S(1)} %bitcast.5), custom_call_target="tpu_custom_call" | custom-call | bytes 1048576 | tf_op jit(solution)/shard_map/pallas_call | solution.py:20
  5.0 2.6 %collective-permute-start = (f32[144,512]{1,0:T(8,128)S(1)}, f32[144,512]{1,0:T(8,128)S(1)}, u32[]{:S(2)}, u32[]{:S(2)}) collective-permute-start(f32[144,512]{1,0:T(8,128)S(1)} %get-tuple-element.25), channel_id=1, source_target_pairs={{0,1},{1,0},{2,3},{3,2},{4,5},{5,4},{6,7},{7,6},{8,9},{9,8},{10,11... | collective-permute-start | bytes 884744 | tf_op jit(solution)/shard_map/ppermute | solution.py:745
  7.7 1.6 %collective-permute-start.3 = (f32[216,128]{1,0:T(8,128)S(1)}, f32[216,128]{1,0:T(8,128)S(1)}, u32[]{:S(2)}, u32[]{:S(2)}) collective-permute-start(f32[216,128]{1,0:T(8,128)S(1)} %get-tuple-element.30), channel_id=1, source_target_pairs={{0,16},{1,17},{2,18},{3,19},{4,20},{5,21},{6,22},{7,23},{8,24},{9,... | collective-permute-start | bytes 331784 | tf_op jit(solution)/shard_map/ppermute | solution.py:753
  9.3 1.6 %collective-permute-start.4 = (f32[216,128]{1,0:T(8,128)S(1)}, f32[216,128]{1,0:T(8,128)S(1)}, u32[]{:S(2)}, u32[]{:S(2)}) collective-permute-start(f32[216,128]{1,0:T(8,128)S(1)} %get-tuple-element.31), channel_id=1, source_target_pairs={{0,2},{1,3},{2,0},{3,1},{4,6},{5,7},{6,4},{7,5},{8,10},{9,11},{10,... | collective-permute-start | bytes 331784 | tf_op jit(solution)/shard_map/ppermute | solution.py:753
  10.8 0.4 %collective-permute-start.5 = (f32[216,128]{1,0:T(8,128)S(1)}, f32[216,128]{1,0:T(8,128)S(1)}, u32[]{:S(2)}, u32[]{:S(2)}) collective-permute-start(f32[216,128]{1,0:T(8,128)S(1)} %get-tuple-element.32), channel_id=1, source_target_pairs={{0,18},{1,19},{2,16},{3,17},{4,22},{5,23},{6,20},{7,21},{8,26},{9,... | collective-permute-start | bytes 331784 | tf_op jit(solution)/shard_map/ppermute | solution.py:753
  11.2 0.7 %collective-permute-start.1 = (f32[144,512]{1,0:T(8,128)S(1)}, f32[144,512]{1,0:T(8,128)S(1)}, u32[]{:S(2)}, u32[]{:S(2)}) collective-permute-start(f32[144,512]{1,0:T(8,128)S(1)} %get-tuple-element.26), channel_id=1, source_target_pairs={{1,2},{3,4},{5,6},{2,1},{4,3},{6,5},{9,10},{11,12},{13,14},{10,9},... | collective-permute-start | bytes 884744 | tf_op jit(solution)/shard_map/ppermute | solution.py:780
  11.9 2.3 %shard_map.86 = (f32[4,24,24,128]{3,2,1,0:T(8,128)S(1)}, f32[3,4,24,128]{3,2,1,0:T(8,128)S(1)}, bf16[512,512]{1,0:T(8,128)(2,1)S(1)}, bf16[512,512]{1,0:T(8,128)(2,1)S(1)}, f32[136,128]{1,0:T(8,128)S(1)}) custom-call(s32[4,4]{1,0:T(4,128)S(1)} %copy-done.3, f32[24]{0:T(128)S(1)} %copy-done.6, f32[2,24]{1,0:T(2,128)S(1)} %copy-done.4, f32[2,8]{1,0:T(2,128)S(1)} %copy-done.5, ...), custom_call_target="tpu_custom_call" | custom-call | bytes 6291456 | tf_op jit(solution)/shard_map/pallas_call | solution.py:20
  14.2 1.0 %collective-permute-done.4.from_tile = f32[216,128]{1,0:T(8,128)S(1)} collective-permute-done((f32[216,128]{1,0:T(8,128)S(1)}, f32[216,128]{1,0:T(8,128)S(1)}, u32[]{:S(2)}, u32[]{:S(2)}) %collective-permute-start.4) | collective-permute-done | bytes 110624 | tf_op jit(solution)/shard_map/ppermute | solution.py:753
  15.2 1.4 %collective-permute-done.5.from_both = f32[216,128]{1,0:T(8,128)S(1)} collective-permute-done((f32[216,128]{1,0:T(8,128)S(1)}, f32[216,128]{1,0:T(8,128)S(1)}, u32[]{:S(2)}, u32[]{:S(2)}) %collective-permute-start.5) | collective-permute-done | bytes 110624 | tf_op jit(solution)/shard_map/ppermute | solution.py:753
  16.7 2.7 %collective-permute-start.6 = (f32[216,128]{1,0:T(8,128)S(1)}, f32[216,128]{1,0:T(8,128)S(1)}, u32[]{:S(2)}, u32[]{:S(2)}) collective-permute-start(f32[216,128]{1,0:T(8,128)S(1)} %get-tuple-element.38), channel_id=1, source_target_pairs={{0,4},{1,5},{2,6},{3,7},{4,0},{5,1},{6,2},{7,3},{8,12},{9,13},{10,... | collective-permute-start | bytes 331784 | tf_op jit(solution)/shard_map/ppermute | solution.py:745
  19.4 3.9 %shard_map.91 = (f32[384,1024]{1,0:T(8,128)}, f32[2,192,128]{2,1,0:T(8,128)S(1)}) custom-call(f32[136,128]{1,0:T(8,128)S(1)} %get-tuple-element.24.refs_0_.refs_1_, f32[384,1024]{1,0:T(8,128)S(1)} %bitcast.6, f32[2,216,128]{2,1,0:T(8,128)S(1)} %shard_map.90.refs_2_.refs_1_), custom_call_target="tpu_custom_call" | custom-call | bytes 8388608 | tf_op jit(solution)/shard_map/pallas_call | solution.py:20
  23.3 4.2 %collective-permute-done.6.refs_2_ = f32[216,128]{1,0:T(8,128)S(1)} collective-permute-done((f32[216,128]{1,0:T(8,128)S(1)}, f32[216,128]{1,0:T(8,128)S(1)}, u32[]{:S(2)}, u32[]{:S(2)}) %collective-permute-start.6) | collective-permute-done | bytes 110624 | tf_op jit(solution)/shard_map/ppermute | solution.py:745
  27.5 0.1 shard_map.94
  27.6 0.1 collective-permute-start.7
  27.7 0.7 %collective-permute-start.8 = (f32[144,128]{1,0:T(8,128)S(1)}, f32[144,128]{1,0:T(8,128)S(1)}, u32[]{:S(2)}, u32[]{:S(2)}) collective-permute-start(f32[144,128]{1,0:T(8,128)S(1)} %get-tuple-element.41), channel_id=1, source_target_pairs={{0,2},{1,3},{2,0},{3,1},{4,6},{5,7},{6,4},{7,5},{8,10},{9,11},{10,... | collective-permute-start | bytes 221192 | tf_op jit(solution)/shard_map/ppermute | solution.py:745
  28.4 2.7 %collective-permute-start.9 = (f32[144,128]{1,0:T(8,128)S(1)}, f32[144,128]{1,0:T(8,128)S(1)}, u32[]{:S(2)}, u32[]{:S(2)}) collective-permute-start(f32[144,128]{1,0:T(8,128)S(1)} %get-tuple-element.42), channel_id=1, source_target_pairs={{0,3},{1,2},{2,1},{3,0},{4,7},{5,6},{6,5},{7,4},{8,11},{9,10},{10,... | collective-permute-start | bytes 221192 | tf_op jit(solution)/shard_map/ppermute | solution.py:745
  31.1 0.9 %shard_map.92 = f32[384,1024]{1,0:T(8,128)} custom-call(f32[136,128]{1,0:T(8,128)S(1)} %get-tuple-element.24.refs_0_.refs_1_, f32[144,512]{1,0:T(8,128)S(1)} %collective-permute-done.refs_1_.refs_3_.refs_2_, f32[144,512]{1,0:T(8,128)S(1)} %collective-permute-done.1.refs_2_.refs_3_, ...), custom_call_target="tpu_custom_call", output_to_operand_aliasing={{}: (4, {})} | custom-call | bytes 1048576 | tf_op jit(solution)/shard_map/pallas_call | solution.py:20
  32.1 1.1 %shard_map.95.refs_6_ = f32[4,24,24,128]{3,2,1,0:T(8,128)S(1)} custom-call(f32[136,128]{1,0:T(8,128)S(1)} %get-tuple-element.24.refs_0_.refs_1_, f32[384,512]{1,0:T(8,128)S(1)} %bitcast.9, f32[144,512]{1,0:T(8,128)S(1)} %collective-permute-done.refs_1_.refs_3_.refs_2_, ...), custom_call_target="tpu_custom_call", output_to_operand_aliasing={{}: (6, {})} | custom-call | bytes 3145728 | tf_op jit(solution)/shard_map/pallas_call | solution.py:20
  33.2 1.0 %collective-permute-done.9.refs_5_ = f32[144,128]{1,0:T(8,128)S(1)} collective-permute-done((f32[144,128]{1,0:T(8,128)S(1)}, f32[144,128]{1,0:T(8,128)S(1)}, u32[]{:S(2)}, u32[]{:S(2)}) %collective-permute-start.9) | collective-permute-done | bytes 73760 | tf_op jit(solution)/shard_map/ppermute | solution.py:745
  34.3 4.7 %shard_map.96 = f32[384,512]{1,0:T(8,128)} custom-call(s32[8,128]{1,0:T(8,128)S(1)} %get-tuple-element.36.refs_0_, f32[136,128]{1,0:T(8,128)S(1)} %get-tuple-element.24.refs_0_.refs_1_, f32[216,128]{1,0:T(8,128)S(1)} %get-tuple-element.39.refs_2_, f32[144,128]{1,0:T(8,128)S(1)} %collective-permute-done.7.refs_3_, ...), custom_call_target="tpu_custom_call" | custom-call | bytes 16777216 | tf_op jit(solution)/shard_map/pallas_call | solution.py:20
  (23 shorter events, 0.2 us)
Async XLA Ops:
  0.6 1.4 %copy-start = (f32[16,24,1024]{2,1,0:T(8,128)S(1)}, f32[16,24,1024]{2,1,0:T(8,128)}, u32[]{:S(2)}) copy-start(f32[16,24,1024]{2,1,0:T(8,128)} %param.7) | copy-start | bytes 4718596
  2.0 0.7 %copy-start.3 = (s32[4,4]{1,0:T(4,128)S(1)}, s32[4,4]{1,0:T(4,128)}, u32[]{:S(2)}) copy-start(s32[4,4]{1,0:T(4,128)} %refs_0_.3) | copy-start | bytes 196
  2.7 1.6 %copy-start.2 = (f32[1,16,24,512]{3,2,1,0:T(8,128)S(1)}, f32[1,16,24,512]{3,2,1,0:T(8,128)}, u32[]{:S(2)}) copy-start(f32[1,16,24,512]{3,2,1,0:T(8,128)} %param.8) | copy-start | bytes 2359300
  3.8 3.8 %collective-permute-start.2 = (f32[2,408,128]{2,1,0:T(8,128)S(1)}, f32[2,408,128]{2,1,0:T(8,128)S(1)}, u32[]{:S(2)}, u32[]{:S(2)}) collective-permute-start(f32[2,408,128]{2,1,0:T(8,128)S(1)} %get-tuple-element.28), channel_id=1, source_target_pairs={{0,8},{8,0},{16,24},{24,16},{1,9},{9,1},{17,25},{25,17},{2,10},{10... | collective-permute-start | bytes 1253384 | tf_op jit(solution)/shard_map/ppermute | solution.py:745
  4.3 7.6 %copy-start.4 = (f32[2,24]{1,0:T(2,128)S(1)}, f32[2,24]{1,0:T(2,128)}, u32[]{:S(2)}) copy-start(f32[2,24]{1,0:T(2,128)} %refs_2_.1) | copy-start | bytes 580
  4.3 7.6 %copy-start.5 = (f32[2,8]{1,0:T(2,128)S(1)}, f32[2,8]{1,0:T(2,128)}, u32[]{:S(2)}) copy-start(f32[2,8]{1,0:T(2,128)} %refs_3_.1) | copy-start | bytes 196
  4.3 7.6 %copy-start.6 = (f32[24]{0:T(128)S(1)}, f32[24]{0:T(128)}, u32[]{:S(2)}) copy-start(f32[24]{0:T(128)} %refs_1_.1) | copy-start | bytes 292
  4.3 7.6 %copy-start.7 = (f32[3]{0:T(128)S(1)}, f32[3]{0:T(128)}, u32[]{:S(2)}) copy-start(f32[3]{0:T(128)} %refs_4_.1) | copy-start | bytes 40
  5.0 18.3 %collective-permute-start = (f32[144,512]{1,0:T(8,128)S(1)}, f32[144,512]{1,0:T(8,128)S(1)}, u32[]{:S(2)}, u32[]{:S(2)}) collective-permute-start(f32[144,512]{1,0:T(8,128)S(1)} %get-tuple-element.25), channel_id=1, source_target_pairs={{0,1},{1,0},{2,3},{3,2},{4,5},{5,4},{6,7},{7,6},{8,9},{9,8},{10,11... | collective-permute-start | bytes 884744 | tf_op jit(solution)/shard_map/ppermute | solution.py:745
  7.7 11.7 %copy-start.1 = (f32[16,24,1024]{2,1,0:T(8,128)S(1)}, f32[16,24,1024]{2,1,0:T(8,128)}, u32[]{:S(2)}) copy-start(f32[16,24,1024]{2,1,0:T(8,128)} %param.7) | copy-start | bytes 4718596
  7.7 6.6 %collective-permute-start.3 = (f32[216,128]{1,0:T(8,128)S(1)}, f32[216,128]{1,0:T(8,128)S(1)}, u32[]{:S(2)}, u32[]{:S(2)}) collective-permute-start(f32[216,128]{1,0:T(8,128)S(1)} %get-tuple-element.30), channel_id=1, source_target_pairs={{0,16},{1,17},{2,18},{3,19},{4,20},{5,21},{6,22},{7,23},{8,24},{9,... | collective-permute-start | bytes 331784 | tf_op jit(solution)/shard_map/ppermute | solution.py:753
  9.3 5.9 %collective-permute-start.4 = (f32[216,128]{1,0:T(8,128)S(1)}, f32[216,128]{1,0:T(8,128)S(1)}, u32[]{:S(2)}, u32[]{:S(2)}) collective-permute-start(f32[216,128]{1,0:T(8,128)S(1)} %get-tuple-element.31), channel_id=1, source_target_pairs={{0,2},{1,3},{2,0},{3,1},{4,6},{5,7},{6,4},{7,5},{8,10},{9,11},{10,... | collective-permute-start | bytes 331784 | tf_op jit(solution)/shard_map/ppermute | solution.py:753
  10.8 5.8 %collective-permute-start.5 = (f32[216,128]{1,0:T(8,128)S(1)}, f32[216,128]{1,0:T(8,128)S(1)}, u32[]{:S(2)}, u32[]{:S(2)}) collective-permute-start(f32[216,128]{1,0:T(8,128)S(1)} %get-tuple-element.32), channel_id=1, source_target_pairs={{0,18},{1,19},{2,16},{3,17},{4,22},{5,23},{6,20},{7,21},{8,26},{9,... | collective-permute-start | bytes 331784 | tf_op jit(solution)/shard_map/ppermute | solution.py:753
  11.2 19.9 %collective-permute-start.1 = (f32[144,512]{1,0:T(8,128)S(1)}, f32[144,512]{1,0:T(8,128)S(1)}, u32[]{:S(2)}, u32[]{:S(2)}) collective-permute-start(f32[144,512]{1,0:T(8,128)S(1)} %get-tuple-element.26), channel_id=1, source_target_pairs={{1,2},{3,4},{5,6},{2,1},{4,3},{6,5},{9,10},{11,12},{13,14},{10,9},... | collective-permute-start | bytes 884744 | tf_op jit(solution)/shard_map/ppermute | solution.py:780
  16.7 10.8 %collective-permute-start.6 = (f32[216,128]{1,0:T(8,128)S(1)}, f32[216,128]{1,0:T(8,128)S(1)}, u32[]{:S(2)}, u32[]{:S(2)}) collective-permute-start(f32[216,128]{1,0:T(8,128)S(1)} %get-tuple-element.38), channel_id=1, source_target_pairs={{0,4},{1,5},{2,6},{3,7},{4,0},{5,1},{6,2},{7,3},{8,12},{9,13},{10,... | collective-permute-start | bytes 331784 | tf_op jit(solution)/shard_map/ppermute | solution.py:745
  27.6 5.6 %collective-permute-start.7 = (f32[144,128]{1,0:T(8,128)S(1)}, f32[144,128]{1,0:T(8,128)S(1)}, u32[]{:S(2)}, u32[]{:S(2)}) collective-permute-start(f32[144,128]{1,0:T(8,128)S(1)} %get-tuple-element.40), channel_id=1, source_target_pairs={{0,1},{1,0},{2,3},{3,2},{4,5},{5,4},{6,7},{7,6},{8,9},{9,8},{10,11... | collective-permute-start | bytes 221192 | tf_op jit(solution)/shard_map/ppermute | solution.py:745
  27.7 5.6 %collective-permute-start.8 = (f32[144,128]{1,0:T(8,128)S(1)}, f32[144,128]{1,0:T(8,128)S(1)}, u32[]{:S(2)}, u32[]{:S(2)}) collective-permute-start(f32[144,128]{1,0:T(8,128)S(1)} %get-tuple-element.41), channel_id=1, source_target_pairs={{0,2},{1,3},{2,0},{3,1},{4,6},{5,7},{6,4},{7,5},{8,10},{9,11},{10,... | collective-permute-start | bytes 221192 | tf_op jit(solution)/shard_map/ppermute | solution.py:745
  28.4 5.9 %collective-permute-start.9 = (f32[144,128]{1,0:T(8,128)S(1)}, f32[144,128]{1,0:T(8,128)S(1)}, u32[]{:S(2)}, u32[]{:S(2)}) collective-permute-start(f32[144,128]{1,0:T(8,128)S(1)} %get-tuple-element.42), channel_id=1, source_target_pairs={{0,3},{1,2},{2,1},{3,0},{4,7},{5,6},{6,5},{7,4},{8,11},{9,10},{10,... | collective-permute-start | bytes 221192 | tf_op jit(solution)/shard_map/ppermute | solution.py:745
